TPU v7x, 32 devices: a whole 2x2x4 slice. The times are simulated.
32 devices in a mesh: phase: 4 (over x, core), ctx: 2 (over y), tp: 4 (over z).
Axes of the slice: x: 2, y: 2, z: 4, core: 2. Of those that a mesh axis runs over, the one named last changes fastest.
Arguments:
- queries: bfloat16 [4, 256, 4096], P('phase', 'ctx', 'tp'), may hold values from -8 to 8
- keys: bfloat16 [4, 256, 512], P('phase', 'ctx', 'tp'), may hold values from -8 to 8
- values: bfloat16 [4, 256, 512], P('phase', 'ctx', 'tp'), may hold values from -6 to 6
- seg_ids: int32 [4, 256], P('phase'), may hold values from 0 to 3, never falling along the last dimension, each value on 1 to 128 neighbouring positions
- out_weight: bfloat16 [4096, 8192], P('tp', 'ctx'), may hold values from -0.5 to 0.5
- embedded: bfloat16 [256, 8192], P('tp', 'ctx'), may hold values from -6 to 6
- hidden_prev: bfloat16 [4, 256, 8192], P('phase', 'tp', 'ctx'), may hold values from -6 to 6
Outputs:
- hidden_next: bfloat16 [4, 256, 8192], P('phase', 'tp', 'ctx')
Inputs may be any that keep to these rules, and one draw needn't show every extreme that they name: `seg_ids`: within each section the segment number never falls; a segment holds at most 128 tokens.
All inputs are finite; a program needn't handle non-finite values.
Results may differ from a plain program's by a relative error of at most 0.015.
Values may be sent and summed in bfloat16 or wider, within the bound.
No kernel may reach another device: no remote copies, remote signals or barrier semaphores. Data moves between devices by JAX's collectives and lax.ppermute only.
A program may use at most 64 MiB of HBM per device.

v0:
```python
import jax
import jax.numpy as jnp
from jax import lax
from jax.sharding import PartitionSpec as P

HEAD_DIM = 128


def passed_along(shard, axis, by):
    peers = lax.axis_size(axis)
    pairs = [(i, i + by) for i in range(peers) if 0 <= i + by < peers]
    return lax.ppermute(shard, axis, pairs)


def on_device(queries, keys, values, seg_ids, out_weight, embedded, hidden_prev):
    shard_rows = queries.shape[1]
    kv_local = keys.shape[2] // HEAD_DIM
    heads_local = queries.shape[2] // HEAD_DIM
    group_size = heads_local // kv_local
    kv_width = kv_local * HEAD_DIM
    score_scale = HEAD_DIM ** (-0.5)
    ctx_place = lax.axis_index("ctx")
    offset = ctx_place * shard_rows
    query_grid = queries[0].reshape(shard_rows, kv_local, group_size, HEAD_DIM)
    segment_row = seg_ids[0]
    query_places = offset + jnp.arange(shard_rows, dtype=jnp.int32)
    query_segs = lax.dynamic_slice_in_dim(segment_row, offset, shard_rows)
    stacked = jnp.concatenate((keys, values), axis=2)
    pieces = lax.all_gather(stacked, "ctx", axis=1, tiled=True)
    length = pieces.shape[1]
    key_grid = pieces[0, :, :kv_width].reshape(length, kv_local, HEAD_DIM)
    value_grid = pieces[0, :, kv_width:].reshape(length, kv_local, HEAD_DIM)
    key_places = jnp.arange(length, dtype=jnp.int32)
    allowed = (query_places[:, None] >= key_places[None, :]) & (key_places[None, :] >= 0)
    allowed = allowed & (query_segs[:, None] == segment_row[None, :])
    mask_grid = allowed[:, None, None, :]
    scores = (
        jnp.einsum("qkgd,nkd->qkgn", query_grid, key_grid, preferred_element_type=jnp.float32)
        * score_scale
    )
    running_max = jnp.full((shard_rows, kv_local, group_size), -1e30, jnp.float32)
    new_max = jnp.maximum(running_max, jnp.max(jnp.where(mask_grid, scores, -1e30), axis=3))
    probs = jnp.where(mask_grid, jnp.exp(scores - new_max[..., None]), 0.0)
    new_sum = jnp.sum(probs, axis=3)
    new_out = jnp.einsum(
        "qkgn,nkd->qkgd", probs.astype(jnp.bfloat16), value_grid, preferred_element_type=jnp.float32
    )
    attended = (
        (new_out / new_sum[..., None])
        .reshape(shard_rows, heads_local * HEAD_DIM)
        .astype(jnp.bfloat16)
    )
    partial_value = jnp.dot(
        lax.all_gather(attended, "ctx", axis=0, tiled=True),
        out_weight,
        preferred_element_type=jnp.float32,
    )
    summed = lax.psum_scatter(
        partial_value.astype(jnp.bfloat16), "tp", scatter_dimension=0, tiled=True
    ).astype(jnp.float32)
    arrived = passed_along(hidden_prev, "phase", 1)
    resid_in = jnp.where(lax.axis_index("phase") == 0, embedded, arrived[0])
    return (resid_in.astype(jnp.float32) + summed).astype(jnp.bfloat16)[None]


def solution(mesh):
    return jax.shard_map(
        on_device,
        mesh=mesh,
        in_specs=(
            P("phase", "ctx", "tp"),
            P("phase", "ctx", "tp"),
            P("phase", "ctx", "tp"),
            P("phase", None),
            P("tp", "ctx"),
            P("tp", "ctx"),
            P("phase", "tp", "ctx"),
        ),
        out_specs=P("phase", "tp", "ctx"),
        check_vma=False,
    )
```

profile of v0, /device:TPU:0, one launch (start us, length us, event | category | flops | bytes accessed | tf_op | source)
XLA Modules:
  0.0 86.1 jit_solution(17171699061803866378)
XLA Ops:
  6.5 0.0 reduce-scatter.2.cloned.1.call-start
  6.5 0.8 pad_maximum_fusion
  7.3 5.9 %all_gather.6 = bf16[1,256,256]{2,1,0:T(8,128)(2,1)S(1)} all-gather(bf16[1,128,256]{2,1,0:T(8,128)(2,1)S(1)} %pad_maximum_fusion), channel_id=1, replica_groups=mesh['phase'=4,'ctx'=2,'tp'=4] {'ctx'}, dimensions={1}, use_global_device_ids=true | all-gather | bytes 196608 | tf_op jit(solution)/shard_map/all_gather | solution.py:29
  13.2 1.0 %copy.14 = bf16[16,8,8,128]{3,2,1,0:T(8,128)(2,1)S(1)} copy(bf16[16,8,8,128]{3,1,2,0:T(8,128)(2,1)} %bitcast.43) | data formatting | bytes 524288
  14.2 0.7 dynamic-slice_bitcast_fusion
  14.8 0.8 fusion.12
  15.6 0.3 select_reduce_fusion
  16.0 0.2 fusion.3
  16.2 0.3 fusion.2
  16.5 0.0 copy-start.1
  16.5 0.0 copy-start
  16.5 8.1 %all_gather.7 = bf16[256,1024]{0,1:T(8,128)(2,1)S(1)} all-gather(bf16[128,1024]{0,1:T(8,128)(2,1)S(1)} %bitcast.42), channel_id=1, replica_groups=mesh['phase'=4,'ctx'=2,'tp'=4] {'ctx'}, dimensions={0}, use_global_device_ids=true | all-gather | bytes 786432 | tf_op jit(solution)/shard_map/all_gather | solution.py:54
  24.6 7.1 %convolution_convert_fusion = bf16[256,4096]{1,0:T(8,128)(2,1)} fusion(bf16[256,1024]{0,1:T(8,128)(2,1)S(1)} %all_gather.7, bf16[1024,4096]{1,0:T(8,128)(2,1)} %param.11), kind=kOutput, calls=%fused_computation | convolution fusion | flops 2148532224 | bytes 11010048 | tf_op jit(solution)/shard_map/dot_general | solution.py:53
  31.7 0.0 reduce-scatter.2.cloned.1.call-update
  31.7 0.0 copy-done.1
  31.7 1.3 %collective-permute-start = (bf16[1,64,4096]{2,1,0:T(8,128)(2,1)S(1)}, bf16[1,64,4096]{2,1,0:T(8,128)(2,1)S(1)}, u32[]{:S(2)}, u32[]{:S(2)}) collective-permute-start(bf16[1,64,4096]{2,1,0:T(8,128)(2,1)S(1)} %copy-done.1), channel_id=1, source_target_pairs={{0,8},{8,16},{16,24},{1,9},{9,17},{17,25},{2,10},{10,18},{18,26},{... | collective-permute-start | bytes 1572872 | tf_op jit(solution)/shard_map/ppermute | solution.py:12
  33.1 1.5 %collective-permute-done = bf16[1,64,4096]{2,1,0:T(8,128)(2,1)S(1)} collective-permute-done((bf16[1,64,4096]{2,1,0:T(8,128)(2,1)S(1)}, bf16[1,64,4096]{2,1,0:T(8,128)(2,1)S(1)}, u32[]{:S(2)}, u32[]{:S(2)}) %collective-permute-start) | collective-permute-done | bytes 524320 | tf_op jit(solution)/shard_map/ppermute | solution.py:12
  34.5 42.7 %reduce-scatter.2.cloned.1.call-done = bf16[64,4096]{1,0:T(8,128)(2,1)} async-done(((bf16[256,4096]{1,0:T(8,128)(2,1)}), bf16[64,4096]{1,0:T(8,128)(2,1)}) %reduce-scatter.2.cloned.1.call-update) | async-done | bytes 524304 | tf_op jit(solution)/shard_map/reduce_scatter | solution.py:58
  77.2 0.0 copy-done
  77.2 2.0 %fusion.7 = bf16[1,64,4096]{2,1,0:T(8,128)(2,1)} fusion(bf16[64,4096]{1,0:T(8,128)(2,1)} %reduce-scatter.2.cloned.1.call-done, bf16[64,4096]{1,0:T(8,128)(2,1)S(1)} %copy-done, bf16[1,64,4096]{2,1,0:T(8,128)(2,1)S(1)} %collective-permute-done, pred[]{:T(512)S(6)} %eq.24), kind=kLoop, calls=%fused_computation.12 | loop fusion | flops 1310720 | bytes 2097153 | tf_op jit(solution)/shard_map/broadcast_in_dim | solution.py:63
  (2 shorter events, 0.0 us)
Async XLA Ops:
  6.5 70.7 %reduce-scatter.2.cloned.1.call-start = ((), (), s32[]{:S(2)}) async-start(), calls=%async_computation.1 | async-start | bytes 2621440 | tf_op jit(solution)/shard_map/reduce_scatter | solution.py:58
  16.5 15.2 %copy-start.1 = (bf16[1,64,4096]{2,1,0:T(8,128)(2,1)S(1)}, bf16[1,64,4096]{2,1,0:T(8,128)(2,1)}, u32[]{:S(2)}) copy-start(bf16[1,64,4096]{2,1,0:T(8,128)(2,1)} %param.13) | copy-start | bytes 1572868
  16.5 60.7 %copy-start = (bf16[64,4096]{1,0:T(8,128)(2,1)S(1)}, bf16[64,4096]{1,0:T(8,128)(2,1)}, u32[]{:S(2)}) copy-start(bf16[64,4096]{1,0:T(8,128)(2,1)} %param.12) | copy-start | bytes 1572868
  31.7 2.8 %collective-permute-start = (bf16[1,64,4096]{2,1,0:T(8,128)(2,1)S(1)}, bf16[1,64,4096]{2,1,0:T(8,128)(2,1)S(1)}, u32[]{:S(2)}, u32[]{:S(2)}) collective-permute-start(bf16[1,64,4096]{2,1,0:T(8,128)(2,1)S(1)} %copy-done.1), channel_id=1, source_target_pairs={{0,8},{8,16},{16,24},{1,9},{9,17},{17,25},{2,10},{10,18},{18,26},{... | collective-permute-start | bytes 1572872 | tf_op jit(solution)/shard_map/ppermute | solution.py:12
Sparse Core Ops, SparseCore 0:
  31.8 45.3 reduce-scatter.1
where the time goes:
time: 86.4 us; the launch traced here: 86.1 us
  waiting for transfers between devices  44.2 us (51%)
  blocking collectives  13.9 us (16%)
  between operations  13.5 us (16%)
  matrix products  7.75 us (9%)
  other arithmetic  3.78 us (4%)
  local copies, waits for them, and re-layouts  1.67 us (2%)
  starting transfers between devices  1.32 us (2%)
    reduce_scatter x1, waiting for transfers between devices, on_device(): lax.psum_scatter(partial_value.astype(jnp.bfloat16), 'tp', scatter_dimens...  42.7 us
    all_gather x1, blocking collectives, on_device(): lax.all_gather(attended, 'ctx', axis=0, tiled=True)  8.06 us
    dot_general x1, matrix products, on_device(): jnp.dot(lax.all_gather(attended, 'ctx', axis=0, tiled=True), out_weight,...  7.11 us
    all_gather x1, blocking collectives, on_device(): pieces = lax.all_gather(stacked, 'ctx', axis=1, tiled=True)  5.86 us
    broadcast_in_dim x1, other arithmetic, on_device(): return (resid_in.astype(jnp.float32) + summed).astype(jnp.bfloat16)[None]  2.02 us
  transfers between devices with their start and end apart: 2, of which 2 were waited for; matrix products, arithmetic and copies ran while one was open for 0% of the time, Pallas kernels for 0%

commit v1 on v0

--- a/solution.py
+++ b/solution.py
@@ -1,15 +1,260 @@
 import jax
 import jax.numpy as jnp
 from jax import lax
+from jax.experimental import pallas as pl
+from jax.experimental.pallas import tpu as pltpu
 from jax.sharding import PartitionSpec as P
 
 HEAD_DIM = 128
+NEG = -1e30
+VMEM = pl.BlockSpec(memory_space=pltpu.VMEM)
+HBM = pl.BlockSpec(memory_space=pltpu.HBM)
+F32 = jnp.float32
+BF16 = jnp.bfloat16
+
+
+def kernel_call(body, out_shape, in_specs, scratch=(), flops=0, moved=0, mib=16):
+    return pl.pallas_call(
+        body,
+        out_shape=out_shape,
+        in_specs=in_specs,
+        out_specs=jax.tree.map(lambda _: VMEM, out_shape),
+        scratch_shapes=list(scratch),
+        compiler_params=pltpu.CompilerParams(vmem_limit_bytes=mib * 1024 * 1024),
+        cost_estimate=pl.CostEstimate(flops=flops, bytes_accessed=moved, transcendentals=0),
+    )
+
+
+def row_blocks(i):
+    return i ^ 3, i ^ 1, i ^ 2, i
+
+
+def pack(q, k, v, seg):
+    rows, width = q.shape[0] // 2, q.shape[1]
+    kw = k.shape[1]
+
+    def body(q_ref, k_ref, v_ref, s_ref, x_ref, y_ref, seg_ref, sems):
+        low = lax.axis_index("tp") & 1
+        pieces = [(q_ref.at[pl.ds(pl.multiple_of((1 - low) * rows, rows), rows)], x_ref.at[:, 0:width])]
+        at = width
+        for ref in (k_ref, v_ref):
+            for part in range(2):
+                pieces.append((ref.at[part * rows:(part + 1) * rows], x_ref.at[:, at:at + kw]))
+                at += kw
+        pieces.append((q_ref.at[pl.ds(pl.multiple_of(low * rows, rows), rows)], y_ref))
+        pieces.append((s_ref, seg_ref))
+        copies = [pltpu.make_async_copy(a, b, sems.at[n]) for n, (a, b) in enumerate(pieces)]
+        for copy in copies:
+            copy.start()
+        for copy in copies:
+            copy.wait()
+
+    return kernel_call(
+        body,
+        (
+            jax.ShapeDtypeStruct((rows, width + 4 * kw), q.dtype),
+            jax.ShapeDtypeStruct((rows, width), q.dtype),
+            jax.ShapeDtypeStruct(seg.shape, seg.dtype),
+        ),
+        [HBM] * 4,
+        [pltpu.SemaphoreType.DMA((7,))],
+        moved=4 * q.size,
+        mib=58,
+    )(q, k, v, seg)
+
+
+def prepare(seg, weight, rows):
+    half = 2 * rows
+    parts = 8
+
+    def body(seg_ref, w_ref, wo_ref, bias_ref, col_ref, sems):
+        depth = w_ref.shape[0] // parts
+        copies = []
+        for p in range(parts):
+            at = pl.ds(p * depth, depth)
+            copies.append(pltpu.make_async_copy(w_ref.at[at], wo_ref.at[at], sems.at[p]))
+        for copy in copies:
+            copy.start()
+        c = lax.axis_index("ctx")
+        seg_all = seg_ref[...].astype(F32)
+        col_ref[...] = jnp.transpose(jnp.broadcast_to(seg_all, (128, 2 * half)))
+        low, high = seg_all[:, :half], seg_all[:, half:]
+        seg_keys = jnp.concatenate((jnp.where(c == 0, low, high), jnp.where(c == 0, high, low)), axis=1)
+        column = lax.broadcasted_iota(jnp.int32, (rows, 2 * half), 1)
+        key_place = jnp.where(column < half, column + c * half, column - c * half)
+        for b, block in enumerate(row_blocks(lax.axis_index("tp"))):
+            at = pl.multiple_of(block * rows, rows)
+            row_place = lax.broadcasted_iota(jnp.int32, (rows, 2 * half), 0) + at
+            allowed = (row_place >= key_place) & (col_ref[pl.ds(at, rows), 0:1] == seg_keys)
+            bias_ref[b * rows:(b + 1) * rows, :] = jnp.where(allowed, 0.0, NEG)
+        for copy in copies:
+            copy.wait()
+
+    return kernel_call(
+        body,
+        (jax.ShapeDtypeStruct(weight.shape, weight.dtype), jax.ShapeDtypeStruct((4 * rows, 2 * half), F32)),
+        [VMEM, HBM],
+        [pltpu.VMEM((2 * half, 128), F32), pltpu.SemaphoreType.DMA((parts,))],
+        moved=weight.size * 4,
+    )(seg, weight)
+
+
+def keys_values(mine, other, width):
+    kw = (mine.shape[1] - width) // 4
+
+    def piece(ref, n):
+        return ref[:, width + n * kw:width + (n + 1) * kw]
+
+    k = jnp.concatenate([piece(r, n) for r in (mine, other) for n in (0, 1)], axis=0)
+    v = jnp.concatenate([piece(r, n) for r in (mine, other) for n in (2, 3)], axis=0)
+    return k, v
+
+
+def attend(q, k, v, bias):
+    rows = q.shape[0]
+    heads = q.shape[1] // HEAD_DIM
+    stacked = jnp.concatenate([q[:, h * HEAD_DIM:(h + 1) * HEAD_DIM] for h in range(heads)], axis=0)
+    s = lax.dot_general(stacked, k, (((1,), (1,)), ((), ())), preferred_element_type=F32)
+    s = (s.reshape(heads, rows, -1) + bias[None]).reshape(heads * rows, -1)
+    top = jnp.max(s, axis=1, keepdims=True)
+    p = jnp.exp((s - top) * (HEAD_DIM ** -0.5))
+    total = jnp.sum(p, axis=1, keepdims=True)
+    o = jnp.dot(p.astype(BF16), v, preferred_element_type=F32)
+    o = (o / total).astype(BF16)
+    return jnp.concatenate([o[h * rows:(h + 1) * rows] for h in range(heads)], axis=1)
+
+
+def product(att, w_ref, at, width, store, tile=512):
+    for t in range(0, width, tile):
+        store(t, tile, jnp.dot(att, w_ref[:, at + t:at + t + tile], preferred_element_type=F32))
+
+
+def choose(c, i, mine, other):
+    return jnp.where(c == i >> 1, mine, other)
+
+
+def first_block(mine, other, width, bias, weight):
+    rows = mine.shape[0]
+    cols = weight.shape[1] // 2
+
+    def body(mine_ref, other_ref, bias_ref, w_ref, a0_ref, a1_ref, att_ref):
+        c, i = lax.axis_index("ctx"), lax.axis_index("tp")
+        q = choose(c, i, other_ref[:, :width], mine_ref[:, :width])
+        k, v = keys_values(mine_ref, other_ref, width)
+        att_ref[...] = attend(q, k, v, bias_ref[:rows])
+
+        def store(t, tile, part):
+            ref = a0_ref if t < cols else a1_ref
+            ref[:, t % cols:t % cols + tile] = part.astype(BF16)
+
+        product(att_ref[...], w_ref, 0, 2 * cols, store)
+
+    out = jax.ShapeDtypeStruct((rows, cols), BF16)
+    return kernel_call(
+        body,
+        (out, out),
+        [VMEM] * 4,
+        [pltpu.VMEM((rows, width), BF16)],
+        flops=4 * rows * width * cols,
+        moved=weight.size * 2,
+    )(mine, other, bias, weight)
+
+
+def add_parts(n, rows, cols, att, w_ref, at, got_ref, m_ref, f_ref, o_ref):
+    def store(t, tile, part):
+        m_ref[:, t:t + tile] = part[:rows].astype(BF16)
+        f_ref[:, t:t + tile] = (part[rows:2 * rows] + got_ref[:, t:t + tile].astype(F32)).astype(BF16)
+        o_ref[:, t:t + tile] = part[2 * rows:]
+
+    product(att, w_ref, at, cols, store)
+
+
+def other_first(mine, other, qy, ry, bias, weight, got):
+    rows, width = qy.shape
+    cols = weight.shape[1] // 2
+
+    def body(mine_ref, other_ref, qy_ref, ry_ref, bias_ref, w_ref, got_ref, m_ref, f_ref, o_ref, att_ref):
+        c, i = lax.axis_index("ctx"), lax.axis_index("tp")
+        k, v = keys_values(mine_ref, other_ref, width)
+        blocks = (
+            choose(c, i, mine_ref[:, :width], other_ref[:, :width]),
+            choose(c, i, ry_ref[...], qy_ref[...]),
+            choose(c, i, qy_ref[...], ry_ref[...]),
+        )
+        for b, q in enumerate(blocks):
+            att_ref[b * rows:(b + 1) * rows, :] = attend(q, k, v, bias_ref[(b + 1) * rows:(b + 2) * rows])
+        add_parts(3, rows, cols, att_ref[...], w_ref, 0, got_ref, m_ref, f_ref, o_ref)
+
+    part = jax.ShapeDtypeStruct((rows, cols), BF16)
+    return kernel_call(
+        body,
+        (part, part, jax.ShapeDtypeStruct((rows, cols), F32), jax.ShapeDtypeStruct((3 * rows, width), BF16)),
+        [VMEM] * 7,
+        flops=6 * rows * width * cols,
+        moved=weight.size * 2,
+    )(mine, other, qy, ry, bias, weight, got)
+
+
+def other_second(att, weight, got):
+    rows, width = att.shape[0] // 3, att.shape[1]
+    cols = weight.shape[1] // 2
+
+    def body(att_ref, w_ref, got_ref, m_ref, f_ref, o_ref):
+        add_parts(3, rows, cols, att_ref[...], w_ref, cols, got_ref, m_ref, f_ref, o_ref)
+
+    part = jax.ShapeDtypeStruct((rows, cols), BF16)
+    return kernel_call(
+        body,
+        (part, part, jax.ShapeDtypeStruct((rows, cols), F32)),
+        [VMEM] * 3,
+        flops=6 * rows * width * cols,
+        moved=weight.size,
+    )(att, weight, got)
+
+
+def swap(x, axis, by):
+    peers = lax.axis_size(axis)
+    return lax.ppermute(x, axis, [(i, i ^ by) for i in range(peers)])
+
+
+def after(x, *others):
+    return lax.optimization_barrier((x,) + others)[0]
 
 
 def passed_along(shard, axis, by):
     peers = lax.axis_size(axis)
     pairs = [(i, i + by) for i in range(peers) if 0 <= i + by < peers]
     return lax.ppermute(shard, axis, pairs)
+
+
+def residual(embedded, hidden_prev):
+    arrived = passed_along(hidden_prev, "phase", 1)
+    return jnp.where(lax.axis_index("phase") == 0, embedded, arrived[0])
+
+
+def on_pair(queries, keys, values, seg_ids, out_weight, embedded, hidden_prev):
+    q = queries[0]
+    rows, width = q.shape[0] // 2, q.shape[1]
+    mine, qy, seg = pack(q, keys[0], values[0], seg_ids)
+    other = swap(mine, "ctx", 1)
+    weight, bias = prepare(seg, out_weight, rows)
+    a0, a1 = first_block(mine, other, width, bias, weight)
+    ry = swap(after(qy, a0), "ctx", 1)
+    got0 = swap(a0, "tp", 1)
+    got1 = swap(a1, "tp", 1)
+    m0, f0, own0, att = other_first(mine, other, qy, ry, bias, weight, got0)
+    gotm0 = swap(m0, "tp", 1)
+    y0 = swap(f0, "tp", 2)
+    m1, f1, own1 = other_second(att, weight, got1)
+    gotm1 = swap(m1, "tp", 1)
+    y1 = swap(f1, "tp", 2)
+    prev = after(hidden_prev, a1)
+    cols = weight.shape[1] // 2
+    base0 = own0 + residual(embedded[:, :cols], prev[:, :, :cols]).astype(F32) + gotm0.astype(F32)
+    base1 = own1 + residual(embedded[:, cols:], prev[:, :, cols:]).astype(F32) + gotm1.astype(F32)
+    base0, base1 = lax.optimization_barrier((base0, base1, y0))[:2]
+    out = jnp.concatenate((base0 + y0.astype(F32), base1 + y1.astype(F32)), axis=1)
+    return out.astype(BF16)[None]
 
 
 def on_device(queries, keys, values, seg_ids, out_weight, embedded, hidden_prev):
@@ -38,8 +283,8 @@
         jnp.einsum("qkgd,nkd->qkgn", query_grid, key_grid, preferred_element_type=jnp.float32)
         * score_scale
     )
-    running_max = jnp.full((shard_rows, kv_local, group_size), -1e30, jnp.float32)
-    new_max = jnp.maximum(running_max, jnp.max(jnp.where(mask_grid, scores, -1e30), axis=3))
+    running_max = jnp.full((shard_rows, kv_local, group_size), NEG, jnp.float32)
+    new_max = jnp.maximum(running_max, jnp.max(jnp.where(mask_grid, scores, NEG), axis=3))
     probs = jnp.where(mask_grid, jnp.exp(scores - new_max[..., None]), 0.0)
     new_sum = jnp.sum(probs, axis=3)
     new_out = jnp.einsum(
@@ -58,14 +303,14 @@
     summed = lax.psum_scatter(
         partial_value.astype(jnp.bfloat16), "tp", scatter_dimension=0, tiled=True
     ).astype(jnp.float32)
-    arrived = passed_along(hidden_prev, "phase", 1)
-    resid_in = jnp.where(lax.axis_index("phase") == 0, embedded, arrived[0])
+    resid_in = residual(embedded, hidden_prev)
     return (resid_in.astype(jnp.float32) + summed).astype(jnp.bfloat16)[None]
 
 
 def solution(mesh):
+    fast = mesh.shape["ctx"] == 2 and mesh.shape["tp"] == 4
     return jax.shard_map(
-        on_device,
+        on_pair if fast else on_device,
         mesh=mesh,
         in_specs=(
             P("phase", "ctx", "tp"),

time: 86.4 us -> 52.9 us (0.61)
  waiting for transfers between devices: 44.2 us -> 19.8 us
  starting transfers between devices: 1.32 us -> 19.2 us
  blocking collectives: 13.9 us -> 0 us
  between operations: 13.5 us -> 0.1 us
  matrix products: 7.75 us -> 0 us
  Pallas kernels: 0 us -> 7.2 us
  local copies, waits for them, and re-layouts: 1.67 us -> 4.07 us
  other arithmetic: 3.78 us -> 2.29 us
    reduce_scatter x1 -> x0, waiting for transfers between devices: 42.7 us -> none  [on_device(): lax.psum_scatter(partial_value.astype(jnp.bfloat16), 'tp', scatter_dimens...]
    ppermute x0 -> x8, waiting for transfers between devices: none -> 19.8 us  [swap(): return lax.ppermute(x, axis, [(i, i ^ by) for i in range(peers)])]
    all_gather x2 -> x0, blocking collectives: 13.9 us -> none  [the longest x1 8.06 us: on_device(): lax.all_gather(attended, 'ctx', axis=0, tiled=True)]
    ppermute x0 -> x8, starting transfers between devices: none -> 12.9 us  [swap(): return lax.ppermute(x, axis, [(i, i ^ by) for i in range(peers)])]
    dot_general x3 -> x0, matrix products: 7.75 us -> none  [the longest x1 7.11 us: on_device(): jnp.dot(lax.all_gather(attended, 'ctx', axis=0, tiled=True), out_weight,...]
    pallas_call x0 -> x5, Pallas kernels: none -> 7.2 us  [the longest x1 1.89 us: first_block(): kernel_call(body, (out, out), [VMEM] * 4, [pltpu.VMEM((rows, width), BF16...]
    ppermute x1 -> x2, starting transfers between devices: 1.32 us -> 6.26 us  [passed_along(): return lax.ppermute(shard, axis, pairs)]
    unnamed x5 -> x12, local copies, waits for them, and re-layouts: 1 us -> 4.04 us
  transfers between devices with their start and end apart: 2 -> 10, of which waited for: 2 -> 4; matrix products, arithmetic and copies ran while one was open for 0% -> 3% of each run, Pallas kernels for 0% -> 7%
where the time goes in v1:
time: 52.9 us; the launch traced here: 52.7 us
  waiting for transfers between devices  19.8 us (37%)
  starting transfers between devices  19.2 us (36%)
  Pallas kernels  7.2 us (14%)
  local copies, waits for them, and re-layouts  4.07 us (8%)
  other arithmetic  2.29 us (4%)
    ppermute x8, waiting for transfers between devices, swap(): return lax.ppermute(x, axis, [(i, i ^ by) for i in range(peers)])  19.8 us
    ppermute x8, starting transfers between devices, swap(): return lax.ppermute(x, axis, [(i, i ^ by) for i in range(peers)])  12.9 us
    ppermute x2, starting transfers between devices, passed_along(): return lax.ppermute(shard, axis, pairs)  6.26 us
    unnamed x12, local copies, waits for them, and re-layouts  4.04 us
    pallas_call x1, Pallas kernels, first_block(): kernel_call(body, (out, out), [VMEM] * 4, [pltpu.VMEM((rows, width), BF16...  1.89 us
    pallas_call x1, Pallas kernels, pack(): kernel_call(body, (jax.ShapeDtypeStruct((rows, width + 4 * kw), q.dtype),...  1.82 us
    pallas_call x1, Pallas kernels, other_first(): kernel_call(body, (part, part, jax.ShapeDtypeStruct((rows, cols), F32), j...  1.62 us
    add x1, other arithmetic, on_pair(): own1 + residual(embedded[:, cols:], prev[:, :, cols:]).astype(F32)  1.36 us
  transfers between devices with their start and end apart: 10, of which 4 were waited for; matrix products, arithmetic and copies ran while one was open for 3% of the time, Pallas kernels for 7%

profile of v1, /device:TPU:0, one launch (start us, length us, event | category | flops | bytes accessed | tf_op | source)
XLA Modules:
  0.0 52.7 jit_solution(6993948012996158626)
XLA Ops:
  0.0 1.8 %shard_map.73 = (bf16[64,1536]{1,0:T(8,128)(2,1)}, bf16[64,1024]{1,0:T(8,128)(2,1)}, s32[1,256]{1,0:T(1,128)}) custom-call(bf16[128,1024]{1,0:T(8,128)(2,1)} %bitcast.15, bf16[128,128]{1,0:T(8,128)(2,1)} %bitcast.16, bf16[128,128]{1,0:T(8,128)(2,1)} %bitcast.17, s32[1,256]{1,0:T(1,128)} %s_ref.1), custom_call_target="tpu_custom_call" | custom-call | bytes 524288 | tf_op jit(solution)/shard_map/pallas_call | solution.py:52
  1.8 3.0 %collective-permute-start = (bf16[64,1536]{1,0:T(8,128)(2,1)}, bf16[64,1536]{1,0:T(8,128)(2,1)S(1)}, u32[]{:S(2)}, u32[]{:S(2)}) collective-permute-start(bf16[64,1536]{1,0:T(8,128)(2,1)} %get-tuple-element.23.mine_ref), channel_id=1, source_target_pairs={{0,4},{4,0},{1,5},{5,1},{2,6},{6,2},{3,7},{7,3},{8,12},{12,8},{9,1... | collective-permute-start | bytes 589832 | tf_op jit(solution)/shard_map/ppermute | solution.py:217
  4.9 3.4 %copy-done = bf16[1024,4096]{1,0:T(8,128)(2,1)S(1)} copy-done((bf16[1024,4096]{1,0:T(8,128)(2,1)S(1)}, bf16[1024,4096]{1,0:T(8,128)(2,1)}, u32[]{:S(2)}) %copy-start) | copy-done | bytes 8388632
  8.2 0.6 %copy-done.3 = s32[1,256]{1,0:T(1,128)S(1)} copy-done((s32[1,256]{1,0:T(1,128)S(1)}, s32[1,256]{1,0:T(1,128)}, u32[]{:S(2)}) %copy-start.3) | copy-done | bytes 1048
  8.9 0.9 %shard_map.74 = (bf16[1024,4096]{1,0:T(8,128)(2,1)S(1)}, f32[256,256]{1,0:T(8,128)S(1)}) custom-call(s32[1,256]{1,0:T(1,128)S(1)} %copy-done.3, bf16[1024,4096]{1,0:T(8,128)(2,1)S(1)} %copy-done), custom_call_target="tpu_custom_call" | custom-call | bytes 16777216 | tf_op jit(solution)/shard_map/pallas_call | solution.py:93
  9.7 0.2 collective-permute-done.other_ref
  10.0 0.0 copy-done.1
  10.0 1.9 %shard_map.75 = (bf16[64,2048]{1,0:T(8,128)(2,1)S(1)}, bf16[64,2048]{1,0:T(8,128)(2,1)S(1)}) custom-call(bf16[64,1536]{1,0:T(8,128)(2,1)S(1)} %copy-done.1, bf16[64,1536]{1,0:T(8,128)(2,1)S(1)} %collective-permute-done.other_ref, f32[256,256]{1,0:T(8,128)S(1)} %get-tuple-element.26.bias_ref, bf16[1024,4096]{1,0:T(8,128)(2,1)S(1)} %get-tuple-element.27.w_ref), custom_call_target="tpu_custom_call" | custom-call | flops 536870912 | bytes 8388608 | tf_op jit(solution)/shard_map/pallas_call | solution.py:153
  11.9 1.9 %collective-permute-start.2 = (bf16[64,2048]{1,0:T(8,128)(2,1)S(1)}, bf16[64,2048]{1,0:T(8,128)(2,1)S(1)}, u32[]{:S(2)}, u32[]{:S(2)}) collective-permute-start(bf16[64,2048]{1,0:T(8,128)(2,1)S(1)} %get-tuple-element.28), channel_id=1, source_target_pairs={{0,1},{1,0},{2,3},{3,2},{4,5},{5,4},{6,7},{7,6},{8,9},{9,8},{10,11... | collective-permute-start | bytes 786440 | tf_op jit(solution)/shard_map/ppermute | solution.py:217
  13.7 0.2 collective-permute-start.5
  14.0 1.7 %collective-permute-start.1 = (bf16[64,1024]{1,0:T(8,128)(2,1)S(1)}, bf16[64,1024]{1,0:T(8,128)(2,1)S(1)}, u32[]{:S(2)}, u32[]{:S(2)}) collective-permute-start(bf16[64,1024]{1,0:T(8,128)(2,1)S(1)} %copy-done.2), channel_id=1, source_target_pairs={{0,4},{4,0},{1,5},{5,1},{2,6},{6,2},{3,7},{7,3},{8,12},{12,8},{9,1... | collective-permute-start | bytes 393224 | tf_op jit(solution)/shard_map/ppermute | solution.py:217
  15.7 0.0 copy-done.4
  15.7 1.3 %collective-permute-start.6 = (bf16[1,64,2048]{2,1,0:T(8,128)(2,1)S(1)}, bf16[1,64,2048]{2,1,0:T(8,128)(2,1)S(1)}, u32[]{:S(2)}, u32[]{:S(2)}) collective-permute-start(bf16[1,64,2048]{2,1,0:T(8,128)(2,1)S(1)} %get-tuple-element.43), channel_id=1, source_target_pairs={{0,8},{8,16},{16,24},{1,9},{9,17},{17,25},{2,10},{10,18},{18,26},{... | collective-permute-start | bytes 786440 | tf_op jit(solution)/shard_map/ppermute | solution.py:227
  17.1 0.0 copy-start.5
  17.1 5.0 %collective-permute-start.3 = (bf16[1,64,2048]{2,1,0:T(8,128)(2,1)S(1)}, bf16[1,64,2048]{2,1,0:T(8,128)(2,1)}, u32[]{:S(2)}, u32[]{:S(2)}) collective-permute-start(bf16[1,64,2048]{2,1,0:T(8,128)(2,1)S(1)} %get-tuple-element.44), channel_id=1, source_target_pairs={{0,8},{8,16},{16,24},{1,9},{9,17},{17,25},{2,10},{10,18},{18,26},{... | collective-permute-start | bytes 786440 | tf_op jit(solution)/shard_map/ppermute | solution.py:227
  22.0 0.0 collective-permute-done.1.ry_ref
  22.0 0.0 collective-permute-done.2.got_ref
  22.0 1.6 %shard_map.76 = (bf16[64,2048]{1,0:T(8,128)(2,1)S(1)}, bf16[64,2048]{1,0:T(8,128)(2,1)S(1)}, f32[64,2048]{1,0:T(8,128)S(1)}, bf16[192,1024]{1,0:T(8,128)(2,1)S(1)}) custom-call(bf16[64,1536]{1,0:T(8,128)(2,1)S(1)} %copy-done.1, bf16[64,1536]{1,0:T(8,128)(2,1)S(1)} %collective-permute-done.other_ref, bf16[64,1024]{1,0:T(8,128)(2,1)S(1)} %copy-done.2, ...), custom_call_target="tpu_custom_call" | custom-call | flops 805306368 | bytes 8388608 | tf_op jit(solution)/shard_map/pallas_call | solution.py:189
  23.7 1.6 %collective-permute-start.4 = (bf16[64,2048]{1,0:T(8,128)(2,1)S(1)}, bf16[64,2048]{1,0:T(8,128)(2,1)}, u32[]{:S(2)}, u32[]{:S(2)}) collective-permute-start(bf16[64,2048]{1,0:T(8,128)(2,1)S(1)} %get-tuple-element.33), channel_id=1, source_target_pairs={{0,1},{1,0},{2,3},{3,2},{4,5},{5,4},{6,7},{7,6},{8,9},{9,8},{10,11... | collective-permute-start | bytes 786440 | tf_op jit(solution)/shard_map/ppermute | solution.py:217
  25.3 0.0 collective-permute-done.5.got_ref
  25.3 1.0 %shard_map.77 = (bf16[64,2048]{1,0:T(8,128)(2,1)S(1)}, bf16[64,2048]{1,0:T(8,128)(2,1)S(1)}, f32[64,2048]{1,0:T(8,128)S(1)}) custom-call(bf16[192,1024]{1,0:T(8,128)(2,1)S(1)} %get-tuple-element.34.att_ref, bf16[1024,4096]{1,0:T(8,128)(2,1)S(1)} %get-tuple-element.27.w_ref, bf16[64,2048]{1,0:T(8,128)(2,1)S(1)} %collective-permute-done.5.got_ref), custom_call_target="tpu_custom_call" | custom-call | flops 805306368 | bytes 4194304 | tf_op jit(solution)/shard_map/pallas_call | solution.py:206
  26.3 1.5 %collective-permute-start.7 = (bf16[64,2048]{1,0:T(8,128)(2,1)S(1)}, bf16[64,2048]{1,0:T(8,128)(2,1)}, u32[]{:S(2)}, u32[]{:S(2)}) collective-permute-start(bf16[64,2048]{1,0:T(8,128)(2,1)S(1)} %get-tuple-element.36), channel_id=1, source_target_pairs={{0,1},{1,0},{2,3},{3,2},{4,5},{5,4},{6,7},{7,6},{8,9},{9,8},{10,11... | collective-permute-start | bytes 786440 | tf_op jit(solution)/shard_map/ppermute | solution.py:217
  27.8 2.6 %collective-permute-start.8 = (bf16[64,2048]{1,0:T(8,128)(2,1)S(1)}, bf16[64,2048]{1,0:T(8,128)(2,1)S(1)}, u32[]{:S(2)}, u32[]{:S(2)}) collective-permute-start(bf16[64,2048]{1,0:T(8,128)(2,1)S(1)} %get-tuple-element.37), channel_id=1, source_target_pairs={{0,2},{1,3},{2,0},{3,1},{4,6},{5,7},{6,4},{7,5},{8,10},{9,11},{10,... | collective-permute-start | bytes 786440 | tf_op jit(solution)/shard_map/ppermute | solution.py:217
  30.4 0.0 collective-permute-done.6
  30.4 0.3 collective-permute-start.9
  30.8 0.0 collective-permute-done.3
  30.8 12.0 %collective-permute-done.4 = bf16[64,2048]{1,0:T(8,128)(2,1)} collective-permute-done((bf16[64,2048]{1,0:T(8,128)(2,1)S(1)}, bf16[64,2048]{1,0:T(8,128)(2,1)}, u32[]{:S(2)}, u32[]{:S(2)}) %collective-permute-start.4) | collective-permute-done | bytes 262176 | tf_op jit(solution)/shard_map/ppermute | solution.py:217
  42.8 3.9 %collective-permute-done.7 = bf16[64,2048]{1,0:T(8,128)(2,1)} collective-permute-done((bf16[64,2048]{1,0:T(8,128)(2,1)S(1)}, bf16[64,2048]{1,0:T(8,128)(2,1)}, u32[]{:S(2)}, u32[]{:S(2)}) %collective-permute-start.7) | collective-permute-done | bytes 262176 | tf_op jit(solution)/shard_map/ppermute | solution.py:217
  46.7 1.4 %convert_add_fusion = (f32[64,2048]{1,0:T(8,128)S(1)}, f32[64,2048]{1,0:T(8,128)S(1)}) fusion(bf16[64,2048]{1,0:T(8,128)(2,1)} %collective-permute-done.7, f32[64,2048]{1,0:T(8,128)S(1)} %get-tuple-element.35, bf16[1,64,2048]{2,1,0:T(8,128)(2,1)S(1)} %collective-permute-done.6, bf16[64,4096]{1,0:T(8,128)(2,1)S(1)} %copy-done.5, pred[]{:T(512)S(6)} %eq.4, ...), kind=kLoop, calls=%fused_computation.3 | loop fusion | flops 1310720 | bytes 3670017 | tf_op jit(solution)/shard_map/add | solution.py:254
  48.1 0.0 collective-permute-done.8
  48.1 3.7 %collective-permute-done.9 = bf16[64,2048]{1,0:T(8,128)(2,1)S(1)} collective-permute-done((bf16[64,2048]{1,0:T(8,128)(2,1)S(1)}, bf16[64,2048]{1,0:T(8,128)(2,1)S(1)}, u32[]{:S(2)}, u32[]{:S(2)}) %collective-permute-start.9) | collective-permute-done | bytes 262176 | tf_op jit(solution)/shard_map/ppermute | solution.py:217
  51.8 0.8 %pad_maximum_fusion = bf16[1,64,4096]{2,1,0:T(8,128)(2,1)} fusion(bf16[1,64,2048]{2,1,0:T(8,128)(2,1)S(1)} %fusion.1, bf16[1,64,2048]{2,1,0:T(8,128)(2,1)S(1)} %fusion), kind=kLoop, calls=%fused_computation | loop fusion | flops 1048576 | bytes 1048576 | tf_op jit(solution)/shard_map/concatenate | solution.py:256
  (10 shorter events, 0.1 us)
Async XLA Ops:
  1.8 8.1 %collective-permute-start = (bf16[64,1536]{1,0:T(8,128)(2,1)}, bf16[64,1536]{1,0:T(8,128)(2,1)S(1)}, u32[]{:S(2)}, u32[]{:S(2)}) collective-permute-start(bf16[64,1536]{1,0:T(8,128)(2,1)} %get-tuple-element.23.mine_ref), channel_id=1, source_target_pairs={{0,4},{4,0},{1,5},{5,1},{2,6},{6,2},{3,7},{7,3},{8,12},{12,8},{9,1... | collective-permute-start | bytes 589832 | tf_op jit(solution)/shard_map/ppermute | solution.py:217
  4.9 3.4 %copy-start = (bf16[1024,4096]{1,0:T(8,128)(2,1)S(1)}, bf16[1024,4096]{1,0:T(8,128)(2,1)}, u32[]{:S(2)}) copy-start(bf16[1024,4096]{1,0:T(8,128)(2,1)} %w_ref.1) | copy-start | bytes 25165828
  8.2 0.6 %copy-start.3 = (s32[1,256]{1,0:T(1,128)S(1)}, s32[1,256]{1,0:T(1,128)}, u32[]{:S(2)}) copy-start(s32[1,256]{1,0:T(1,128)} %get-tuple-element.25.seg_ref) | copy-start | bytes 3076
  8.9 1.1 %copy-start.1 = (bf16[64,1536]{1,0:T(8,128)(2,1)S(1)}, bf16[64,1536]{1,0:T(8,128)(2,1)}, u32[]{:S(2)}) copy-start(bf16[64,1536]{1,0:T(8,128)(2,1)} %get-tuple-element.23.mine_ref) | copy-start | bytes 589828
  8.9 5.1 %copy-start.2 = (bf16[64,1024]{1,0:T(8,128)(2,1)S(1)}, bf16[64,1024]{1,0:T(8,128)(2,1)}, u32[]{:S(2)}) copy-start(bf16[64,1024]{1,0:T(8,128)(2,1)} %get-tuple-element.29.qy_ref) | copy-start | bytes 393220
  8.9 6.8 %copy-start.4 = (bf16[1,64,4096]{2,1,0:T(8,128)(2,1)S(1)}, bf16[1,64,4096]{2,1,0:T(8,128)(2,1)}, u32[]{:S(2)}) copy-start(bf16[1,64,4096]{2,1,0:T(8,128)(2,1)} %param.13) | copy-start | bytes 1572868
  11.9 10.2 %collective-permute-start.2 = (bf16[64,2048]{1,0:T(8,128)(2,1)S(1)}, bf16[64,2048]{1,0:T(8,128)(2,1)S(1)}, u32[]{:S(2)}, u32[]{:S(2)}) collective-permute-start(bf16[64,2048]{1,0:T(8,128)(2,1)S(1)} %get-tuple-element.28), channel_id=1, source_target_pairs={{0,1},{1,0},{2,3},{3,2},{4,5},{5,4},{6,7},{7,6},{8,9},{9,8},{10,11... | collective-permute-start | bytes 786440 | tf_op jit(solution)/shard_map/ppermute | solution.py:217
  13.7 11.6 %collective-permute-start.5 = (bf16[64,2048]{1,0:T(8,128)(2,1)S(1)}, bf16[64,2048]{1,0:T(8,128)(2,1)S(1)}, u32[]{:S(2)}, u32[]{:S(2)}) collective-permute-start(bf16[64,2048]{1,0:T(8,128)(2,1)S(1)} %get-tuple-element.31), channel_id=1, source_target_pairs={{0,1},{1,0},{2,3},{3,2},{4,5},{5,4},{6,7},{7,6},{8,9},{9,8},{10,11... | collective-permute-start | bytes 786440 | tf_op jit(solution)/shard_map/ppermute | solution.py:217
  14.0 8.1 %collective-permute-start.1 = (bf16[64,1024]{1,0:T(8,128)(2,1)S(1)}, bf16[64,1024]{1,0:T(8,128)(2,1)S(1)}, u32[]{:S(2)}, u32[]{:S(2)}) collective-permute-start(bf16[64,1024]{1,0:T(8,128)(2,1)S(1)} %copy-done.2), channel_id=1, source_target_pairs={{0,4},{4,0},{1,5},{5,1},{2,6},{6,2},{3,7},{7,3},{8,12},{12,8},{9,1... | collective-permute-start | bytes 393224 | tf_op jit(solution)/shard_map/ppermute | solution.py:217
  15.7 14.7 %collective-permute-start.6 = (bf16[1,64,2048]{2,1,0:T(8,128)(2,1)S(1)}, bf16[1,64,2048]{2,1,0:T(8,128)(2,1)S(1)}, u32[]{:S(2)}, u32[]{:S(2)}) collective-permute-start(bf16[1,64,2048]{2,1,0:T(8,128)(2,1)S(1)} %get-tuple-element.43), channel_id=1, source_target_pairs={{0,8},{8,16},{16,24},{1,9},{9,17},{17,25},{2,10},{10,18},{18,26},{... | collective-permute-start | bytes 786440 | tf_op jit(solution)/shard_map/ppermute | solution.py:227
  17.1 29.6 %copy-start.5 = (bf16[64,4096]{1,0:T(8,128)(2,1)S(1)}, bf16[64,4096]{1,0:T(8,128)(2,1)}, u32[]{:S(2)}) copy-start(bf16[64,4096]{1,0:T(8,128)(2,1)} %param.12) | copy-start | bytes 1572868
  17.1 13.7 %collective-permute-start.3 = (bf16[1,64,2048]{2,1,0:T(8,128)(2,1)S(1)}, bf16[1,64,2048]{2,1,0:T(8,128)(2,1)}, u32[]{:S(2)}, u32[]{:S(2)}) collective-permute-start(bf16[1,64,2048]{2,1,0:T(8,128)(2,1)S(1)} %get-tuple-element.44), channel_id=1, source_target_pairs={{0,8},{8,16},{16,24},{1,9},{9,17},{17,25},{2,10},{10,18},{18,26},{... | collective-permute-start | bytes 786440 | tf_op jit(solution)/shard_map/ppermute | solution.py:227
  23.7 19.1 %collective-permute-start.4 = (bf16[64,2048]{1,0:T(8,128)(2,1)S(1)}, bf16[64,2048]{1,0:T(8,128)(2,1)}, u32[]{:S(2)}, u32[]{:S(2)}) collective-permute-start(bf16[64,2048]{1,0:T(8,128)(2,1)S(1)} %get-tuple-element.33), channel_id=1, source_target_pairs={{0,1},{1,0},{2,3},{3,2},{4,5},{5,4},{6,7},{7,6},{8,9},{9,8},{10,11... | collective-permute-start | bytes 786440 | tf_op jit(solution)/shard_map/ppermute | solution.py:217
  26.3 20.4 %collective-permute-start.7 = (bf16[64,2048]{1,0:T(8,128)(2,1)S(1)}, bf16[64,2048]{1,0:T(8,128)(2,1)}, u32[]{:S(2)}, u32[]{:S(2)}) collective-permute-start(bf16[64,2048]{1,0:T(8,128)(2,1)S(1)} %get-tuple-element.36), channel_id=1, source_target_pairs={{0,1},{1,0},{2,3},{3,2},{4,5},{5,4},{6,7},{7,6},{8,9},{9,8},{10,11... | collective-permute-start | bytes 786440 | tf_op jit(solution)/shard_map/ppermute | solution.py:217
  27.8 20.2 %collective-permute-start.8 = (bf16[64,2048]{1,0:T(8,128)(2,1)S(1)}, bf16[64,2048]{1,0:T(8,128)(2,1)S(1)}, u32[]{:S(2)}, u32[]{:S(2)}) collective-permute-start(bf16[64,2048]{1,0:T(8,128)(2,1)S(1)} %get-tuple-element.37), channel_id=1, source_target_pairs={{0,2},{1,3},{2,0},{3,1},{4,6},{5,7},{6,4},{7,5},{8,10},{9,11},{10,... | collective-permute-start | bytes 786440 | tf_op jit(solution)/shard_map/ppermute | solution.py:217
  30.4 21.4 %collective-permute-start.9 = (bf16[64,2048]{1,0:T(8,128)(2,1)S(1)}, bf16[64,2048]{1,0:T(8,128)(2,1)S(1)}, u32[]{:S(2)}, u32[]{:S(2)}) collective-permute-start(bf16[64,2048]{1,0:T(8,128)(2,1)S(1)} %get-tuple-element.40), channel_id=1, source_target_pairs={{0,2},{1,3},{2,0},{3,1},{4,6},{5,7},{6,4},{7,5},{8,10},{9,11},{10,... | collective-permute-start | bytes 786440 | tf_op jit(solution)/shard_map/ppermute | solution.py:217

commit v2 on v1

--- a/solution.py
+++ b/solution.py
@@ -133,74 +133,66 @@
     return jnp.where(c == i >> 1, mine, other)
 
 
-def first_block(mine, other, width, bias, weight):
+def attend_blocks(mine, other, bias, halves=()):
     rows = mine.shape[0]
-    cols = weight.shape[1] // 2
-
-    def body(mine_ref, other_ref, bias_ref, w_ref, a0_ref, a1_ref, att_ref):
+    width = mine.shape[1] - 4 * HEAD_DIM
+    n = 3 if halves else 1
+
+    def body(mine_ref, other_ref, bias_ref, *rest):
         c, i = lax.axis_index("ctx"), lax.axis_index("tp")
-        q = choose(c, i, other_ref[:, :width], mine_ref[:, :width])
+        att_ref = rest[-1]
         k, v = keys_values(mine_ref, other_ref, width)
-        att_ref[...] = attend(q, k, v, bias_ref[:rows])
-
+        if halves:
+            qy_ref, ry_ref = rest[:2]
+            blocks = (
+                choose(c, i, mine_ref[:, :width], other_ref[:, :width]),
+                choose(c, i, ry_ref[...], qy_ref[...]),
+                choose(c, i, qy_ref[...], ry_ref[...]),
+            )
+        else:
+            blocks = (choose(c, i, other_ref[:, :width], mine_ref[:, :width]),)
+        first = 1 if halves else 0
+        for b, q in enumerate(blocks):
+            att_ref[b * rows:(b + 1) * rows, :] = attend(q, k, v, bias_ref[(first + b) * rows:(first + b + 1) * rows])
+
+    return kernel_call(
+        body,
+        jax.ShapeDtypeStruct((n * rows, width), BF16),
+        [VMEM] * (3 + len(halves)),
+        flops=0,
+        moved=mine.size,
+    )(mine, other, bias, *halves)
+
+
+def first_part(att, weight, at, cols):
+    rows, width = att.shape
+
+    def body(att_ref, w_ref, a_ref):
         def store(t, tile, part):
-            ref = a0_ref if t < cols else a1_ref
-            ref[:, t % cols:t % cols + tile] = part.astype(BF16)
-
-        product(att_ref[...], w_ref, 0, 2 * cols, store)
-
-    out = jax.ShapeDtypeStruct((rows, cols), BF16)
-    return kernel_call(
-        body,
-        (out, out),
-        [VMEM] * 4,
-        [pltpu.VMEM((rows, width), BF16)],
-        flops=4 * rows * width * cols,
-        moved=weight.size * 2,
-    )(mine, other, bias, weight)
-
-
-def add_parts(n, rows, cols, att, w_ref, at, got_ref, m_ref, f_ref, o_ref):
-    def store(t, tile, part):
-        m_ref[:, t:t + tile] = part[:rows].astype(BF16)
-        f_ref[:, t:t + tile] = (part[rows:2 * rows] + got_ref[:, t:t + tile].astype(F32)).astype(BF16)
-        o_ref[:, t:t + tile] = part[2 * rows:]
-
-    product(att, w_ref, at, cols, store)
-
-
-def other_first(mine, other, qy, ry, bias, weight, got):
-    rows, width = qy.shape
-    cols = weight.shape[1] // 2
-
-    def body(mine_ref, other_ref, qy_ref, ry_ref, bias_ref, w_ref, got_ref, m_ref, f_ref, o_ref, att_ref):
-        c, i = lax.axis_index("ctx"), lax.axis_index("tp")
-        k, v = keys_values(mine_ref, other_ref, width)
-        blocks = (
-            choose(c, i, mine_ref[:, :width], other_ref[:, :width]),
-            choose(c, i, ry_ref[...], qy_ref[...]),
-            choose(c, i, qy_ref[...], ry_ref[...]),
-        )
-        for b, q in enumerate(blocks):
-            att_ref[b * rows:(b + 1) * rows, :] = attend(q, k, v, bias_ref[(b + 1) * rows:(b + 2) * rows])
-        add_parts(3, rows, cols, att_ref[...], w_ref, 0, got_ref, m_ref, f_ref, o_ref)
-
-    part = jax.ShapeDtypeStruct((rows, cols), BF16)
-    return kernel_call(
-        body,
-        (part, part, jax.ShapeDtypeStruct((rows, cols), F32), jax.ShapeDtypeStruct((3 * rows, width), BF16)),
-        [VMEM] * 7,
-        flops=6 * rows * width * cols,
-        moved=weight.size * 2,
-    )(mine, other, qy, ry, bias, weight, got)
-
-
-def other_second(att, weight, got):
+            a_ref[:, t:t + tile] = part.astype(BF16)
+
+        product(att_ref[...], w_ref, at, cols, store)
+
+    return kernel_call(
+        body,
+        jax.ShapeDtypeStruct((rows, cols), BF16),
+        [VMEM] * 2,
+        flops=2 * rows * width * cols,
+        moved=weight.size,
+    )(att, weight)
+
+
+def other_parts(att, weight, got, at):
     rows, width = att.shape[0] // 3, att.shape[1]
-    cols = weight.shape[1] // 2
+    cols = got.shape[1]
 
     def body(att_ref, w_ref, got_ref, m_ref, f_ref, o_ref):
-        add_parts(3, rows, cols, att_ref[...], w_ref, cols, got_ref, m_ref, f_ref, o_ref)
+        def store(t, tile, part):
+            m_ref[:, t:t + tile] = part[:rows].astype(BF16)
+            f_ref[:, t:t + tile] = (part[rows:2 * rows] + got_ref[:, t:t + tile].astype(F32)).astype(BF16)
+            o_ref[:, t:t + tile] = part[2 * rows:]
+
+        product(att_ref[...], w_ref, at, cols, store)
 
     part = jax.ShapeDtypeStruct((rows, cols), BF16)
     return kernel_call(
@@ -212,6 +204,54 @@
     )(att, weight, got)
 
 
+def add_far(own, y):
+    def body(o_ref, y_ref, out_ref):
+        out_ref[...] = o_ref[...] + y_ref[...].astype(F32)
+
+    return kernel_call(body, jax.ShapeDtypeStruct(own.shape, F32), [VMEM] * 2, moved=own.size * 10)(own, y)
+
+
+def add_rest(sum0, own1, gotm0, y1, gotm1):
+    rows, cols = sum0.shape
+
+    def body(s_ref, o_ref, m0_ref, y_ref, m1_ref, out_ref):
+        out_ref[:, :cols] = s_ref[...] + m0_ref[...].astype(F32)
+        out_ref[:, cols:] = o_ref[...] + m1_ref[...].astype(F32) + y_ref[...].astype(F32)
+
+    return kernel_call(body, jax.ShapeDtypeStruct((rows, 2 * cols), F32), [VMEM] * 5, moved=sum0.size * 22)(
+        sum0, own1, gotm0, y1, gotm1
+    )
+
+
+def finish(branch, embedded, arrived):
+    rows, cols = branch.shape
+    n = len(arrived)
+    step = cols // n
+
+    def body(b_ref, e_ref, *rest):
+        pieces, out_ref, done_ref, sems = rest[:n], rest[n], rest[n + 1], rest[n + 2]
+        first = lax.axis_index("phase") == 0
+        copies = []
+        for p in range(n):
+            at = slice(p * step, (p + 1) * step)
+            resid = jnp.where(first, e_ref[:, at], pieces[p][...])
+            done_ref[:, at] = (resid.astype(F32) + b_ref[:, at]).astype(BF16)
+            copies.append(pltpu.make_async_copy(done_ref.at[:, at], out_ref.at[:, at], sems.at[p]))
+            copies[-1].start()
+        for copy in copies:
+            copy.wait()
+
+    return pl.pallas_call(
+        body,
+        out_shape=jax.ShapeDtypeStruct((rows, cols), BF16),
+        in_specs=[VMEM] * (2 + n),
+        out_specs=HBM,
+        scratch_shapes=[pltpu.VMEM((rows, cols), BF16), pltpu.SemaphoreType.DMA((n,))],
+        compiler_params=pltpu.CompilerParams(vmem_limit_bytes=16 * 1024 * 1024),
+        cost_estimate=pl.CostEstimate(flops=0, bytes_accessed=branch.size * 10, transcendentals=0),
+    )(branch, embedded, *arrived)
+
+
 def swap(x, axis, by):
     peers = lax.axis_size(axis)
     return lax.ppermute(x, axis, [(i, i ^ by) for i in range(peers)])
@@ -234,27 +274,29 @@
 
 def on_pair(queries, keys, values, seg_ids, out_weight, embedded, hidden_prev):
     q = queries[0]
-    rows, width = q.shape[0] // 2, q.shape[1]
+    rows = q.shape[0] // 2
+    cols = out_weight.shape[1] // 2
     mine, qy, seg = pack(q, keys[0], values[0], seg_ids)
     other = swap(mine, "ctx", 1)
     weight, bias = prepare(seg, out_weight, rows)
-    a0, a1 = first_block(mine, other, width, bias, weight)
+    att = attend_blocks(mine, other, bias)
+    a0 = first_part(att, weight, 0, cols)
+    got0 = swap(a0, "tp", 1)
+    a1 = first_part(att, weight, cols, cols)
+    got1 = swap(a1, "tp", 1)
     ry = swap(after(qy, a0), "ctx", 1)
-    got0 = swap(a0, "tp", 1)
-    got1 = swap(a1, "tp", 1)
-    m0, f0, own0, att = other_first(mine, other, qy, ry, bias, weight, got0)
+    rest = attend_blocks(mine, other, bias, (qy, ry))
+    m0, f0, own0 = other_parts(rest, weight, got0, 0)
     gotm0 = swap(m0, "tp", 1)
     y0 = swap(f0, "tp", 2)
-    m1, f1, own1 = other_second(att, weight, got1)
+    m1, f1, own1 = other_parts(rest, weight, got1, cols)
     gotm1 = swap(m1, "tp", 1)
     y1 = swap(f1, "tp", 2)
-    prev = after(hidden_prev, a1)
-    cols = weight.shape[1] // 2
-    base0 = own0 + residual(embedded[:, :cols], prev[:, :, :cols]).astype(F32) + gotm0.astype(F32)
-    base1 = own1 + residual(embedded[:, cols:], prev[:, :, cols:]).astype(F32) + gotm1.astype(F32)
-    base0, base1 = lax.optimization_barrier((base0, base1, y0))[:2]
-    out = jnp.concatenate((base0 + y0.astype(F32), base1 + y1.astype(F32)), axis=1)
-    return out.astype(BF16)[None]
+    prev = after(hidden_prev, f1)[0]
+    arrived = [passed_along(prev[:, at:at + cols], "phase", 1) for at in (0, cols)]
+    sum0 = add_far(own0, y0)
+    branch = add_rest(sum0, own1, gotm0, y1, gotm1)
+    return finish(branch, embedded, arrived)[None]
 
 
 def on_device(queries, keys, values, seg_ids, out_weight, embedded, hidden_prev):

time: 52.9 us -> 48.4 us (0.915)
  waiting for transfers between devices: 19.8 us -> 16.7 us
  other arithmetic: 2.29 us -> 0 us
  Pallas kernels: 7.2 us -> 8.68 us
  starting transfers between devices: 19.2 us -> 18.5 us
    ppermute x8, waiting for transfers between devices: 19.8 us -> 16.7 us  [swap(): return lax.ppermute(x, axis, [(i, i ^ by) for i in range(peers)])]
    pallas_call x3 -> x9, Pallas kernels: 4.53 us -> 6.01 us  [the longest x2 2.05 us: other_parts(): kernel_call(body, (part, part, jax.ShapeDtypeStruct((rows, cols), F32)),...]
    ppermute x2, starting transfers between devices: 6.26 us -> 4.79 us  [passed_along(): return lax.ppermute(shard, axis, pairs)]
    add x1 -> x0, other arithmetic: 1.36 us -> none  [on_pair(): own1 + residual(embedded[:, cols:], prev[:, :, cols:]).astype(F32)]
    concatenate x3 -> x0, other arithmetic: 0.92 us -> none  [on_pair(): jnp.concatenate((base0 + y0.astype(F32), base1 + y1.astype(F32)), axis=1)]
    ppermute x8, starting transfers between devices: 12.9 us -> 13.7 us  [swap(): return lax.ppermute(x, axis, [(i, i ^ by) for i in range(peers)])]
  transfers between devices with their start and end apart: 10 -> 10, of which waited for: 4 -> 8; matrix products, arithmetic and copies ran while one was open for 3% -> 0% of each run, Pallas kernels for 7% -> 10%
where the time goes in v2:
time: 48.4 us; the launch traced here: 48.1 us
  starting transfers between devices  18.5 us (38%)
  waiting for transfers between devices  16.7 us (35%)
  Pallas kernels  8.68 us (18%)
  local copies, waits for them, and re-layouts  4.12 us (9%)
    ppermute x8, waiting for transfers between devices, swap(): return lax.ppermute(x, axis, [(i, i ^ by) for i in range(peers)])  16.7 us
    ppermute x8, starting transfers between devices, swap(): return lax.ppermute(x, axis, [(i, i ^ by) for i in range(peers)])  13.7 us
    ppermute x2, starting transfers between devices, passed_along(): return lax.ppermute(shard, axis, pairs)  4.79 us
    unnamed x12, local copies, waits for them, and re-layouts  4.08 us
    pallas_call x2, Pallas kernels, other_parts(): kernel_call(body, (part, part, jax.ShapeDtypeStruct((rows, cols), F32)),...  2.05 us
    pallas_call x1, Pallas kernels, pack(): kernel_call(body, (jax.ShapeDtypeStruct((rows, width + 4 * kw), q.dtype),...  1.82 us
    pallas_call x2, Pallas kernels, first_part(): kernel_call(body, jax.ShapeDtypeStruct((rows, cols), BF16), [VMEM] * 2, f...  1.67 us
    pallas_call x2, Pallas kernels, attend_blocks(): kernel_call(body, jax.ShapeDtypeStruct((n * rows, width), BF16), [VMEM] *...  1.26 us
  transfers between devices with their start and end apart: 10, of which 8 were waited for; matrix products, arithmetic and copies ran while one was open for 0% of the time, Pallas kernels for 10%

profile of v2, /device:TPU:0, one launch (start us, length us, event | category | flops | bytes accessed | tf_op | source)
XLA Modules:
  0.0 48.1 jit_solution(4822880191121317211)
XLA Ops:
  0.0 1.8 %shard_map.73 = (bf16[64,1536]{1,0:T(8,128)(2,1)}, bf16[64,1024]{1,0:T(8,128)(2,1)}, s32[1,256]{1,0:T(1,128)}) custom-call(bf16[128,1024]{1,0:T(8,128)(2,1)} %bitcast.6, bf16[128,128]{1,0:T(8,128)(2,1)} %bitcast.7, bf16[128,128]{1,0:T(8,128)(2,1)} %bitcast.8, s32[1,256]{1,0:T(1,128)} %s_ref.1), custom_call_target="tpu_custom_call" | custom-call | bytes 524288 | tf_op jit(solution)/shard_map/pallas_call | solution.py:52
  1.8 3.0 %collective-permute-start = (bf16[64,1536]{1,0:T(8,128)(2,1)}, bf16[64,1536]{1,0:T(8,128)(2,1)S(1)}, u32[]{:S(2)}, u32[]{:S(2)}) collective-permute-start(bf16[64,1536]{1,0:T(8,128)(2,1)} %get-tuple-element.18.mine_ref), channel_id=1, source_target_pairs={{0,4},{4,0},{1,5},{5,1},{2,6},{6,2},{3,7},{7,3},{8,12},{12,8},{9,1... | collective-permute-start | bytes 589832 | tf_op jit(solution)/shard_map/ppermute | solution.py:257
  4.9 3.4 %copy-done = bf16[1024,4096]{1,0:T(8,128)(2,1)S(1)} copy-done((bf16[1024,4096]{1,0:T(8,128)(2,1)S(1)}, bf16[1024,4096]{1,0:T(8,128)(2,1)}, u32[]{:S(2)}) %copy-start) | copy-done | bytes 8388632
  8.2 0.7 %copy-done.4 = s32[1,256]{1,0:T(1,128)S(1)} copy-done((s32[1,256]{1,0:T(1,128)S(1)}, s32[1,256]{1,0:T(1,128)}, u32[]{:S(2)}) %copy-start.4) | copy-done | bytes 1048
  8.9 0.9 %shard_map.74 = (bf16[1024,4096]{1,0:T(8,128)(2,1)S(1)}, f32[256,256]{1,0:T(8,128)S(1)}) custom-call(s32[1,256]{1,0:T(1,128)S(1)} %copy-done.4, bf16[1024,4096]{1,0:T(8,128)(2,1)S(1)} %copy-done), custom_call_target="tpu_custom_call" | custom-call | bytes 16777216 | tf_op jit(solution)/shard_map/pallas_call | solution.py:93
  9.8 0.2 collective-permute-done.other_ref
  10.0 0.5 %shard_map.75.att_ref = bf16[64,1024]{1,0:T(8,128)(2,1)S(1)} custom-call(bf16[64,1536]{1,0:T(8,128)(2,1)S(1)} %copy-done.1, bf16[64,1536]{1,0:T(8,128)(2,1)S(1)} %collective-permute-done.other_ref, f32[256,256]{1,0:T(8,128)S(1)} %get-tuple-element.20.bias_ref), custom_call_target="tpu_custom_call" | custom-call | bytes 98304 | tf_op jit(solution)/shard_map/pallas_call | solution.py:158
  10.5 0.8 %shard_map.76 = bf16[64,2048]{1,0:T(8,128)(2,1)S(1)} custom-call(bf16[64,1024]{1,0:T(8,128)(2,1)S(1)} %shard_map.75.att_ref, bf16[1024,4096]{1,0:T(8,128)(2,1)S(1)} %get-tuple-element.22.w_ref), custom_call_target="tpu_custom_call" | custom-call | flops 268435456 | bytes 4194304 | tf_op jit(solution)/shard_map/pallas_call | solution.py:176
  11.3 1.9 %collective-permute-start.2 = (bf16[64,2048]{1,0:T(8,128)(2,1)S(1)}, bf16[64,2048]{1,0:T(8,128)(2,1)S(1)}, u32[]{:S(2)}, u32[]{:S(2)}) collective-permute-start(bf16[64,2048]{1,0:T(8,128)(2,1)S(1)} %shard_map.76), channel_id=1, source_target_pairs={{0,1},{1,0},{2,3},{3,2},{4,5},{5,4},{6,7},{7,6},{8,9},{9,8},{10,11... | collective-permute-start | bytes 786440 | tf_op jit(solution)/shard_map/ppermute | solution.py:257
  13.2 0.8 %shard_map.80 = bf16[64,2048]{1,0:T(8,128)(2,1)S(1)} custom-call(bf16[64,1024]{1,0:T(8,128)(2,1)S(1)} %shard_map.75.att_ref, bf16[1024,4096]{1,0:T(8,128)(2,1)S(1)} %get-tuple-element.22.w_ref), custom_call_target="tpu_custom_call" | custom-call | flops 268435456 | bytes 4194304 | tf_op jit(solution)/shard_map/pallas_call | solution.py:176
  14.0 0.3 collective-permute-start.4
  14.3 1.7 %collective-permute-start.1 = (bf16[64,1024]{1,0:T(8,128)(2,1)S(1)}, bf16[64,1024]{1,0:T(8,128)(2,1)S(1)}, u32[]{:S(2)}, u32[]{:S(2)}) collective-permute-start(bf16[64,1024]{1,0:T(8,128)(2,1)S(1)} %copy-done.3), channel_id=1, source_target_pairs={{0,4},{4,0},{1,5},{5,1},{2,6},{6,2},{3,7},{7,3},{8,12},{12,8},{9,1... | collective-permute-start | bytes 393224 | tf_op jit(solution)/shard_map/ppermute | solution.py:257
  16.1 3.2 %collective-permute-done.1.rest_1_ = bf16[64,1024]{1,0:T(8,128)(2,1)S(1)} collective-permute-done((bf16[64,1024]{1,0:T(8,128)(2,1)S(1)}, bf16[64,1024]{1,0:T(8,128)(2,1)S(1)}, u32[]{:S(2)}, u32[]{:S(2)}) %collective-permute-start.1) | collective-permute-done | bytes 131104 | tf_op jit(solution)/shard_map/ppermute | solution.py:257
  19.3 0.8 %shard_map.77.att_ref = bf16[192,1024]{1,0:T(8,128)(2,1)S(1)} custom-call(bf16[64,1536]{1,0:T(8,128)(2,1)S(1)} %copy-done.1, bf16[64,1536]{1,0:T(8,128)(2,1)S(1)} %collective-permute-done.other_ref, f32[256,256]{1,0:T(8,128)S(1)} %get-tuple-element.20.bias_ref, bf16[64,1024]{1,0:T(8,128)(2,1)S(1)} %copy-done.3, ...), custom_call_target="tpu_custom_call" | custom-call | bytes 98304 | tf_op jit(solution)/shard_map/pallas_call | solution.py:158
  20.1 0.0 copy-start.5
  20.1 0.5 %collective-permute-done.2.got_ref = bf16[64,2048]{1,0:T(8,128)(2,1)S(1)} collective-permute-done((bf16[64,2048]{1,0:T(8,128)(2,1)S(1)}, bf16[64,2048]{1,0:T(8,128)(2,1)S(1)}, u32[]{:S(2)}, u32[]{:S(2)}) %collective-permute-start.2) | collective-permute-done | bytes 262176 | tf_op jit(solution)/shard_map/ppermute | solution.py:257
  20.6 1.0 %shard_map.78 = (bf16[64,2048]{1,0:T(8,128)(2,1)S(1)}, bf16[64,2048]{1,0:T(8,128)(2,1)S(1)}, f32[64,2048]{1,0:T(8,128)S(1)}) custom-call(bf16[192,1024]{1,0:T(8,128)(2,1)S(1)} %shard_map.77.att_ref, bf16[1024,4096]{1,0:T(8,128)(2,1)S(1)} %get-tuple-element.22.w_ref, bf16[64,2048]{1,0:T(8,128)(2,1)S(1)} %collective-permute-done.2.got_ref), custom_call_target="tpu_custom_call" | custom-call | flops 805306368 | bytes 4194304 | tf_op jit(solution)/shard_map/pallas_call | solution.py:198
  21.7 0.0 copy-start.2
  21.7 2.9 %collective-permute-start.3 = (bf16[64,2048]{1,0:T(8,128)(2,1)S(1)}, bf16[64,2048]{1,0:T(8,128)(2,1)S(1)}, u32[]{:S(2)}, u32[]{:S(2)}) collective-permute-start(bf16[64,2048]{1,0:T(8,128)(2,1)S(1)} %get-tuple-element.25), channel_id=1, source_target_pairs={{0,2},{1,3},{2,0},{3,1},{4,6},{5,7},{6,4},{7,5},{8,10},{9,11},{10,... | collective-permute-start | bytes 786440 | tf_op jit(solution)/shard_map/ppermute | solution.py:257
  24.5 1.6 %collective-permute-start.5 = (bf16[64,2048]{1,0:T(8,128)(2,1)S(1)}, bf16[64,2048]{1,0:T(8,128)(2,1)S(1)}, u32[]{:S(2)}, u32[]{:S(2)}) collective-permute-start(bf16[64,2048]{1,0:T(8,128)(2,1)S(1)} %get-tuple-element.27), channel_id=1, source_target_pairs={{0,1},{1,0},{2,3},{3,2},{4,5},{5,4},{6,7},{7,6},{8,9},{9,8},{10,11... | collective-permute-start | bytes 786440 | tf_op jit(solution)/shard_map/ppermute | solution.py:257
  26.1 4.1 %collective-permute-done.4.got_ref = bf16[64,2048]{1,0:T(8,128)(2,1)S(1)} collective-permute-done((bf16[64,2048]{1,0:T(8,128)(2,1)S(1)}, bf16[64,2048]{1,0:T(8,128)(2,1)S(1)}, u32[]{:S(2)}, u32[]{:S(2)}) %collective-permute-start.4) | collective-permute-done | bytes 262176 | tf_op jit(solution)/shard_map/ppermute | solution.py:257
  30.3 1.0 %shard_map.81 = (bf16[64,2048]{1,0:T(8,128)(2,1)S(1)}, bf16[64,2048]{1,0:T(8,128)(2,1)S(1)}, f32[64,2048]{1,0:T(8,128)S(1)}) custom-call(bf16[192,1024]{1,0:T(8,128)(2,1)S(1)} %shard_map.77.att_ref, bf16[1024,4096]{1,0:T(8,128)(2,1)S(1)} %get-tuple-element.22.w_ref, bf16[64,2048]{1,0:T(8,128)(2,1)S(1)} %collective-permute-done.4.got_ref), custom_call_target="tpu_custom_call" | custom-call | flops 805306368 | bytes 4194304 | tf_op jit(solution)/shard_map/pallas_call | solution.py:198
  31.3 0.1 collective-permute-start.6
  31.4 2.2 %collective-permute-start.7 = (bf16[64,2048]{1,0:T(8,128)(2,1)S(1)}, bf16[64,2048]{1,0:T(8,128)(2,1)S(1)}, u32[]{:S(2)}, u32[]{:S(2)}) collective-permute-start(bf16[64,2048]{1,0:T(8,128)(2,1)S(1)} %get-tuple-element.29), channel_id=1, source_target_pairs={{0,1},{1,0},{2,3},{3,2},{4,5},{5,4},{6,7},{7,6},{8,9},{9,8},{10,11... | collective-permute-start | bytes 786440 | tf_op jit(solution)/shard_map/ppermute | solution.py:257
  33.6 1.3 %collective-permute-start.8 = (bf16[64,2048]{1,0:T(8,128)(2,1)S(1)}, bf16[64,2048]{1,0:T(8,128)(2,1)S(1)}, u32[]{:S(2)}, u32[]{:S(2)}) collective-permute-start(bf16[64,2048]{1,0:T(8,128)(2,1)S(1)} %get-tuple-element.32), channel_id=1, source_target_pairs={{0,8},{8,16},{16,24},{1,9},{9,17},{17,25},{2,10},{10,18},{18,26},{... | collective-permute-start | bytes 786440 | tf_op jit(solution)/shard_map/ppermute | solution.py:267
  35.0 0.7 %collective-permute-done.3.y_ref = bf16[64,2048]{1,0:T(8,128)(2,1)S(1)} collective-permute-done((bf16[64,2048]{1,0:T(8,128)(2,1)S(1)}, bf16[64,2048]{1,0:T(8,128)(2,1)S(1)}, u32[]{:S(2)}, u32[]{:S(2)}) %collective-permute-start.3) | collective-permute-done | bytes 262176 | tf_op jit(solution)/shard_map/ppermute | solution.py:257
  35.6 3.5 %collective-permute-start.9 = (bf16[64,2048]{1,0:T(8,128)(2,1)S(1)}, bf16[64,2048]{1,0:T(8,128)(2,1)S(1)}, u32[]{:S(2)}, u32[]{:S(2)}) collective-permute-start(bf16[64,2048]{1,0:T(8,128)(2,1)S(1)} %get-tuple-element.31), channel_id=1, source_target_pairs={{0,8},{8,16},{16,24},{1,9},{9,17},{17,25},{2,10},{10,18},{18,26},{... | collective-permute-start | bytes 786440 | tf_op jit(solution)/shard_map/ppermute | solution.py:267
  39.2 2.3 %collective-permute-done.5.m0_ref = bf16[64,2048]{1,0:T(8,128)(2,1)S(1)} collective-permute-done((bf16[64,2048]{1,0:T(8,128)(2,1)S(1)}, bf16[64,2048]{1,0:T(8,128)(2,1)S(1)}, u32[]{:S(2)}, u32[]{:S(2)}) %collective-permute-start.5) | collective-permute-done | bytes 262176 | tf_op jit(solution)/shard_map/ppermute | solution.py:257
  41.5 3.6 %collective-permute-done.6.y_ref = bf16[64,2048]{1,0:T(8,128)(2,1)S(1)} collective-permute-done((bf16[64,2048]{1,0:T(8,128)(2,1)S(1)}, bf16[64,2048]{1,0:T(8,128)(2,1)S(1)}, u32[]{:S(2)}, u32[]{:S(2)}) %collective-permute-start.6) | collective-permute-done | bytes 262176 | tf_op jit(solution)/shard_map/ppermute | solution.py:257
  45.1 2.0 %collective-permute-done.7.m1_ref = bf16[64,2048]{1,0:T(8,128)(2,1)S(1)} collective-permute-done((bf16[64,2048]{1,0:T(8,128)(2,1)S(1)}, bf16[64,2048]{1,0:T(8,128)(2,1)S(1)}, u32[]{:S(2)}, u32[]{:S(2)}) %collective-permute-start.7) | collective-permute-done | bytes 262176 | tf_op jit(solution)/shard_map/ppermute | solution.py:257
  47.1 0.1 shard_map.82.b_ref
  47.3 0.9 %shard_map.83 = bf16[64,4096]{1,0:T(8,128)(2,1)} custom-call(f32[64,4096]{1,0:T(8,128)S(1)} %shard_map.82.b_ref, bf16[64,4096]{1,0:T(8,128)(2,1)S(1)} %copy-done.2, bf16[64,2048]{1,0:T(8,128)(2,1)S(1)} %collective-permute-done.8.rest_0_, bf16[64,2048]{1,0:T(8,128)(2,1)S(1)} %collective-permute-done.9.rest_1_), custom_call_target="tpu_custom_call" | custom-call | bytes 2621440 | tf_op jit(solution)/shard_map/pallas_call | solution.py:244
  (12 shorter events, 0.1 us)
Async XLA Ops:
  1.8 8.1 %collective-permute-start = (bf16[64,1536]{1,0:T(8,128)(2,1)}, bf16[64,1536]{1,0:T(8,128)(2,1)S(1)}, u32[]{:S(2)}, u32[]{:S(2)}) collective-permute-start(bf16[64,1536]{1,0:T(8,128)(2,1)} %get-tuple-element.18.mine_ref), channel_id=1, source_target_pairs={{0,4},{4,0},{1,5},{5,1},{2,6},{6,2},{3,7},{7,3},{8,12},{12,8},{9,1... | collective-permute-start | bytes 589832 | tf_op jit(solution)/shard_map/ppermute | solution.py:257
  4.9 3.4 %copy-start = (bf16[1024,4096]{1,0:T(8,128)(2,1)S(1)}, bf16[1024,4096]{1,0:T(8,128)(2,1)}, u32[]{:S(2)}) copy-start(bf16[1024,4096]{1,0:T(8,128)(2,1)} %w_ref.1) | copy-start | bytes 25165828
  8.2 0.7 %copy-start.4 = (s32[1,256]{1,0:T(1,128)S(1)}, s32[1,256]{1,0:T(1,128)}, u32[]{:S(2)}) copy-start(s32[1,256]{1,0:T(1,128)} %get-tuple-element.19.seg_ref) | copy-start | bytes 3076
  8.9 1.1 %copy-start.1 = (bf16[64,1536]{1,0:T(8,128)(2,1)S(1)}, bf16[64,1536]{1,0:T(8,128)(2,1)}, u32[]{:S(2)}) copy-start(bf16[64,1536]{1,0:T(8,128)(2,1)} %get-tuple-element.18.mine_ref) | copy-start | bytes 589828
  10.5 3.9 %copy-start.3 = (bf16[64,1024]{1,0:T(8,128)(2,1)S(1)}, bf16[64,1024]{1,0:T(8,128)(2,1)}, u32[]{:S(2)}) copy-start(bf16[64,1024]{1,0:T(8,128)(2,1)} %get-tuple-element.23.rest_0_) | copy-start | bytes 393220
  11.3 9.3 %collective-permute-start.2 = (bf16[64,2048]{1,0:T(8,128)(2,1)S(1)}, bf16[64,2048]{1,0:T(8,128)(2,1)S(1)}, u32[]{:S(2)}, u32[]{:S(2)}) collective-permute-start(bf16[64,2048]{1,0:T(8,128)(2,1)S(1)} %shard_map.76), channel_id=1, source_target_pairs={{0,1},{1,0},{2,3},{3,2},{4,5},{5,4},{6,7},{7,6},{8,9},{9,8},{10,11... | collective-permute-start | bytes 786440 | tf_op jit(solution)/shard_map/ppermute | solution.py:257
  14.0 16.2 %collective-permute-start.4 = (bf16[64,2048]{1,0:T(8,128)(2,1)S(1)}, bf16[64,2048]{1,0:T(8,128)(2,1)S(1)}, u32[]{:S(2)}, u32[]{:S(2)}) collective-permute-start(bf16[64,2048]{1,0:T(8,128)(2,1)S(1)} %shard_map.80), channel_id=1, source_target_pairs={{0,1},{1,0},{2,3},{3,2},{4,5},{5,4},{6,7},{7,6},{8,9},{9,8},{10,11... | collective-permute-start | bytes 786440 | tf_op jit(solution)/shard_map/ppermute | solution.py:257
  14.3 5.0 %collective-permute-start.1 = (bf16[64,1024]{1,0:T(8,128)(2,1)S(1)}, bf16[64,1024]{1,0:T(8,128)(2,1)S(1)}, u32[]{:S(2)}, u32[]{:S(2)}) collective-permute-start(bf16[64,1024]{1,0:T(8,128)(2,1)S(1)} %copy-done.3), channel_id=1, source_target_pairs={{0,4},{4,0},{1,5},{5,1},{2,6},{6,2},{3,7},{7,3},{8,12},{12,8},{9,1... | collective-permute-start | bytes 393224 | tf_op jit(solution)/shard_map/ppermute | solution.py:257
  20.1 13.5 %copy-start.5 = (bf16[1,64,4096]{2,1,0:T(8,128)(2,1)S(1)}, bf16[1,64,4096]{2,1,0:T(8,128)(2,1)}, u32[]{:S(2)}) copy-start(bf16[1,64,4096]{2,1,0:T(8,128)(2,1)} %param.13) | copy-start | bytes 1572868
  21.7 25.6 %copy-start.2 = (bf16[64,4096]{1,0:T(8,128)(2,1)S(1)}, bf16[64,4096]{1,0:T(8,128)(2,1)}, u32[]{:S(2)}) copy-start(bf16[64,4096]{1,0:T(8,128)(2,1)} %e_ref.1) | copy-start | bytes 1572868
  21.7 14.0 %collective-permute-start.3 = (bf16[64,2048]{1,0:T(8,128)(2,1)S(1)}, bf16[64,2048]{1,0:T(8,128)(2,1)S(1)}, u32[]{:S(2)}, u32[]{:S(2)}) collective-permute-start(bf16[64,2048]{1,0:T(8,128)(2,1)S(1)} %get-tuple-element.25), channel_id=1, source_target_pairs={{0,2},{1,3},{2,0},{3,1},{4,6},{5,7},{6,4},{7,5},{8,10},{9,11},{10,... | collective-permute-start | bytes 786440 | tf_op jit(solution)/shard_map/ppermute | solution.py:257
  24.5 17.0 %collective-permute-start.5 = (bf16[64,2048]{1,0:T(8,128)(2,1)S(1)}, bf16[64,2048]{1,0:T(8,128)(2,1)S(1)}, u32[]{:S(2)}, u32[]{:S(2)}) collective-permute-start(bf16[64,2048]{1,0:T(8,128)(2,1)S(1)} %get-tuple-element.27), channel_id=1, source_target_pairs={{0,1},{1,0},{2,3},{3,2},{4,5},{5,4},{6,7},{7,6},{8,9},{9,8},{10,11... | collective-permute-start | bytes 786440 | tf_op jit(solution)/shard_map/ppermute | solution.py:257
  31.3 13.8 %collective-permute-start.6 = (bf16[64,2048]{1,0:T(8,128)(2,1)S(1)}, bf16[64,2048]{1,0:T(8,128)(2,1)S(1)}, u32[]{:S(2)}, u32[]{:S(2)}) collective-permute-start(bf16[64,2048]{1,0:T(8,128)(2,1)S(1)} %get-tuple-element.28), channel_id=1, source_target_pairs={{0,2},{1,3},{2,0},{3,1},{4,6},{5,7},{6,4},{7,5},{8,10},{9,11},{10,... | collective-permute-start | bytes 786440 | tf_op jit(solution)/shard_map/ppermute | solution.py:257
  31.4 15.7 %collective-permute-start.7 = (bf16[64,2048]{1,0:T(8,128)(2,1)S(1)}, bf16[64,2048]{1,0:T(8,128)(2,1)S(1)}, u32[]{:S(2)}, u32[]{:S(2)}) collective-permute-start(bf16[64,2048]{1,0:T(8,128)(2,1)S(1)} %get-tuple-element.29), channel_id=1, source_target_pairs={{0,1},{1,0},{2,3},{3,2},{4,5},{5,4},{6,7},{7,6},{8,9},{9,8},{10,11... | collective-permute-start | bytes 786440 | tf_op jit(solution)/shard_map/ppermute | solution.py:257
  33.6 13.6 %collective-permute-start.8 = (bf16[64,2048]{1,0:T(8,128)(2,1)S(1)}, bf16[64,2048]{1,0:T(8,128)(2,1)S(1)}, u32[]{:S(2)}, u32[]{:S(2)}) collective-permute-start(bf16[64,2048]{1,0:T(8,128)(2,1)S(1)} %get-tuple-element.32), channel_id=1, source_target_pairs={{0,8},{8,16},{16,24},{1,9},{9,17},{17,25},{2,10},{10,18},{18,26},{... | collective-permute-start | bytes 786440 | tf_op jit(solution)/shard_map/ppermute | solution.py:267
  35.6 11.6 %collective-permute-start.9 = (bf16[64,2048]{1,0:T(8,128)(2,1)S(1)}, bf16[64,2048]{1,0:T(8,128)(2,1)S(1)}, u32[]{:S(2)}, u32[]{:S(2)}) collective-permute-start(bf16[64,2048]{1,0:T(8,128)(2,1)S(1)} %get-tuple-element.31), channel_id=1, source_target_pairs={{0,8},{8,16},{16,24},{1,9},{9,17},{17,25},{2,10},{10,18},{18,26},{... | collective-permute-start | bytes 786440 | tf_op jit(solution)/shard_map/ppermute | solution.py:267

commit v3 on v2

--- a/solution.py
+++ b/solution.py
@@ -29,52 +29,10 @@
     return i ^ 3, i ^ 1, i ^ 2, i
 
 
-def pack(q, k, v, seg):
-    rows, width = q.shape[0] // 2, q.shape[1]
-    kw = k.shape[1]
-
-    def body(q_ref, k_ref, v_ref, s_ref, x_ref, y_ref, seg_ref, sems):
-        low = lax.axis_index("tp") & 1
-        pieces = [(q_ref.at[pl.ds(pl.multiple_of((1 - low) * rows, rows), rows)], x_ref.at[:, 0:width])]
-        at = width
-        for ref in (k_ref, v_ref):
-            for part in range(2):
-                pieces.append((ref.at[part * rows:(part + 1) * rows], x_ref.at[:, at:at + kw]))
-                at += kw
-        pieces.append((q_ref.at[pl.ds(pl.multiple_of(low * rows, rows), rows)], y_ref))
-        pieces.append((s_ref, seg_ref))
-        copies = [pltpu.make_async_copy(a, b, sems.at[n]) for n, (a, b) in enumerate(pieces)]
-        for copy in copies:
-            copy.start()
-        for copy in copies:
-            copy.wait()
-
-    return kernel_call(
-        body,
-        (
-            jax.ShapeDtypeStruct((rows, width + 4 * kw), q.dtype),
-            jax.ShapeDtypeStruct((rows, width), q.dtype),
-            jax.ShapeDtypeStruct(seg.shape, seg.dtype),
-        ),
-        [HBM] * 4,
-        [pltpu.SemaphoreType.DMA((7,))],
-        moved=4 * q.size,
-        mib=58,
-    )(q, k, v, seg)
-
-
-def prepare(seg, weight, rows):
+def mask(seg, rows):
     half = 2 * rows
-    parts = 8
-
-    def body(seg_ref, w_ref, wo_ref, bias_ref, col_ref, sems):
-        depth = w_ref.shape[0] // parts
-        copies = []
-        for p in range(parts):
-            at = pl.ds(p * depth, depth)
-            copies.append(pltpu.make_async_copy(w_ref.at[at], wo_ref.at[at], sems.at[p]))
-        for copy in copies:
-            copy.start()
+
+    def body(seg_ref, bias_ref, col_ref):
         c = lax.axis_index("ctx")
         seg_all = seg_ref[...].astype(F32)
         col_ref[...] = jnp.transpose(jnp.broadcast_to(seg_all, (128, 2 * half)))
@@ -87,27 +45,14 @@
             row_place = lax.broadcasted_iota(jnp.int32, (rows, 2 * half), 0) + at
             allowed = (row_place >= key_place) & (col_ref[pl.ds(at, rows), 0:1] == seg_keys)
             bias_ref[b * rows:(b + 1) * rows, :] = jnp.where(allowed, 0.0, NEG)
-        for copy in copies:
-            copy.wait()
 
     return kernel_call(
         body,
-        (jax.ShapeDtypeStruct(weight.shape, weight.dtype), jax.ShapeDtypeStruct((4 * rows, 2 * half), F32)),
-        [VMEM, HBM],
-        [pltpu.VMEM((2 * half, 128), F32), pltpu.SemaphoreType.DMA((parts,))],
-        moved=weight.size * 4,
-    )(seg, weight)
-
-
-def keys_values(mine, other, width):
-    kw = (mine.shape[1] - width) // 4
-
-    def piece(ref, n):
-        return ref[:, width + n * kw:width + (n + 1) * kw]
-
-    k = jnp.concatenate([piece(r, n) for r in (mine, other) for n in (0, 1)], axis=0)
-    v = jnp.concatenate([piece(r, n) for r in (mine, other) for n in (2, 3)], axis=0)
-    return k, v
+        jax.ShapeDtypeStruct((4 * rows, 2 * half), F32),
+        [VMEM],
+        [pltpu.VMEM((2 * half, 128), F32)],
+        moved=1024,
+    )(seg)
 
 
 def attend(q, k, v, bias):
@@ -124,33 +69,33 @@
     return jnp.concatenate([o[h * rows:(h + 1) * rows] for h in range(heads)], axis=1)
 
 
-def product(att, w_ref, at, width, store, tile=512):
-    for t in range(0, width, tile):
-        store(t, tile, jnp.dot(att, w_ref[:, at + t:at + t + tile], preferred_element_type=F32))
+def product(att, w_ref, store, tile=512):
+    for t in range(0, w_ref.shape[1], tile):
+        store(t, tile, jnp.dot(att, w_ref[:, t:t + tile], preferred_element_type=F32))
 
 
 def choose(c, i, mine, other):
     return jnp.where(c == i >> 1, mine, other)
 
 
-def attend_blocks(mine, other, bias, halves=()):
-    rows = mine.shape[0]
-    width = mine.shape[1] - 4 * HEAD_DIM
+def attend_blocks(kv, bias, qx, rx, halves=()):
+    rows, width = qx.shape
     n = 3 if halves else 1
 
-    def body(mine_ref, other_ref, bias_ref, *rest):
+    def body(kl, vl, kr, vr, bias_ref, qx_ref, rx_ref, *rest):
         c, i = lax.axis_index("ctx"), lax.axis_index("tp")
         att_ref = rest[-1]
-        k, v = keys_values(mine_ref, other_ref, width)
+        k = jnp.concatenate((kl[...], kr[...]), axis=0)
+        v = jnp.concatenate((vl[...], vr[...]), axis=0)
         if halves:
             qy_ref, ry_ref = rest[:2]
             blocks = (
-                choose(c, i, mine_ref[:, :width], other_ref[:, :width]),
+                choose(c, i, qx_ref[...], rx_ref[...]),
                 choose(c, i, ry_ref[...], qy_ref[...]),
                 choose(c, i, qy_ref[...], ry_ref[...]),
             )
         else:
-            blocks = (choose(c, i, other_ref[:, :width], mine_ref[:, :width]),)
+            blocks = (choose(c, i, rx_ref[...], qx_ref[...]),)
         first = 1 if halves else 0
         for b, q in enumerate(blocks):
             att_ref[b * rows:(b + 1) * rows, :] = attend(q, k, v, bias_ref[(first + b) * rows:(first + b + 1) * rows])
@@ -158,20 +103,20 @@
     return kernel_call(
         body,
         jax.ShapeDtypeStruct((n * rows, width), BF16),
-        [VMEM] * (3 + len(halves)),
-        flops=0,
-        moved=mine.size,
-    )(mine, other, bias, *halves)
-
-
-def first_part(att, weight, at, cols):
+        [VMEM] * (7 + len(halves)),
+        moved=qx.size * 4,
+    )(*kv, bias, qx, rx, *halves)
+
+
+def first_part(att, weight):
     rows, width = att.shape
+    cols = weight.shape[1]
 
     def body(att_ref, w_ref, a_ref):
         def store(t, tile, part):
             a_ref[:, t:t + tile] = part.astype(BF16)
 
-        product(att_ref[...], w_ref, at, cols, store)
+        product(att_ref[...], w_ref, store)
 
     return kernel_call(
         body,
@@ -182,7 +127,7 @@
     )(att, weight)
 
 
-def other_parts(att, weight, got, at):
+def other_parts(att, weight, got):
     rows, width = att.shape[0] // 3, att.shape[1]
     cols = got.shape[1]
 
@@ -192,7 +137,7 @@
             f_ref[:, t:t + tile] = (part[rows:2 * rows] + got_ref[:, t:t + tile].astype(F32)).astype(BF16)
             o_ref[:, t:t + tile] = part[2 * rows:]
 
-        product(att_ref[...], w_ref, at, cols, store)
+        product(att_ref[...], w_ref, store)
 
     part = jax.ShapeDtypeStruct((rows, cols), BF16)
     return kernel_call(
@@ -276,20 +221,26 @@
     q = queries[0]
     rows = q.shape[0] // 2
     cols = out_weight.shape[1] // 2
-    mine, qy, seg = pack(q, keys[0], values[0], seg_ids)
-    other = swap(mine, "ctx", 1)
-    weight, bias = prepare(seg, out_weight, rows)
-    att = attend_blocks(mine, other, bias)
-    a0 = first_part(att, weight, 0, cols)
+    k, v = keys[0], values[0]
+    kr, vr = swap(k, "ctx", 1), swap(v, "ctx", 1)
+    low = lax.axis_index("tp") & 1
+    qx = lax.dynamic_slice_in_dim(q, (1 - low) * rows, rows)
+    qy = lax.dynamic_slice_in_dim(q, low * rows, rows)
+    rx = swap(qx, "ctx", 1)
+    ry = swap(qy, "ctx", 1)
+    bias, left = lax.optimization_barrier((mask(seg_ids, rows), out_weight[:, :cols]))
+    kv = (k, v, kr, vr)
+    att = attend_blocks(kv, bias, qx, rx)
+    a0 = first_part(att, left)
     got0 = swap(a0, "tp", 1)
-    a1 = first_part(att, weight, cols, cols)
+    right = after(out_weight, a0)[:, cols:]
+    rest = attend_blocks(kv, bias, qx, rx, (qy, ry))
+    a1 = first_part(att, right)
     got1 = swap(a1, "tp", 1)
-    ry = swap(after(qy, a0), "ctx", 1)
-    rest = attend_blocks(mine, other, bias, (qy, ry))
-    m0, f0, own0 = other_parts(rest, weight, got0, 0)
+    m0, f0, own0 = other_parts(rest, left, got0)
     gotm0 = swap(m0, "tp", 1)
     y0 = swap(f0, "tp", 2)
-    m1, f1, own1 = other_parts(rest, weight, got1, cols)
+    m1, f1, own1 = other_parts(rest, right, got1)
     gotm1 = swap(m1, "tp", 1)
     y1 = swap(f1, "tp", 2)
     prev = after(hidden_prev, f1)[0]

time: 48.4 us -> 47.6 us (0.983)
  Pallas kernels: 8.68 us -> 6.21 us
  local copies, waits for them, and re-layouts: 4.12 us -> 4.96 us
  starting transfers between devices: 18.5 us -> 19.1 us
    unnamed x12, local copies, waits for them, and re-layouts: 4.08 us -> 0.71 us
    slice x0 -> x2, local copies, waits for them, and re-layouts: none -> 3.23 us  [the longest x1 2.66 us: on_pair(): out_weight[:, :cols]]
    ppermute x8 -> x10, starting transfers between devices: 13.7 us -> 16.5 us  [swap(): return lax.ppermute(x, axis, [(i, i ^ by) for i in range(peers)])]
    pallas_call x2 -> x1, Pallas kernels: 2.67 us -> 0.21 us  [mask(): kernel_call(body, jax.ShapeDtypeStruct((4 * rows, 2 * half), F32), [VMEM]...]
    ppermute x2, starting transfers between devices: 4.79 us -> 2.6 us  [passed_along(): return lax.ppermute(shard, axis, pairs)]
    dynamic_slice x0 -> x1, local copies, waits for them, and re-layouts: none -> 0.98 us  [on_pair(): qy = lax.dynamic_slice_in_dim(q, low * rows, rows)]
    ppermute x8 -> x10, waiting for transfers between devices: 16.7 us -> 16.9 us  [swap(): return lax.ppermute(x, axis, [(i, i ^ by) for i in range(peers)])]
  transfers between devices with their start and end apart: 10 -> 12, of which waited for: 8 -> 5; matrix products, arithmetic and copies ran while one was open for 0% -> 7% of each run, Pallas kernels for 10% -> 8%
where the time goes in v3:
time: 47.6 us; the launch traced here: 47.4 us
  starting transfers between devices  19.1 us (40%)
  waiting for transfers between devices  16.9 us (36%)
  Pallas kernels  6.21 us (13%)
  local copies, waits for them, and re-layouts  4.96 us (10%)
    ppermute x10, waiting for transfers between devices, swap(): return lax.ppermute(x, axis, [(i, i ^ by) for i in range(peers)])  16.9 us
    ppermute x10, starting transfers between devices, swap(): return lax.ppermute(x, axis, [(i, i ^ by) for i in range(peers)])  16.5 us
    slice x1, local copies, waits for them, and re-layouts, on_pair(): out_weight[:, :cols]  2.66 us
    ppermute x2, starting transfers between devices, passed_along(): return lax.ppermute(shard, axis, pairs)  2.6 us
    pallas_call x2, Pallas kernels, other_parts(): kernel_call(body, (part, part, jax.ShapeDtypeStruct((rows, cols), F32)),...  2.02 us
    pallas_call x2, Pallas kernels, first_part(): kernel_call(body, jax.ShapeDtypeStruct((rows, cols), BF16), [VMEM] * 2, f...  1.68 us
    pallas_call x2, Pallas kernels, attend_blocks(): kernel_call(body, jax.ShapeDtypeStruct((n * rows, width), BF16), [VMEM] *...  1.27 us
    dynamic_slice x1, local copies, waits for them, and re-layouts, on_pair(): qy = lax.dynamic_slice_in_dim(q, low * rows, rows)  0.98 us
  transfers between devices with their start and end apart: 12, of which 5 were waited for; matrix products, arithmetic and copies ran while one was open for 7% of the time, Pallas kernels for 8%

profile of v3, /device:TPU:0, one launch (start us, length us, event | category | flops | bytes accessed | tf_op | source)
XLA Modules:
  0.0 47.4 jit_solution(18124012380767833593)
XLA Ops:
  0.0 1.0 %dynamic-slice_bitcast_fusion = (bf16[64,1024]{1,0:T(8,128)(2,1)S(1)}, bf16[64,1024]{1,0:T(8,128)(2,1)S(1)}) fusion(bf16[1,128,1024]{2,1,0:T(8,128)(2,1)} %param.7, s32[]{:T(128)S(6)} %select_n.7, s32[]{:T(128)S(6)} %select_n.6), kind=kLoop, calls=%fused_computation | loop fusion | bytes 524296 | tf_op jit(solution)/shard_map/dynamic_slice | solution.py:228
  1.0 3.0 %collective-permute-start.2 = (bf16[64,1024]{1,0:T(8,128)(2,1)S(1)}, bf16[64,1024]{1,0:T(8,128)(2,1)S(1)}, u32[]{:S(2)}, u32[]{:S(2)}) collective-permute-start(bf16[64,1024]{1,0:T(8,128)(2,1)S(1)} %get-tuple-element.28.qx_ref), channel_id=1, source_target_pairs={{0,4},{4,0},{1,5},{5,1},{2,6},{6,2},{3,7},{7,3},{8,12},{12,8},{9,1... | collective-permute-start | bytes 393224 | tf_op jit(solution)/shard_map/ppermute | solution.py:202
  4.0 0.1 collective-permute-start
  4.1 1.9 %collective-permute-start.1 = (bf16[128,128]{1,0:T(8,128)(2,1)}, bf16[128,128]{1,0:T(8,128)(2,1)S(1)}, u32[]{:S(2)}, u32[]{:S(2)}) collective-permute-start(bf16[128,128]{1,0:T(8,128)(2,1)} %bitcast.11), channel_id=1, source_target_pairs={{0,4},{4,0},{1,5},{5,1},{2,6},{6,2},{3,7},{7,3},{8,12},{12,8},{9,1... | collective-permute-start | bytes 98312 | tf_op jit(solution)/shard_map/ppermute | solution.py:202
  6.0 0.7 %copy-done.3 = s32[1,256]{1,0:T(1,128)S(1)} copy-done((s32[1,256]{1,0:T(1,128)S(1)}, s32[1,256]{1,0:T(1,128)}, u32[]{:S(2)}) %copy-start.3) | copy-done | bytes 1048
  6.7 0.2 shard_map.73.bias_ref
  6.9 0.0 copy-start.1
  7.0 0.0 copy-start.2
  7.0 2.7 %slice.12.w_ref = bf16[1024,2048]{1,0:T(8,128)(2,1)S(1)} slice(bf16[1024,4096]{1,0:T(8,128)(2,1)} %param.11), slice={[0:1024], [0:2048]} | slice | bytes 8388608 | tf_op jit(solution)/shard_map/slice | solution.py:231
  9.7 0.5 %shard_map.75.att_ref = bf16[64,1024]{1,0:T(8,128)(2,1)S(1)} custom-call(bf16[128,128]{1,0:T(8,128)(2,1)S(1)} %bitcast.9, bf16[128,128]{1,0:T(8,128)(2,1)S(1)} %bitcast.12, bf16[128,128]{1,0:T(8,128)(2,1)S(1)} %collective-permute-done.kr, bf16[128,128]{1,0:T(8,128)(2,1)S(1)} %collective-permute-done.1.vr, f32[256,256]{1,0:T(8,128)S(1)} %shard_map.73.bias_ref, ...), custom_call_target="tpu_custom_call" | custom-call | bytes 262144 | tf_op jit(solution)/shard_map/pallas_call | solution.py:103
  10.2 0.8 %shard_map.76 = bf16[64,2048]{1,0:T(8,128)(2,1)S(1)} custom-call(bf16[64,1024]{1,0:T(8,128)(2,1)S(1)} %shard_map.75.att_ref, bf16[1024,2048]{1,0:T(8,128)(2,1)S(1)} %slice.12.w_ref), custom_call_target="tpu_custom_call" | custom-call | flops 268435456 | bytes 2097152 | tf_op jit(solution)/shard_map/pallas_call | solution.py:121
  11.0 1.6 %collective-permute-start.4 = (bf16[64,2048]{1,0:T(8,128)(2,1)S(1)}, bf16[64,2048]{1,0:T(8,128)(2,1)S(1)}, u32[]{:S(2)}, u32[]{:S(2)}) collective-permute-start(bf16[64,2048]{1,0:T(8,128)(2,1)S(1)} %shard_map.76), channel_id=1, source_target_pairs={{0,1},{1,0},{2,3},{3,2},{4,5},{5,4},{6,7},{7,6},{8,9},{9,8},{10,11... | collective-permute-start | bytes 786440 | tf_op jit(solution)/shard_map/ppermute | solution.py:202
  12.7 0.6 %slice.13.w_ref = bf16[1024,2048]{1,0:T(8,128)(2,1)S(1)} slice(bf16[1024,4096]{1,0:T(8,128)(2,1)S(1)} %copy-done.4), slice={[0:1024], [2048:4096]} | slice | bytes 8388608 | tf_op jit(solution)/shard_map/slice | solution.py:236
  13.3 0.8 %shard_map.79 = bf16[64,2048]{1,0:T(8,128)(2,1)S(1)} custom-call(bf16[64,1024]{1,0:T(8,128)(2,1)S(1)} %shard_map.75.att_ref, bf16[1024,2048]{1,0:T(8,128)(2,1)S(1)} %slice.13.w_ref), custom_call_target="tpu_custom_call" | custom-call | flops 268435456 | bytes 2097152 | tf_op jit(solution)/shard_map/pallas_call | solution.py:121
  14.1 0.6 %collective-permute-start.6 = (bf16[64,2048]{1,0:T(8,128)(2,1)S(1)}, bf16[64,2048]{1,0:T(8,128)(2,1)S(1)}, u32[]{:S(2)}, u32[]{:S(2)}) collective-permute-start(bf16[64,2048]{1,0:T(8,128)(2,1)S(1)} %shard_map.79), channel_id=1, source_target_pairs={{0,1},{1,0},{2,3},{3,2},{4,5},{5,4},{6,7},{7,6},{8,9},{9,8},{10,11... | collective-permute-start | bytes 786440 | tf_op jit(solution)/shard_map/ppermute | solution.py:202
  14.7 0.9 %collective-permute-start.3 = (bf16[64,1024]{1,0:T(8,128)(2,1)S(1)}, bf16[64,1024]{1,0:T(8,128)(2,1)S(1)}, u32[]{:S(2)}, u32[]{:S(2)}) collective-permute-start(bf16[64,1024]{1,0:T(8,128)(2,1)S(1)} %get-tuple-element.27.rest_0_), channel_id=1, source_target_pairs={{0,4},{4,0},{1,5},{5,1},{2,6},{6,2},{3,7},{7,3},{8,12},{12,8},{9,1... | collective-permute-start | bytes 393224 | tf_op jit(solution)/shard_map/ppermute | solution.py:202
  15.6 4.1 %collective-permute-done.3.rest_1_ = bf16[64,1024]{1,0:T(8,128)(2,1)S(1)} collective-permute-done((bf16[64,1024]{1,0:T(8,128)(2,1)S(1)}, bf16[64,1024]{1,0:T(8,128)(2,1)S(1)}, u32[]{:S(2)}, u32[]{:S(2)}) %collective-permute-start.3) | collective-permute-done | bytes 131104 | tf_op jit(solution)/shard_map/ppermute | solution.py:202
  19.7 0.8 %shard_map.74.att_ref = bf16[192,1024]{1,0:T(8,128)(2,1)S(1)} custom-call(bf16[128,128]{1,0:T(8,128)(2,1)S(1)} %bitcast.10, bf16[128,128]{1,0:T(8,128)(2,1)S(1)} %bitcast.13, bf16[128,128]{1,0:T(8,128)(2,1)S(1)} %collective-permute-done.kr, bf16[128,128]{1,0:T(8,128)(2,1)S(1)} %collective-permute-done.1.vr, f32[256,256]{1,0:T(8,128)S(1)} %shard_map.73.bias_ref, ...), custom_call_target="tpu_custom_call" | custom-call | bytes 262144 | tf_op jit(solution)/shard_map/pallas_call | solution.py:103
  20.5 1.0 %shard_map.77 = (bf16[64,2048]{1,0:T(8,128)(2,1)S(1)}, bf16[64,2048]{1,0:T(8,128)(2,1)S(1)}, f32[64,2048]{1,0:T(8,128)S(1)}) custom-call(bf16[192,1024]{1,0:T(8,128)(2,1)S(1)} %shard_map.74.att_ref, bf16[1024,2048]{1,0:T(8,128)(2,1)S(1)} %slice.12.w_ref, bf16[64,2048]{1,0:T(8,128)(2,1)S(1)} %collective-permute-done.4.got_ref), custom_call_target="tpu_custom_call" | custom-call | flops 805306368 | bytes 2097152 | tf_op jit(solution)/shard_map/pallas_call | solution.py:143
  21.5 2.7 %collective-permute-start.5 = (bf16[64,2048]{1,0:T(8,128)(2,1)S(1)}, bf16[64,2048]{1,0:T(8,128)(2,1)S(1)}, u32[]{:S(2)}, u32[]{:S(2)}) collective-permute-start(bf16[64,2048]{1,0:T(8,128)(2,1)S(1)} %get-tuple-element.18), channel_id=1, source_target_pairs={{0,2},{1,3},{2,0},{3,1},{4,6},{5,7},{6,4},{7,5},{8,10},{9,11},{10,... | collective-permute-start | bytes 786440 | tf_op jit(solution)/shard_map/ppermute | solution.py:202
  24.1 1.5 %collective-permute-start.7 = (bf16[64,2048]{1,0:T(8,128)(2,1)S(1)}, bf16[64,2048]{1,0:T(8,128)(2,1)S(1)}, u32[]{:S(2)}, u32[]{:S(2)}) collective-permute-start(bf16[64,2048]{1,0:T(8,128)(2,1)S(1)} %get-tuple-element.21), channel_id=1, source_target_pairs={{0,1},{1,0},{2,3},{3,2},{4,5},{5,4},{6,7},{7,6},{8,9},{9,8},{10,11... | collective-permute-start | bytes 786440 | tf_op jit(solution)/shard_map/ppermute | solution.py:202
  25.6 1.6 %collective-permute-done.6.got_ref = bf16[64,2048]{1,0:T(8,128)(2,1)S(1)} collective-permute-done((bf16[64,2048]{1,0:T(8,128)(2,1)S(1)}, bf16[64,2048]{1,0:T(8,128)(2,1)S(1)}, u32[]{:S(2)}, u32[]{:S(2)}) %collective-permute-start.6) | collective-permute-done | bytes 262176 | tf_op jit(solution)/shard_map/ppermute | solution.py:202
  27.2 1.0 %shard_map.80 = (bf16[64,2048]{1,0:T(8,128)(2,1)S(1)}, bf16[64,2048]{1,0:T(8,128)(2,1)S(1)}, f32[64,2048]{1,0:T(8,128)S(1)}) custom-call(bf16[192,1024]{1,0:T(8,128)(2,1)S(1)} %shard_map.74.att_ref, bf16[1024,2048]{1,0:T(8,128)(2,1)S(1)} %slice.13.w_ref, bf16[64,2048]{1,0:T(8,128)(2,1)S(1)} %collective-permute-done.6.got_ref), custom_call_target="tpu_custom_call" | custom-call | flops 805306368 | bytes 2097152 | tf_op jit(solution)/shard_map/pallas_call | solution.py:143
  28.3 1.7 %collective-permute-start.8 = (bf16[64,2048]{1,0:T(8,128)(2,1)S(1)}, bf16[64,2048]{1,0:T(8,128)(2,1)S(1)}, u32[]{:S(2)}, u32[]{:S(2)}) collective-permute-start(bf16[64,2048]{1,0:T(8,128)(2,1)S(1)} %get-tuple-element.22), channel_id=1, source_target_pairs={{0,2},{1,3},{2,0},{3,1},{4,6},{5,7},{6,4},{7,5},{8,10},{9,11},{10,... | collective-permute-start | bytes 786440 | tf_op jit(solution)/shard_map/ppermute | solution.py:202
  30.0 2.5 %collective-permute-start.9 = (bf16[64,2048]{1,0:T(8,128)(2,1)S(1)}, bf16[64,2048]{1,0:T(8,128)(2,1)S(1)}, u32[]{:S(2)}, u32[]{:S(2)}) collective-permute-start(bf16[64,2048]{1,0:T(8,128)(2,1)S(1)} %get-tuple-element.23), channel_id=1, source_target_pairs={{0,1},{1,0},{2,3},{3,2},{4,5},{5,4},{6,7},{7,6},{8,9},{9,8},{10,11... | collective-permute-start | bytes 786440 | tf_op jit(solution)/shard_map/ppermute | solution.py:202
  32.5 1.3 %collective-permute-start.11 = (bf16[64,2048]{1,0:T(8,128)(2,1)S(1)}, bf16[64,2048]{1,0:T(8,128)(2,1)S(1)}, u32[]{:S(2)}, u32[]{:S(2)}) collective-permute-start(bf16[64,2048]{1,0:T(8,128)(2,1)S(1)} %get-tuple-element.25), channel_id=1, source_target_pairs={{0,8},{8,16},{16,24},{1,9},{9,17},{17,25},{2,10},{10,18},{18,26},{... | collective-permute-start | bytes 786440 | tf_op jit(solution)/shard_map/ppermute | solution.py:212
  33.8 3.6 %collective-permute-done.5.y_ref = bf16[64,2048]{1,0:T(8,128)(2,1)S(1)} collective-permute-done((bf16[64,2048]{1,0:T(8,128)(2,1)S(1)}, bf16[64,2048]{1,0:T(8,128)(2,1)S(1)}, u32[]{:S(2)}, u32[]{:S(2)}) %collective-permute-start.5) | collective-permute-done | bytes 262176 | tf_op jit(solution)/shard_map/ppermute | solution.py:202
  37.5 1.3 %collective-permute-start.10 = (bf16[64,2048]{1,0:T(8,128)(2,1)S(1)}, bf16[64,2048]{1,0:T(8,128)(2,1)S(1)}, u32[]{:S(2)}, u32[]{:S(2)}) collective-permute-start(bf16[64,2048]{1,0:T(8,128)(2,1)S(1)} %get-tuple-element.26), channel_id=1, source_target_pairs={{0,8},{8,16},{16,24},{1,9},{9,17},{17,25},{2,10},{10,18},{18,26},{... | collective-permute-start | bytes 786440 | tf_op jit(solution)/shard_map/ppermute | solution.py:212
  38.8 0.2 collective-permute-done.7.m0_ref
  39.0 7.4 %collective-permute-done.9.m1_ref = bf16[64,2048]{1,0:T(8,128)(2,1)S(1)} collective-permute-done((bf16[64,2048]{1,0:T(8,128)(2,1)S(1)}, bf16[64,2048]{1,0:T(8,128)(2,1)S(1)}, u32[]{:S(2)}, u32[]{:S(2)}) %collective-permute-start.9) | collective-permute-done | bytes 262176 | tf_op jit(solution)/shard_map/ppermute | solution.py:202
  46.4 0.1 shard_map.81.b_ref
  46.5 0.9 %shard_map.82 = bf16[64,4096]{1,0:T(8,128)(2,1)} custom-call(f32[64,4096]{1,0:T(8,128)S(1)} %shard_map.81.b_ref, bf16[64,4096]{1,0:T(8,128)(2,1)S(1)} %copy-done, bf16[64,2048]{1,0:T(8,128)(2,1)S(1)} %collective-permute-done.10.rest_0_, bf16[64,2048]{1,0:T(8,128)(2,1)S(1)} %collective-permute-done.11.rest_1_), custom_call_target="tpu_custom_call" | custom-call | bytes 2621440 | tf_op jit(solution)/shard_map/pallas_call | solution.py:189
  (18 shorter events, 0.1 us)
Async XLA Ops:
  1.0 8.7 %collective-permute-start.2 = (bf16[64,1024]{1,0:T(8,128)(2,1)S(1)}, bf16[64,1024]{1,0:T(8,128)(2,1)S(1)}, u32[]{:S(2)}, u32[]{:S(2)}) collective-permute-start(bf16[64,1024]{1,0:T(8,128)(2,1)S(1)} %get-tuple-element.28.qx_ref), channel_id=1, source_target_pairs={{0,4},{4,0},{1,5},{5,1},{2,6},{6,2},{3,7},{7,3},{8,12},{12,8},{9,1... | collective-permute-start | bytes 393224 | tf_op jit(solution)/shard_map/ppermute | solution.py:202
  4.0 5.6 %collective-permute-start = (bf16[128,128]{1,0:T(8,128)(2,1)}, bf16[128,128]{1,0:T(8,128)(2,1)S(1)}, u32[]{:S(2)}, u32[]{:S(2)}) collective-permute-start(bf16[128,128]{1,0:T(8,128)(2,1)} %bitcast.8), channel_id=1, source_target_pairs={{0,4},{4,0},{1,5},{5,1},{2,6},{6,2},{3,7},{7,3},{8,12},{12,8},{9,1... | collective-permute-start | bytes 98312 | tf_op jit(solution)/shard_map/ppermute | solution.py:202
  4.1 5.6 %collective-permute-start.1 = (bf16[128,128]{1,0:T(8,128)(2,1)}, bf16[128,128]{1,0:T(8,128)(2,1)S(1)}, u32[]{:S(2)}, u32[]{:S(2)}) collective-permute-start(bf16[128,128]{1,0:T(8,128)(2,1)} %bitcast.11), channel_id=1, source_target_pairs={{0,4},{4,0},{1,5},{5,1},{2,6},{6,2},{3,7},{7,3},{8,12},{12,8},{9,1... | collective-permute-start | bytes 98312 | tf_op jit(solution)/shard_map/ppermute | solution.py:202
  6.0 0.7 %copy-start.3 = (s32[1,256]{1,0:T(1,128)S(1)}, s32[1,256]{1,0:T(1,128)}, u32[]{:S(2)}) copy-start(s32[1,256]{1,0:T(1,128)} %seg_ref.1) | copy-start | bytes 3076
  6.9 2.7 %copy-start.1 = (bf16[1,128,128]{2,1,0:T(8,128)(2,1)S(1)}, bf16[1,128,128]{2,1,0:T(8,128)(2,1)}, u32[]{:S(2)}) copy-start(bf16[1,128,128]{2,1,0:T(8,128)(2,1)} %param.8) | copy-start | bytes 98308
  7.0 2.7 %copy-start.2 = (bf16[1,128,128]{2,1,0:T(8,128)(2,1)S(1)}, bf16[1,128,128]{2,1,0:T(8,128)(2,1)}, u32[]{:S(2)}) copy-start(bf16[1,128,128]{2,1,0:T(8,128)(2,1)} %param.9) | copy-start | bytes 98308
  7.0 5.7 %copy-start.4 = (bf16[1024,4096]{1,0:T(8,128)(2,1)S(1)}, bf16[1024,4096]{1,0:T(8,128)(2,1)}, u32[]{:S(2)}) copy-start(bf16[1024,4096]{1,0:T(8,128)(2,1)} %param.11) | copy-start | bytes 25165828
  11.0 9.4 %collective-permute-start.4 = (bf16[64,2048]{1,0:T(8,128)(2,1)S(1)}, bf16[64,2048]{1,0:T(8,128)(2,1)S(1)}, u32[]{:S(2)}, u32[]{:S(2)}) collective-permute-start(bf16[64,2048]{1,0:T(8,128)(2,1)S(1)} %shard_map.76), channel_id=1, source_target_pairs={{0,1},{1,0},{2,3},{3,2},{4,5},{5,4},{6,7},{7,6},{8,9},{9,8},{10,11... | collective-permute-start | bytes 786440 | tf_op jit(solution)/shard_map/ppermute | solution.py:202
  14.1 13.1 %collective-permute-start.6 = (bf16[64,2048]{1,0:T(8,128)(2,1)S(1)}, bf16[64,2048]{1,0:T(8,128)(2,1)S(1)}, u32[]{:S(2)}, u32[]{:S(2)}) collective-permute-start(bf16[64,2048]{1,0:T(8,128)(2,1)S(1)} %shard_map.79), channel_id=1, source_target_pairs={{0,1},{1,0},{2,3},{3,2},{4,5},{5,4},{6,7},{7,6},{8,9},{9,8},{10,11... | collective-permute-start | bytes 786440 | tf_op jit(solution)/shard_map/ppermute | solution.py:202
  14.7 5.0 %collective-permute-start.3 = (bf16[64,1024]{1,0:T(8,128)(2,1)S(1)}, bf16[64,1024]{1,0:T(8,128)(2,1)S(1)}, u32[]{:S(2)}, u32[]{:S(2)}) collective-permute-start(bf16[64,1024]{1,0:T(8,128)(2,1)S(1)} %get-tuple-element.27.rest_0_), channel_id=1, source_target_pairs={{0,4},{4,0},{1,5},{5,1},{2,6},{6,2},{3,7},{7,3},{8,12},{12,8},{9,1... | collective-permute-start | bytes 393224 | tf_op jit(solution)/shard_map/ppermute | solution.py:202
  20.5 12.0 %copy-start.5 = (bf16[1,64,4096]{2,1,0:T(8,128)(2,1)S(1)}, bf16[1,64,4096]{2,1,0:T(8,128)(2,1)}, u32[]{:S(2)}) copy-start(bf16[1,64,4096]{2,1,0:T(8,128)(2,1)} %param.13) | copy-start | bytes 1572868
  21.5 16.0 %collective-permute-start.5 = (bf16[64,2048]{1,0:T(8,128)(2,1)S(1)}, bf16[64,2048]{1,0:T(8,128)(2,1)S(1)}, u32[]{:S(2)}, u32[]{:S(2)}) collective-permute-start(bf16[64,2048]{1,0:T(8,128)(2,1)S(1)} %get-tuple-element.18), channel_id=1, source_target_pairs={{0,2},{1,3},{2,0},{3,1},{4,6},{5,7},{6,4},{7,5},{8,10},{9,11},{10,... | collective-permute-start | bytes 786440 | tf_op jit(solution)/shard_map/ppermute | solution.py:202
  24.1 22.4 %copy-start = (bf16[64,4096]{1,0:T(8,128)(2,1)S(1)}, bf16[64,4096]{1,0:T(8,128)(2,1)}, u32[]{:S(2)}) copy-start(bf16[64,4096]{1,0:T(8,128)(2,1)} %e_ref.1) | copy-start | bytes 1572868
  24.1 14.8 %collective-permute-start.7 = (bf16[64,2048]{1,0:T(8,128)(2,1)S(1)}, bf16[64,2048]{1,0:T(8,128)(2,1)S(1)}, u32[]{:S(2)}, u32[]{:S(2)}) collective-permute-start(bf16[64,2048]{1,0:T(8,128)(2,1)S(1)} %get-tuple-element.21), channel_id=1, source_target_pairs={{0,1},{1,0},{2,3},{3,2},{4,5},{5,4},{6,7},{7,6},{8,9},{9,8},{10,11... | collective-permute-start | bytes 786440 | tf_op jit(solution)/shard_map/ppermute | solution.py:202
  28.3 18.1 %collective-permute-start.8 = (bf16[64,2048]{1,0:T(8,128)(2,1)S(1)}, bf16[64,2048]{1,0:T(8,128)(2,1)S(1)}, u32[]{:S(2)}, u32[]{:S(2)}) collective-permute-start(bf16[64,2048]{1,0:T(8,128)(2,1)S(1)} %get-tuple-element.22), channel_id=1, source_target_pairs={{0,2},{1,3},{2,0},{3,1},{4,6},{5,7},{6,4},{7,5},{8,10},{9,11},{10,... | collective-permute-start | bytes 786440 | tf_op jit(solution)/shard_map/ppermute | solution.py:202
  30.0 16.4 %collective-permute-start.9 = (bf16[64,2048]{1,0:T(8,128)(2,1)S(1)}, bf16[64,2048]{1,0:T(8,128)(2,1)S(1)}, u32[]{:S(2)}, u32[]{:S(2)}) collective-permute-start(bf16[64,2048]{1,0:T(8,128)(2,1)S(1)} %get-tuple-element.23), channel_id=1, source_target_pairs={{0,1},{1,0},{2,3},{3,2},{4,5},{5,4},{6,7},{7,6},{8,9},{9,8},{10,11... | collective-permute-start | bytes 786440 | tf_op jit(solution)/shard_map/ppermute | solution.py:202
  32.5 14.0 %collective-permute-start.11 = (bf16[64,2048]{1,0:T(8,128)(2,1)S(1)}, bf16[64,2048]{1,0:T(8,128)(2,1)S(1)}, u32[]{:S(2)}, u32[]{:S(2)}) collective-permute-start(bf16[64,2048]{1,0:T(8,128)(2,1)S(1)} %get-tuple-element.25), channel_id=1, source_target_pairs={{0,8},{8,16},{16,24},{1,9},{9,17},{17,25},{2,10},{10,18},{18,26},{... | collective-permute-start | bytes 786440 | tf_op jit(solution)/shard_map/ppermute | solution.py:212
  37.5 9.1 %collective-permute-start.10 = (bf16[64,2048]{1,0:T(8,128)(2,1)S(1)}, bf16[64,2048]{1,0:T(8,128)(2,1)S(1)}, u32[]{:S(2)}, u32[]{:S(2)}) collective-permute-start(bf16[64,2048]{1,0:T(8,128)(2,1)S(1)} %get-tuple-element.26), channel_id=1, source_target_pairs={{0,8},{8,16},{16,24},{1,9},{9,17},{17,25},{2,10},{10,18},{18,26},{... | collective-permute-start | bytes 786440 | tf_op jit(solution)/shard_map/ppermute | solution.py:212

commit v4 on v3

--- a/solution.py
+++ b/solution.py
@@ -7,6 +7,9 @@
 
 HEAD_DIM = 128
 NEG = -1e30
+HOLD = 5 * 10**9
+NEAR = 4
+LONG = 3 * 10**9
 VMEM = pl.BlockSpec(memory_space=pltpu.VMEM)
 HBM = pl.BlockSpec(memory_space=pltpu.HBM)
 F32 = jnp.float32
@@ -51,7 +54,7 @@
         jax.ShapeDtypeStruct((4 * rows, 2 * half), F32),
         [VMEM],
         [pltpu.VMEM((2 * half, 128), F32)],
-        moved=1024,
+        flops=LONG,
     )(seg)
 
 
@@ -69,9 +72,9 @@
     return jnp.concatenate([o[h * rows:(h + 1) * rows] for h in range(heads)], axis=1)
 
 
-def product(att, w_ref, store, tile=512):
-    for t in range(0, w_ref.shape[1], tile):
-        store(t, tile, jnp.dot(att, w_ref[:, t:t + tile], preferred_element_type=F32))
+def product(att, w_ref, at, cols, store, tile=512):
+    for t in range(0, cols, tile):
+        store(t, tile, jnp.dot(att, w_ref[:, at + t:at + t + tile], preferred_element_type=F32))
 
 
 def choose(c, i, mine, other):
@@ -108,15 +111,14 @@
     )(*kv, bias, qx, rx, *halves)
 
 
-def first_part(att, weight):
+def first_part(att, weight, at, cols):
     rows, width = att.shape
-    cols = weight.shape[1]
 
     def body(att_ref, w_ref, a_ref):
         def store(t, tile, part):
             a_ref[:, t:t + tile] = part.astype(BF16)
 
-        product(att_ref[...], w_ref, store)
+        product(att_ref[...], w_ref, at, cols, store)
 
     return kernel_call(
         body,
@@ -127,7 +129,7 @@
     )(att, weight)
 
 
-def other_parts(att, weight, got):
+def other_parts(att, weight, at, got, hint):
     rows, width = att.shape[0] // 3, att.shape[1]
     cols = got.shape[1]
 
@@ -137,14 +139,14 @@
             f_ref[:, t:t + tile] = (part[rows:2 * rows] + got_ref[:, t:t + tile].astype(F32)).astype(BF16)
             o_ref[:, t:t + tile] = part[2 * rows:]
 
-        product(att_ref[...], w_ref, store)
+        product(att_ref[...], w_ref, at, cols, store)
 
     part = jax.ShapeDtypeStruct((rows, cols), BF16)
     return kernel_call(
         body,
         (part, part, jax.ShapeDtypeStruct((rows, cols), F32)),
         [VMEM] * 3,
-        flops=6 * rows * width * cols,
+        flops=hint,
         moved=weight.size,
     )(att, weight, got)
 
@@ -156,45 +158,33 @@
     return kernel_call(body, jax.ShapeDtypeStruct(own.shape, F32), [VMEM] * 2, moved=own.size * 10)(own, y)
 
 
-def add_rest(sum0, own1, gotm0, y1, gotm1):
-    rows, cols = sum0.shape
-
-    def body(s_ref, o_ref, m0_ref, y_ref, m1_ref, out_ref):
-        out_ref[:, :cols] = s_ref[...] + m0_ref[...].astype(F32)
-        out_ref[:, cols:] = o_ref[...] + m1_ref[...].astype(F32) + y_ref[...].astype(F32)
-
-    return kernel_call(body, jax.ShapeDtypeStruct((rows, 2 * cols), F32), [VMEM] * 5, moved=sum0.size * 22)(
-        sum0, own1, gotm0, y1, gotm1
-    )
-
-
-def finish(branch, embedded, arrived):
-    rows, cols = branch.shape
-    n = len(arrived)
-    step = cols // n
-
-    def body(b_ref, e_ref, *rest):
-        pieces, out_ref, done_ref, sems = rest[:n], rest[n], rest[n + 1], rest[n + 2]
-        first = lax.axis_index("phase") == 0
-        copies = []
-        for p in range(n):
-            at = slice(p * step, (p + 1) * step)
-            resid = jnp.where(first, e_ref[:, at], pieces[p][...])
-            done_ref[:, at] = (resid.astype(F32) + b_ref[:, at]).astype(BF16)
-            copies.append(pltpu.make_async_copy(done_ref.at[:, at], out_ref.at[:, at], sems.at[p]))
-            copies[-1].start()
-        for copy in copies:
-            copy.wait()
-
+def finish(parts, embedded, arrived, at, out, hint):
+    rows, cols = arrived.shape
+    n = len(parts)
+
+    def body(*refs):
+        e_ref, a_ref = refs[n:n + 2]
+        out_ref, done_ref, sem = refs[-3:]
+        resid = jnp.where(lax.axis_index("phase") == 0, e_ref[:, at:at + cols], a_ref[...])
+        total = resid.astype(F32)
+        for ref in refs[:n]:
+            total = total + ref[...].astype(F32)
+        done_ref[...] = total.astype(BF16)
+        copy = pltpu.make_async_copy(done_ref, out_ref.at[:, at:at + cols], sem)
+        copy.start()
+        copy.wait()
+
+    before = () if out is None else (out,)
     return pl.pallas_call(
         body,
-        out_shape=jax.ShapeDtypeStruct((rows, cols), BF16),
-        in_specs=[VMEM] * (2 + n),
+        out_shape=jax.ShapeDtypeStruct(embedded.shape, BF16),
+        in_specs=[VMEM] * (n + 2) + [HBM] * len(before),
         out_specs=HBM,
-        scratch_shapes=[pltpu.VMEM((rows, cols), BF16), pltpu.SemaphoreType.DMA((n,))],
+        scratch_shapes=[pltpu.VMEM((rows, cols), BF16), pltpu.SemaphoreType.DMA],
+        input_output_aliases={n + 2: 0} if before else {},
         compiler_params=pltpu.CompilerParams(vmem_limit_bytes=16 * 1024 * 1024),
-        cost_estimate=pl.CostEstimate(flops=0, bytes_accessed=branch.size * 10, transcendentals=0),
-    )(branch, embedded, *arrived)
+        cost_estimate=pl.CostEstimate(flops=hint, bytes_accessed=embedded.size * 4, transcendentals=0),
+    )(*parts, embedded, arrived, *before)
 
 
 def swap(x, axis, by):
@@ -221,33 +211,33 @@
     q = queries[0]
     rows = q.shape[0] // 2
     cols = out_weight.shape[1] // 2
+    near = NEAR * cols // 4
     k, v = keys[0], values[0]
-    kr, vr = swap(k, "ctx", 1), swap(v, "ctx", 1)
     low = lax.axis_index("tp") & 1
     qx = lax.dynamic_slice_in_dim(q, (1 - low) * rows, rows)
     qy = lax.dynamic_slice_in_dim(q, low * rows, rows)
     rx = swap(qx, "ctx", 1)
-    ry = swap(qy, "ctx", 1)
-    bias, left = lax.optimization_barrier((mask(seg_ids, rows), out_weight[:, :cols]))
+    kr, vr = swap(after(k, qx), "ctx", 1), swap(after(v, qx), "ctx", 1)
+    bias = mask(seg_ids, rows)
     kv = (k, v, kr, vr)
     att = attend_blocks(kv, bias, qx, rx)
-    a0 = first_part(att, left)
+    a0 = first_part(att, out_weight, 0, near)
     got0 = swap(a0, "tp", 1)
-    right = after(out_weight, a0)[:, cols:]
+    ry = swap(after(qy, a0), "ctx", 1)
+    a1 = first_part(after(att, a0), out_weight, near, 2 * cols - near)
+    got1 = swap(a1, "tp", 1)
     rest = attend_blocks(kv, bias, qx, rx, (qy, ry))
-    a1 = first_part(att, right)
-    got1 = swap(a1, "tp", 1)
-    m0, f0, own0 = other_parts(rest, left, got0)
+    m0, f0, own0 = other_parts(rest, out_weight, 0, got0, HOLD)
     gotm0 = swap(m0, "tp", 1)
     y0 = swap(f0, "tp", 2)
-    m1, f1, own1 = other_parts(rest, right, got1)
+    m1, f1, own1 = other_parts(rest, out_weight, near, got1, 0)
     gotm1 = swap(m1, "tp", 1)
     y1 = swap(f1, "tp", 2)
     prev = after(hidden_prev, f1)[0]
     arrived = [passed_along(prev[:, at:at + cols], "phase", 1) for at in (0, cols)]
     sum0 = add_far(own0, y0)
-    branch = add_rest(sum0, own1, gotm0, y1, gotm1)
-    return finish(branch, embedded, arrived)[None]
+    out = finish((sum0, gotm0), embedded, arrived[0], 0, None, 0)
+    return finish((own1, y1, gotm1), embedded, arrived[1], cols, out, 0)[None]
 
 
 def on_device(queries, keys, values, seg_ids, out_weight, embedded, hidden_prev):

time: 47.6 us -> 46.5 us (0.977)
  starting transfers between devices: 19.1 us -> 23.2 us
  local copies, waits for them, and re-layouts: 4.96 us -> 1.88 us
  waiting for transfers between devices: 16.9 us -> 14 us
  Pallas kernels: 6.21 us -> 6.81 us
    slice x2 -> x0, local copies, waits for them, and re-layouts: 3.23 us -> none  [the longest x1 2.66 us: on_pair(): out_weight[:, :cols]]
    ppermute x10, waiting for transfers between devices: 16.9 us -> 14 us  [swap(): return lax.ppermute(x, axis, [(i, i ^ by) for i in range(peers)])]
    ppermute x2, starting transfers between devices: 2.6 us -> 5.15 us  [passed_along(): return lax.ppermute(shard, axis, pairs)]
    ppermute x10, starting transfers between devices: 16.5 us -> 18.1 us  [swap(): return lax.ppermute(x, axis, [(i, i ^ by) for i in range(peers)])]
    pallas_call x2, Pallas kernels: 0.99 us -> 1.65 us  [finish(): pl.pallas_call(body, out_shape=jax.ShapeDtypeStruct(embedded.shape, BF16)...]
  transfers between devices with their start and end apart: 12 -> 12, of which waited for: 5 -> 6; matrix products, arithmetic and copies ran while one was open for 7% -> 0% of each run, Pallas kernels for 8% -> 10%
where the time goes in v4:
time: 46.5 us; the launch traced here: 46.1 us
  starting transfers between devices  23.2 us (50%)
  waiting for transfers between devices  14 us (30%)
  Pallas kernels  6.81 us (15%)
  local copies, waits for them, and re-layouts  1.88 us (4%)
    ppermute x10, starting transfers between devices, swap(): return lax.ppermute(x, axis, [(i, i ^ by) for i in range(peers)])  18.1 us
    ppermute x10, waiting for transfers between devices, swap(): return lax.ppermute(x, axis, [(i, i ^ by) for i in range(peers)])  14 us
    ppermute x2, starting transfers between devices, passed_along(): return lax.ppermute(shard, axis, pairs)  5.15 us
    pallas_call x2, Pallas kernels, other_parts(): kernel_call(body, (part, part, jax.ShapeDtypeStruct((rows, cols), F32)),...  1.98 us
    pallas_call x2, Pallas kernels, first_part(): kernel_call(body, jax.ShapeDtypeStruct((rows, cols), BF16), [VMEM] * 2, f...  1.67 us
    pallas_call x2, Pallas kernels, finish(): pl.pallas_call(body, out_shape=jax.ShapeDtypeStruct(embedded.shape, BF16)...  1.65 us
    pallas_call x2, Pallas kernels, attend_blocks(): kernel_call(body, jax.ShapeDtypeStruct((n * rows, width), BF16), [VMEM] *...  1.26 us
    dynamic_slice x1, local copies, waits for them, and re-layouts, on_pair(): qy = lax.dynamic_slice_in_dim(q, low * rows, rows)  1.13 us
  transfers between devices with their start and end apart: 12, of which 6 were waited for; matrix products, arithmetic and copies ran while one was open for 0% of the time, Pallas kernels for 10%

profile of v4, /device:TPU:0, one launch (start us, length us, event | category | flops | bytes accessed | tf_op | source)
XLA Modules:
  0.0 46.1 jit_solution(15885877183916243194)
XLA Ops:
  0.0 1.1 %dynamic-slice_bitcast_fusion = (bf16[64,1024]{1,0:T(8,128)(2,1)S(1)}, bf16[64,1024]{1,0:T(8,128)(2,1)S(1)}) fusion(bf16[1,128,1024]{2,1,0:T(8,128)(2,1)} %param.7, s32[]{:T(128)S(6)} %select_n.7, s32[]{:T(128)S(6)} %select_n.6), kind=kLoop, calls=%fused_computation | loop fusion | bytes 524296 | tf_op jit(solution)/shard_map/dynamic_slice | solution.py:218
  1.1 3.0 %collective-permute-start.2 = (bf16[64,1024]{1,0:T(8,128)(2,1)S(1)}, bf16[64,1024]{1,0:T(8,128)(2,1)S(1)}, u32[]{:S(2)}, u32[]{:S(2)}) collective-permute-start(bf16[64,1024]{1,0:T(8,128)(2,1)S(1)} %get-tuple-element.30.qx_ref), channel_id=1, source_target_pairs={{0,4},{4,0},{1,5},{5,1},{2,6},{6,2},{3,7},{7,3},{8,12},{12,8},{9,1... | collective-permute-start | bytes 393224 | tf_op jit(solution)/shard_map/ppermute | solution.py:192
  4.2 0.1 collective-permute-start
  4.3 1.9 %collective-permute-start.1 = (bf16[128,128]{1,0:T(8,128)(2,1)}, bf16[128,128]{1,0:T(8,128)(2,1)S(1)}, u32[]{:S(2)}, u32[]{:S(2)}) collective-permute-start(bf16[128,128]{1,0:T(8,128)(2,1)} %bitcast.11), channel_id=1, source_target_pairs={{0,4},{4,0},{1,5},{5,1},{2,6},{6,2},{3,7},{7,3},{8,12},{12,8},{9,1... | collective-permute-start | bytes 98312 | tf_op jit(solution)/shard_map/ppermute | solution.py:192
  6.2 0.7 %copy-done.4 = s32[1,256]{1,0:T(1,128)S(1)} copy-done((s32[1,256]{1,0:T(1,128)S(1)}, s32[1,256]{1,0:T(1,128)}, u32[]{:S(2)}) %copy-start.4) | copy-done | bytes 1048
  6.9 0.2 shard_map.73.bias_ref
  7.1 1.6 %collective-permute-done.kr = bf16[128,128]{1,0:T(8,128)(2,1)S(1)} collective-permute-done((bf16[128,128]{1,0:T(8,128)(2,1)}, bf16[128,128]{1,0:T(8,128)(2,1)S(1)}, u32[]{:S(2)}, u32[]{:S(2)}) %collective-permute-start) | collective-permute-done | bytes 32800 | tf_op jit(solution)/shard_map/ppermute | solution.py:192
  8.7 0.4 collective-permute-done.1.vr
  9.1 0.5 %shard_map.74.att_ref = bf16[64,1024]{1,0:T(8,128)(2,1)S(1)} custom-call(bf16[128,128]{1,0:T(8,128)(2,1)S(1)} %bitcast.9, bf16[128,128]{1,0:T(8,128)(2,1)S(1)} %bitcast.12, bf16[128,128]{1,0:T(8,128)(2,1)S(1)} %collective-permute-done.kr, bf16[128,128]{1,0:T(8,128)(2,1)S(1)} %collective-permute-done.1.vr, f32[256,256]{1,0:T(8,128)S(1)} %shard_map.73.bias_ref, ...), custom_call_target="tpu_custom_call" | custom-call | bytes 262144 | tf_op jit(solution)/shard_map/pallas_call | solution.py:106
  9.6 0.8 %shard_map.75 = bf16[64,2048]{1,0:T(8,128)(2,1)S(1)} custom-call(bf16[64,1024]{1,0:T(8,128)(2,1)S(1)} %shard_map.74.att_ref, bf16[1024,4096]{1,0:T(8,128)(2,1)S(1)} %copy-done), custom_call_target="tpu_custom_call" | custom-call | flops 268435456 | bytes 4194304 | tf_op jit(solution)/shard_map/pallas_call | solution.py:123
  10.4 1.9 %collective-permute-start.8 = (bf16[64,2048]{1,0:T(8,128)(2,1)S(1)}, bf16[64,2048]{1,0:T(8,128)(2,1)S(1)}, u32[]{:S(2)}, u32[]{:S(2)}) collective-permute-start(bf16[64,2048]{1,0:T(8,128)(2,1)S(1)} %shard_map.75), channel_id=1, source_target_pairs={{0,1},{1,0},{2,3},{3,2},{4,5},{5,4},{6,7},{7,6},{8,9},{9,8},{10,11... | collective-permute-start | bytes 786440 | tf_op jit(solution)/shard_map/ppermute | solution.py:192
  12.3 1.5 %collective-permute-start.3 = (bf16[64,1024]{1,0:T(8,128)(2,1)S(1)}, bf16[64,1024]{1,0:T(8,128)(2,1)S(1)}, u32[]{:S(2)}, u32[]{:S(2)}) collective-permute-start(bf16[64,1024]{1,0:T(8,128)(2,1)S(1)} %get-tuple-element.18.rest_0_), channel_id=1, source_target_pairs={{0,4},{4,0},{1,5},{5,1},{2,6},{6,2},{3,7},{7,3},{8,12},{12,8},{9,1... | collective-permute-start | bytes 393224 | tf_op jit(solution)/shard_map/ppermute | solution.py:192
  13.8 0.8 %shard_map.77 = bf16[64,2048]{1,0:T(8,128)(2,1)S(1)} custom-call(bf16[64,1024]{1,0:T(8,128)(2,1)S(1)} %shard_map.74.att_ref, bf16[1024,4096]{1,0:T(8,128)(2,1)S(1)} %copy-done), custom_call_target="tpu_custom_call" | custom-call | flops 268435456 | bytes 4194304 | tf_op jit(solution)/shard_map/pallas_call | solution.py:123
  14.7 0.5 %collective-permute-start.4 = (bf16[64,2048]{1,0:T(8,128)(2,1)S(1)}, bf16[64,2048]{1,0:T(8,128)(2,1)S(1)}, u32[]{:S(2)}, u32[]{:S(2)}) collective-permute-start(bf16[64,2048]{1,0:T(8,128)(2,1)S(1)} %shard_map.77), channel_id=1, source_target_pairs={{0,1},{1,0},{2,3},{3,2},{4,5},{5,4},{6,7},{7,6},{8,9},{9,8},{10,11... | collective-permute-start | bytes 786440 | tf_op jit(solution)/shard_map/ppermute | solution.py:192
  15.2 2.1 %collective-permute-done.3.rest_1_ = bf16[64,1024]{1,0:T(8,128)(2,1)S(1)} collective-permute-done((bf16[64,1024]{1,0:T(8,128)(2,1)S(1)}, bf16[64,1024]{1,0:T(8,128)(2,1)S(1)}, u32[]{:S(2)}, u32[]{:S(2)}) %collective-permute-start.3) | collective-permute-done | bytes 131104 | tf_op jit(solution)/shard_map/ppermute | solution.py:192
  17.3 0.8 %shard_map.76.att_ref = bf16[192,1024]{1,0:T(8,128)(2,1)S(1)} custom-call(bf16[128,128]{1,0:T(8,128)(2,1)S(1)} %bitcast.10, bf16[128,128]{1,0:T(8,128)(2,1)S(1)} %bitcast.13, bf16[128,128]{1,0:T(8,128)(2,1)S(1)} %collective-permute-done.kr, bf16[128,128]{1,0:T(8,128)(2,1)S(1)} %collective-permute-done.1.vr, f32[256,256]{1,0:T(8,128)S(1)} %shard_map.73.bias_ref, ...), custom_call_target="tpu_custom_call" | custom-call | bytes 262144 | tf_op jit(solution)/shard_map/pallas_call | solution.py:106
  18.1 1.7 %collective-permute-done.8.got_ref = bf16[64,2048]{1,0:T(8,128)(2,1)S(1)} collective-permute-done((bf16[64,2048]{1,0:T(8,128)(2,1)S(1)}, bf16[64,2048]{1,0:T(8,128)(2,1)S(1)}, u32[]{:S(2)}, u32[]{:S(2)}) %collective-permute-start.8) | collective-permute-done | bytes 262176 | tf_op jit(solution)/shard_map/ppermute | solution.py:192
  19.8 1.0 %shard_map.79 = (bf16[64,2048]{1,0:T(8,128)(2,1)S(1)}, bf16[64,2048]{1,0:T(8,128)(2,1)S(1)}, f32[64,2048]{1,0:T(8,128)S(1)}) custom-call(bf16[192,1024]{1,0:T(8,128)(2,1)S(1)} %shard_map.76.att_ref, bf16[1024,4096]{1,0:T(8,128)(2,1)S(1)} %copy-done, bf16[64,2048]{1,0:T(8,128)(2,1)S(1)} %collective-permute-done.8.got_ref), custom_call_target="tpu_custom_call" | custom-call | flops 5000000000 | bytes 4194304 | tf_op jit(solution)/shard_map/pallas_call | solution.py:145
  20.8 0.0 copy-start.5
  20.8 0.0 copy-start.1
  20.8 2.9 %collective-permute-start.9 = (bf16[64,2048]{1,0:T(8,128)(2,1)S(1)}, bf16[64,2048]{1,0:T(8,128)(2,1)S(1)}, u32[]{:S(2)}, u32[]{:S(2)}) collective-permute-start(bf16[64,2048]{1,0:T(8,128)(2,1)S(1)} %get-tuple-element.25), channel_id=1, source_target_pairs={{0,2},{1,3},{2,0},{3,1},{4,6},{5,7},{6,4},{7,5},{8,10},{9,11},{10,... | collective-permute-start | bytes 786440 | tf_op jit(solution)/shard_map/ppermute | solution.py:192
  23.7 1.6 %collective-permute-start.10 = (bf16[64,2048]{1,0:T(8,128)(2,1)S(1)}, bf16[64,2048]{1,0:T(8,128)(2,1)S(1)}, u32[]{:S(2)}, u32[]{:S(2)}) collective-permute-start(bf16[64,2048]{1,0:T(8,128)(2,1)S(1)} %get-tuple-element.26), channel_id=1, source_target_pairs={{0,1},{1,0},{2,3},{3,2},{4,5},{5,4},{6,7},{7,6},{8,9},{9,8},{10,11... | collective-permute-start | bytes 786440 | tf_op jit(solution)/shard_map/ppermute | solution.py:192
  25.2 4.4 %collective-permute-done.4.got_ref = bf16[64,2048]{1,0:T(8,128)(2,1)S(1)} collective-permute-done((bf16[64,2048]{1,0:T(8,128)(2,1)S(1)}, bf16[64,2048]{1,0:T(8,128)(2,1)S(1)}, u32[]{:S(2)}, u32[]{:S(2)}) %collective-permute-start.4) | collective-permute-done | bytes 262176 | tf_op jit(solution)/shard_map/ppermute | solution.py:192
  29.6 1.0 %shard_map.78 = (bf16[64,2048]{1,0:T(8,128)(2,1)S(1)}, bf16[64,2048]{1,0:T(8,128)(2,1)S(1)}, f32[64,2048]{1,0:T(8,128)S(1)}) custom-call(bf16[192,1024]{1,0:T(8,128)(2,1)S(1)} %shard_map.76.att_ref, bf16[1024,4096]{1,0:T(8,128)(2,1)S(1)} %copy-done, bf16[64,2048]{1,0:T(8,128)(2,1)S(1)} %collective-permute-done.4.got_ref), custom_call_target="tpu_custom_call" | custom-call | bytes 4194304 | tf_op jit(solution)/shard_map/pallas_call | solution.py:145
  30.6 1.6 %collective-permute-start.5 = (bf16[64,2048]{1,0:T(8,128)(2,1)S(1)}, bf16[64,2048]{1,0:T(8,128)(2,1)S(1)}, u32[]{:S(2)}, u32[]{:S(2)}) collective-permute-start(bf16[64,2048]{1,0:T(8,128)(2,1)S(1)} %get-tuple-element.21), channel_id=1, source_target_pairs={{0,2},{1,3},{2,0},{3,1},{4,6},{5,7},{6,4},{7,5},{8,10},{9,11},{10,... | collective-permute-start | bytes 786440 | tf_op jit(solution)/shard_map/ppermute | solution.py:192
  32.3 1.3 %collective-permute-start.11 = (bf16[64,2048]{1,0:T(8,128)(2,1)S(1)}, bf16[64,2048]{1,0:T(8,128)(2,1)S(1)}, u32[]{:S(2)}, u32[]{:S(2)}) collective-permute-start(bf16[64,2048]{1,0:T(8,128)(2,1)S(1)} %get-tuple-element.27), channel_id=1, source_target_pairs={{0,8},{8,16},{16,24},{1,9},{9,17},{17,25},{2,10},{10,18},{18,26},{... | collective-permute-start | bytes 786440 | tf_op jit(solution)/shard_map/ppermute | solution.py:202
  33.6 3.0 %collective-permute-start.6 = (bf16[64,2048]{1,0:T(8,128)(2,1)S(1)}, bf16[64,2048]{1,0:T(8,128)(2,1)S(1)}, u32[]{:S(2)}, u32[]{:S(2)}) collective-permute-start(bf16[64,2048]{1,0:T(8,128)(2,1)S(1)} %get-tuple-element.22), channel_id=1, source_target_pairs={{0,1},{1,0},{2,3},{3,2},{4,5},{5,4},{6,7},{7,6},{8,9},{9,8},{10,11... | collective-permute-start | bytes 786440 | tf_op jit(solution)/shard_map/ppermute | solution.py:192
  36.7 0.0 collective-permute-done.9.y_ref
  36.7 3.8 %collective-permute-start.7 = (bf16[64,2048]{1,0:T(8,128)(2,1)S(1)}, bf16[64,2048]{1,0:T(8,128)(2,1)S(1)}, u32[]{:S(2)}, u32[]{:S(2)}) collective-permute-start(bf16[64,2048]{1,0:T(8,128)(2,1)S(1)} %get-tuple-element.28), channel_id=1, source_target_pairs={{0,8},{8,16},{16,24},{1,9},{9,17},{17,25},{2,10},{10,18},{18,26},{... | collective-permute-start | bytes 786440 | tf_op jit(solution)/shard_map/ppermute | solution.py:202
  40.6 0.8 %shard_map.81.refs_5_ = bf16[64,4096]{1,0:T(8,128)(2,1)} custom-call(f32[64,2048]{1,0:T(8,128)S(1)} %shard_map.80.refs_0_, bf16[64,2048]{1,0:T(8,128)(2,1)S(1)} %collective-permute-done.10.refs_1_, bf16[64,4096]{1,0:T(8,128)(2,1)S(1)} %copy-done.1, bf16[64,2048]{1,0:T(8,128)(2,1)S(1)} %collective-permute-done.11.refs_3_), custom_call_target="tpu_custom_call" | custom-call | bytes 1048576 | tf_op jit(solution)/shard_map/pallas_call | solution.py:178
  41.4 3.8 %collective-permute-done.6.refs_2_ = bf16[64,2048]{1,0:T(8,128)(2,1)S(1)} collective-permute-done((bf16[64,2048]{1,0:T(8,128)(2,1)S(1)}, bf16[64,2048]{1,0:T(8,128)(2,1)S(1)}, u32[]{:S(2)}, u32[]{:S(2)}) %collective-permute-start.6) | collective-permute-done | bytes 262176 | tf_op jit(solution)/shard_map/ppermute | solution.py:192
  45.2 0.8 %shard_map.82 = bf16[64,4096]{1,0:T(8,128)(2,1)} custom-call(f32[64,2048]{1,0:T(8,128)S(1)} %get-tuple-element.20.refs_0_, bf16[64,2048]{1,0:T(8,128)(2,1)S(1)} %collective-permute-done.5.refs_1_, bf16[64,2048]{1,0:T(8,128)(2,1)S(1)} %collective-permute-done.6.refs_2_, bf16[64,4096]{1,0:T(8,128)(2,1)S(1)} %copy-done.1, ...), custom_call_target="tpu_custom_call", output_to_operand_aliasing={{}: (5, {})} | custom-call | bytes 1048576 | tf_op jit(solution)/shard_map/pallas_call | solution.py:178
  (16 shorter events, 0.1 us)
Async XLA Ops:
  0.0 9.1 %copy-start.2 = (bf16[1,128,128]{2,1,0:T(8,128)(2,1)S(1)}, bf16[1,128,128]{2,1,0:T(8,128)(2,1)}, u32[]{:S(2)}) copy-start(bf16[1,128,128]{2,1,0:T(8,128)(2,1)} %param.8) | copy-start | bytes 98308
  0.0 9.1 %copy-start.3 = (bf16[1,128,128]{2,1,0:T(8,128)(2,1)S(1)}, bf16[1,128,128]{2,1,0:T(8,128)(2,1)}, u32[]{:S(2)}) copy-start(bf16[1,128,128]{2,1,0:T(8,128)(2,1)} %param.9) | copy-start | bytes 98308
  0.0 9.6 %copy-start = (bf16[1024,4096]{1,0:T(8,128)(2,1)S(1)}, bf16[1024,4096]{1,0:T(8,128)(2,1)}, u32[]{:S(2)}) copy-start(bf16[1024,4096]{1,0:T(8,128)(2,1)} %w_ref.7) | copy-start | bytes 25165828
  1.1 7.9 %collective-permute-start.2 = (bf16[64,1024]{1,0:T(8,128)(2,1)S(1)}, bf16[64,1024]{1,0:T(8,128)(2,1)S(1)}, u32[]{:S(2)}, u32[]{:S(2)}) collective-permute-start(bf16[64,1024]{1,0:T(8,128)(2,1)S(1)} %get-tuple-element.30.qx_ref), channel_id=1, source_target_pairs={{0,4},{4,0},{1,5},{5,1},{2,6},{6,2},{3,7},{7,3},{8,12},{12,8},{9,1... | collective-permute-start | bytes 393224 | tf_op jit(solution)/shard_map/ppermute | solution.py:192
  4.2 4.5 %collective-permute-start = (bf16[128,128]{1,0:T(8,128)(2,1)}, bf16[128,128]{1,0:T(8,128)(2,1)S(1)}, u32[]{:S(2)}, u32[]{:S(2)}) collective-permute-start(bf16[128,128]{1,0:T(8,128)(2,1)} %bitcast.8), channel_id=1, source_target_pairs={{0,4},{4,0},{1,5},{5,1},{2,6},{6,2},{3,7},{7,3},{8,12},{12,8},{9,1... | collective-permute-start | bytes 98312 | tf_op jit(solution)/shard_map/ppermute | solution.py:192
  4.3 4.8 %collective-permute-start.1 = (bf16[128,128]{1,0:T(8,128)(2,1)}, bf16[128,128]{1,0:T(8,128)(2,1)S(1)}, u32[]{:S(2)}, u32[]{:S(2)}) collective-permute-start(bf16[128,128]{1,0:T(8,128)(2,1)} %bitcast.11), channel_id=1, source_target_pairs={{0,4},{4,0},{1,5},{5,1},{2,6},{6,2},{3,7},{7,3},{8,12},{12,8},{9,1... | collective-permute-start | bytes 98312 | tf_op jit(solution)/shard_map/ppermute | solution.py:192
  6.2 0.7 %copy-start.4 = (s32[1,256]{1,0:T(1,128)S(1)}, s32[1,256]{1,0:T(1,128)}, u32[]{:S(2)}) copy-start(s32[1,256]{1,0:T(1,128)} %seg_ref.1) | copy-start | bytes 3076
  10.4 9.3 %collective-permute-start.8 = (bf16[64,2048]{1,0:T(8,128)(2,1)S(1)}, bf16[64,2048]{1,0:T(8,128)(2,1)S(1)}, u32[]{:S(2)}, u32[]{:S(2)}) collective-permute-start(bf16[64,2048]{1,0:T(8,128)(2,1)S(1)} %shard_map.75), channel_id=1, source_target_pairs={{0,1},{1,0},{2,3},{3,2},{4,5},{5,4},{6,7},{7,6},{8,9},{9,8},{10,11... | collective-permute-start | bytes 786440 | tf_op jit(solution)/shard_map/ppermute | solution.py:192
  12.3 5.0 %collective-permute-start.3 = (bf16[64,1024]{1,0:T(8,128)(2,1)S(1)}, bf16[64,1024]{1,0:T(8,128)(2,1)S(1)}, u32[]{:S(2)}, u32[]{:S(2)}) collective-permute-start(bf16[64,1024]{1,0:T(8,128)(2,1)S(1)} %get-tuple-element.18.rest_0_), channel_id=1, source_target_pairs={{0,4},{4,0},{1,5},{5,1},{2,6},{6,2},{3,7},{7,3},{8,12},{12,8},{9,1... | collective-permute-start | bytes 393224 | tf_op jit(solution)/shard_map/ppermute | solution.py:192
  14.7 14.9 %collective-permute-start.4 = (bf16[64,2048]{1,0:T(8,128)(2,1)S(1)}, bf16[64,2048]{1,0:T(8,128)(2,1)S(1)}, u32[]{:S(2)}, u32[]{:S(2)}) collective-permute-start(bf16[64,2048]{1,0:T(8,128)(2,1)S(1)} %shard_map.77), channel_id=1, source_target_pairs={{0,1},{1,0},{2,3},{3,2},{4,5},{5,4},{6,7},{7,6},{8,9},{9,8},{10,11... | collective-permute-start | bytes 786440 | tf_op jit(solution)/shard_map/ppermute | solution.py:192
  20.8 11.5 %copy-start.5 = (bf16[1,64,4096]{2,1,0:T(8,128)(2,1)S(1)}, bf16[1,64,4096]{2,1,0:T(8,128)(2,1)}, u32[]{:S(2)}) copy-start(bf16[1,64,4096]{2,1,0:T(8,128)(2,1)} %param.13) | copy-start | bytes 1572868
  20.8 19.8 %copy-start.1 = (bf16[64,4096]{1,0:T(8,128)(2,1)S(1)}, bf16[64,4096]{1,0:T(8,128)(2,1)}, u32[]{:S(2)}) copy-start(bf16[64,4096]{1,0:T(8,128)(2,1)} %refs_3_.1) | copy-start | bytes 1572868
  20.8 15.9 %collective-permute-start.9 = (bf16[64,2048]{1,0:T(8,128)(2,1)S(1)}, bf16[64,2048]{1,0:T(8,128)(2,1)S(1)}, u32[]{:S(2)}, u32[]{:S(2)}) collective-permute-start(bf16[64,2048]{1,0:T(8,128)(2,1)S(1)} %get-tuple-element.25), channel_id=1, source_target_pairs={{0,2},{1,3},{2,0},{3,1},{4,6},{5,7},{6,4},{7,5},{8,10},{9,11},{10,... | collective-permute-start | bytes 786440 | tf_op jit(solution)/shard_map/ppermute | solution.py:192
  23.7 16.9 %collective-permute-start.10 = (bf16[64,2048]{1,0:T(8,128)(2,1)S(1)}, bf16[64,2048]{1,0:T(8,128)(2,1)S(1)}, u32[]{:S(2)}, u32[]{:S(2)}) collective-permute-start(bf16[64,2048]{1,0:T(8,128)(2,1)S(1)} %get-tuple-element.26), channel_id=1, source_target_pairs={{0,1},{1,0},{2,3},{3,2},{4,5},{5,4},{6,7},{7,6},{8,9},{9,8},{10,11... | collective-permute-start | bytes 786440 | tf_op jit(solution)/shard_map/ppermute | solution.py:192
  30.6 14.6 %collective-permute-start.5 = (bf16[64,2048]{1,0:T(8,128)(2,1)S(1)}, bf16[64,2048]{1,0:T(8,128)(2,1)S(1)}, u32[]{:S(2)}, u32[]{:S(2)}) collective-permute-start(bf16[64,2048]{1,0:T(8,128)(2,1)S(1)} %get-tuple-element.21), channel_id=1, source_target_pairs={{0,2},{1,3},{2,0},{3,1},{4,6},{5,7},{6,4},{7,5},{8,10},{9,11},{10,... | collective-permute-start | bytes 786440 | tf_op jit(solution)/shard_map/ppermute | solution.py:192
  32.3 8.3 %collective-permute-start.11 = (bf16[64,2048]{1,0:T(8,128)(2,1)S(1)}, bf16[64,2048]{1,0:T(8,128)(2,1)S(1)}, u32[]{:S(2)}, u32[]{:S(2)}) collective-permute-start(bf16[64,2048]{1,0:T(8,128)(2,1)S(1)} %get-tuple-element.27), channel_id=1, source_target_pairs={{0,8},{8,16},{16,24},{1,9},{9,17},{17,25},{2,10},{10,18},{18,26},{... | collective-permute-start | bytes 786440 | tf_op jit(solution)/shard_map/ppermute | solution.py:202
  33.6 11.6 %collective-permute-start.6 = (bf16[64,2048]{1,0:T(8,128)(2,1)S(1)}, bf16[64,2048]{1,0:T(8,128)(2,1)S(1)}, u32[]{:S(2)}, u32[]{:S(2)}) collective-permute-start(bf16[64,2048]{1,0:T(8,128)(2,1)S(1)} %get-tuple-element.22), channel_id=1, source_target_pairs={{0,1},{1,0},{2,3},{3,2},{4,5},{5,4},{6,7},{7,6},{8,9},{9,8},{10,11... | collective-permute-start | bytes 786440 | tf_op jit(solution)/shard_map/ppermute | solution.py:192
  36.7 8.6 %collective-permute-start.7 = (bf16[64,2048]{1,0:T(8,128)(2,1)S(1)}, bf16[64,2048]{1,0:T(8,128)(2,1)S(1)}, u32[]{:S(2)}, u32[]{:S(2)}) collective-permute-start(bf16[64,2048]{1,0:T(8,128)(2,1)S(1)} %get-tuple-element.28), channel_id=1, source_target_pairs={{0,8},{8,16},{16,24},{1,9},{9,17},{17,25},{2,10},{10,18},{18,26},{... | collective-permute-start | bytes 786440 | tf_op jit(solution)/shard_map/ppermute | solution.py:202

commit v5 on v4

--- a/solution.py
+++ b/solution.py
@@ -7,9 +7,8 @@
 
 HEAD_DIM = 128
 NEG = -1e30
+LONG = 3 * 10**9
 HOLD = 5 * 10**9
-NEAR = 4
-LONG = 3 * 10**9
 VMEM = pl.BlockSpec(memory_space=pltpu.VMEM)
 HBM = pl.BlockSpec(memory_space=pltpu.HBM)
 F32 = jnp.float32
@@ -81,34 +80,50 @@
     return jnp.where(c == i >> 1, mine, other)
 
 
-def attend_blocks(kv, bias, qx, rx, halves=()):
+def other_blocks(kv, bias, qx, rx, qy, ry):
     rows, width = qx.shape
-    n = 3 if halves else 1
-
-    def body(kl, vl, kr, vr, bias_ref, qx_ref, rx_ref, *rest):
+
+    def body(kl, vl, kr, vr, bias_ref, qx_ref, rx_ref, qy_ref, ry_ref, att_ref):
         c, i = lax.axis_index("ctx"), lax.axis_index("tp")
-        att_ref = rest[-1]
         k = jnp.concatenate((kl[...], kr[...]), axis=0)
         v = jnp.concatenate((vl[...], vr[...]), axis=0)
-        if halves:
-            qy_ref, ry_ref = rest[:2]
-            blocks = (
-                choose(c, i, qx_ref[...], rx_ref[...]),
-                choose(c, i, ry_ref[...], qy_ref[...]),
-                choose(c, i, qy_ref[...], ry_ref[...]),
-            )
-        else:
-            blocks = (choose(c, i, rx_ref[...], qx_ref[...]),)
-        first = 1 if halves else 0
+        blocks = (
+            choose(c, i, qx_ref[...], rx_ref[...]),
+            choose(c, i, ry_ref[...], qy_ref[...]),
+            choose(c, i, qy_ref[...], ry_ref[...]),
+        )
         for b, q in enumerate(blocks):
-            att_ref[b * rows:(b + 1) * rows, :] = attend(q, k, v, bias_ref[(first + b) * rows:(first + b + 1) * rows])
-
-    return kernel_call(
-        body,
-        jax.ShapeDtypeStruct((n * rows, width), BF16),
-        [VMEM] * (7 + len(halves)),
+            att_ref[b * rows:(b + 1) * rows, :] = attend(q, k, v, bias_ref[(b + 1) * rows:(b + 2) * rows])
+
+    return kernel_call(
+        body,
+        jax.ShapeDtypeStruct((3 * rows, width), BF16),
+        [VMEM] * 9,
         moved=qx.size * 4,
-    )(*kv, bias, qx, rx, *halves)
+    )(*kv, bias, qx, rx, qy, ry)
+
+
+def first_block(kv, bias, qx, rx, weight, cols):
+    rows, width = qx.shape
+
+    def body(kl, vl, kr, vr, bias_ref, qx_ref, rx_ref, w_ref, a_ref, att_ref):
+        c, i = lax.axis_index("ctx"), lax.axis_index("tp")
+        k = jnp.concatenate((kl[...], kr[...]), axis=0)
+        v = jnp.concatenate((vl[...], vr[...]), axis=0)
+        att_ref[...] = attend(choose(c, i, rx_ref[...], qx_ref[...]), k, v, bias_ref[:rows])
+
+        def store(t, tile, part):
+            a_ref[:, t:t + tile] = part.astype(BF16)
+
+        product(att_ref[...], w_ref, 0, cols, store)
+
+    return kernel_call(
+        body,
+        (jax.ShapeDtypeStruct((rows, cols), BF16), jax.ShapeDtypeStruct((rows, width), BF16)),
+        [VMEM] * 8,
+        flops=2 * rows * width * cols,
+        moved=weight.size,
+    )(*kv, bias, qx, rx, weight)
 
 
 def first_part(att, weight, at, cols):
@@ -158,21 +173,26 @@
     return kernel_call(body, jax.ShapeDtypeStruct(own.shape, F32), [VMEM] * 2, moved=own.size * 10)(own, y)
 
 
-def finish(parts, embedded, arrived, at, out, hint):
+def finish(parts, embedded, arrived, at, out):
     rows, cols = arrived.shape
     n = len(parts)
+    step = cols // 2
 
     def body(*refs):
         e_ref, a_ref = refs[n:n + 2]
-        out_ref, done_ref, sem = refs[-3:]
-        resid = jnp.where(lax.axis_index("phase") == 0, e_ref[:, at:at + cols], a_ref[...])
-        total = resid.astype(F32)
-        for ref in refs[:n]:
-            total = total + ref[...].astype(F32)
-        done_ref[...] = total.astype(BF16)
-        copy = pltpu.make_async_copy(done_ref, out_ref.at[:, at:at + cols], sem)
-        copy.start()
-        copy.wait()
+        out_ref, done_ref, sems = refs[-3:]
+        first = lax.axis_index("phase") == 0
+        copies = []
+        for p in range(2):
+            a, b = p * step, (p + 1) * step
+            total = jnp.where(first, e_ref[:, at + a:at + b], a_ref[:, a:b]).astype(F32)
+            for ref in refs[:n]:
+                total = total + ref[:, a:b].astype(F32)
+            done_ref[:, a:b] = total.astype(BF16)
+            copies.append(pltpu.make_async_copy(done_ref.at[:, a:b], out_ref.at[:, at + a:at + b], sems.at[p]))
+            copies[-1].start()
+        for copy in copies:
+            copy.wait()
 
     before = () if out is None else (out,)
     return pl.pallas_call(
@@ -180,10 +200,10 @@
         out_shape=jax.ShapeDtypeStruct(embedded.shape, BF16),
         in_specs=[VMEM] * (n + 2) + [HBM] * len(before),
         out_specs=HBM,
-        scratch_shapes=[pltpu.VMEM((rows, cols), BF16), pltpu.SemaphoreType.DMA],
+        scratch_shapes=[pltpu.VMEM((rows, cols), BF16), pltpu.SemaphoreType.DMA((2,))],
         input_output_aliases={n + 2: 0} if before else {},
         compiler_params=pltpu.CompilerParams(vmem_limit_bytes=16 * 1024 * 1024),
-        cost_estimate=pl.CostEstimate(flops=hint, bytes_accessed=embedded.size * 4, transcendentals=0),
+        cost_estimate=pl.CostEstimate(flops=0, bytes_accessed=embedded.size * 4, transcendentals=0),
     )(*parts, embedded, arrived, *before)
 
 
@@ -211,7 +231,6 @@
     q = queries[0]
     rows = q.shape[0] // 2
     cols = out_weight.shape[1] // 2
-    near = NEAR * cols // 4
     k, v = keys[0], values[0]
     low = lax.axis_index("tp") & 1
     qx = lax.dynamic_slice_in_dim(q, (1 - low) * rows, rows)
@@ -220,24 +239,23 @@
     kr, vr = swap(after(k, qx), "ctx", 1), swap(after(v, qx), "ctx", 1)
     bias = mask(seg_ids, rows)
     kv = (k, v, kr, vr)
-    att = attend_blocks(kv, bias, qx, rx)
-    a0 = first_part(att, out_weight, 0, near)
+    a0, att = first_block(kv, bias, qx, rx, out_weight, cols)
     got0 = swap(a0, "tp", 1)
     ry = swap(after(qy, a0), "ctx", 1)
-    a1 = first_part(after(att, a0), out_weight, near, 2 * cols - near)
+    a1 = first_part(after(att, a0), out_weight, cols, cols)
     got1 = swap(a1, "tp", 1)
-    rest = attend_blocks(kv, bias, qx, rx, (qy, ry))
+    rest = other_blocks(kv, bias, qx, rx, qy, ry)
     m0, f0, own0 = other_parts(rest, out_weight, 0, got0, HOLD)
     gotm0 = swap(m0, "tp", 1)
     y0 = swap(f0, "tp", 2)
-    m1, f1, own1 = other_parts(rest, out_weight, near, got1, 0)
+    m1, f1, own1 = other_parts(rest, out_weight, cols, got1, 0)
     gotm1 = swap(m1, "tp", 1)
     y1 = swap(f1, "tp", 2)
     prev = after(hidden_prev, f1)[0]
     arrived = [passed_along(prev[:, at:at + cols], "phase", 1) for at in (0, cols)]
     sum0 = add_far(own0, y0)
-    out = finish((sum0, gotm0), embedded, arrived[0], 0, None, 0)
-    return finish((own1, y1, gotm1), embedded, arrived[1], cols, out, 0)[None]
+    out = finish((sum0, gotm0), embedded, arrived[0], 0, None)
+    return finish((own1, y1, gotm1), embedded, arrived[1], cols, out)[None]
 
 
 def on_device(queries, keys, values, seg_ids, out_weight, embedded, hidden_prev):
@@ -290,10 +308,14 @@
     return (resid_in.astype(jnp.float32) + summed).astype(jnp.bfloat16)[None]
 
 
+def on_any(queries, keys, *rest):
+    pair = lax.axis_size("ctx") == 2 and lax.axis_size("tp") == 4 and keys.shape[2] == HEAD_DIM
+    return (on_pair if pair else on_device)(queries, keys, *rest)
+
+
 def solution(mesh):
-    fast = mesh.shape["ctx"] == 2 and mesh.shape["tp"] == 4
     return jax.shard_map(
-        on_pair if fast else on_device,
+        on_any,
         mesh=mesh,
         in_specs=(
             P("phase", "ctx", "tp"),

time: 46.5 us -> 46.3 us (level)
    pallas_call x2 -> x1, Pallas kernels: 1.67 us -> 0.83 us  [first_part(): kernel_call(body, jax.ShapeDtypeStruct((rows, cols), BF16), [VMEM] * 2, f...]
    pallas_call x2, Pallas kernels: 1.26 us -> 1.94 us  [the longest x1 1.17 us: first_block(): kernel_call(body, (jax.ShapeDtypeStruct((rows, cols), BF16), jax.ShapeDty...]
where the time goes in v5:
time: 46.3 us; the launch traced here: 45.9 us
  starting transfers between devices  23.2 us (50%)
  waiting for transfers between devices  14 us (30%)
  Pallas kernels  6.59 us (14%)
  local copies, waits for them, and re-layouts  1.88 us (4%)
    ppermute x10, starting transfers between devices, swap(): return lax.ppermute(x, axis, [(i, i ^ by) for i in range(peers)])  18.1 us
    ppermute x10, waiting for transfers between devices, swap(): return lax.ppermute(x, axis, [(i, i ^ by) for i in range(peers)])  14 us
    ppermute x2, starting transfers between devices, passed_along(): return lax.ppermute(shard, axis, pairs)  5.13 us
    pallas_call x2, Pallas kernels, other_parts(): kernel_call(body, (part, part, jax.ShapeDtypeStruct((rows, cols), F32)),...  1.99 us
    pallas_call x2, Pallas kernels, finish(): pl.pallas_call(body, out_shape=jax.ShapeDtypeStruct(embedded.shape, BF16)...  1.57 us
    pallas_call x1, Pallas kernels, first_block(): kernel_call(body, (jax.ShapeDtypeStruct((rows, cols), BF16), jax.ShapeDty...  1.17 us
    dynamic_slice x1, local copies, waits for them, and re-layouts, on_pair(): qy = lax.dynamic_slice_in_dim(q, low * rows, rows)  1.13 us
  transfers between devices with their start and end apart: 12, of which 6 were waited for; matrix products, arithmetic and copies ran while one was open for 0% of the time, Pallas kernels for 10%

profile of v5, /device:TPU:0, one launch (start us, length us, event | category | flops | bytes accessed | tf_op | source)
XLA Modules:
  0.0 45.9 jit_solution(13039859188768648565)
XLA Ops:
  0.0 1.1 %dynamic-slice_bitcast_fusion = (bf16[64,1024]{1,0:T(8,128)(2,1)S(1)}, bf16[64,1024]{1,0:T(8,128)(2,1)S(1)}) fusion(bf16[1,128,1024]{2,1,0:T(8,128)(2,1)} %param.7, s32[]{:T(128)S(6)} %select_n.7, s32[]{:T(128)S(6)} %select_n.6), kind=kLoop, calls=%fused_computation | loop fusion | bytes 524296 | tf_op jit(solution)/shard_map/dynamic_slice | solution.py:237
  1.1 3.0 %collective-permute-start.2 = (bf16[64,1024]{1,0:T(8,128)(2,1)S(1)}, bf16[64,1024]{1,0:T(8,128)(2,1)S(1)}, u32[]{:S(2)}, u32[]{:S(2)}) collective-permute-start(bf16[64,1024]{1,0:T(8,128)(2,1)S(1)} %get-tuple-element.34.qx_ref), channel_id=1, source_target_pairs={{0,4},{4,0},{1,5},{5,1},{2,6},{6,2},{3,7},{7,3},{8,12},{12,8},{9,1... | collective-permute-start | bytes 393224 | tf_op jit(solution)/shard_map/ppermute | solution.py:212
  4.2 0.1 collective-permute-start
  4.3 1.9 %collective-permute-start.1 = (bf16[128,128]{1,0:T(8,128)(2,1)}, bf16[128,128]{1,0:T(8,128)(2,1)S(1)}, u32[]{:S(2)}, u32[]{:S(2)}) collective-permute-start(bf16[128,128]{1,0:T(8,128)(2,1)} %bitcast.11), channel_id=1, source_target_pairs={{0,4},{4,0},{1,5},{5,1},{2,6},{6,2},{3,7},{7,3},{8,12},{12,8},{9,1... | collective-permute-start | bytes 98312 | tf_op jit(solution)/shard_map/ppermute | solution.py:212
  6.2 0.7 %copy-done.4 = s32[1,256]{1,0:T(1,128)S(1)} copy-done((s32[1,256]{1,0:T(1,128)S(1)}, s32[1,256]{1,0:T(1,128)}, u32[]{:S(2)}) %copy-start.4) | copy-done | bytes 1048
  6.9 0.2 shard_map.73.bias_ref
  7.1 1.6 %collective-permute-done.kr = bf16[128,128]{1,0:T(8,128)(2,1)S(1)} collective-permute-done((bf16[128,128]{1,0:T(8,128)(2,1)}, bf16[128,128]{1,0:T(8,128)(2,1)S(1)}, u32[]{:S(2)}, u32[]{:S(2)}) %collective-permute-start) | collective-permute-done | bytes 32800 | tf_op jit(solution)/shard_map/ppermute | solution.py:212
  8.7 0.4 collective-permute-done.1.vr
  9.1 0.0 collective-permute-done.2.rx_ref
  9.1 1.2 %shard_map.74 = (bf16[64,2048]{1,0:T(8,128)(2,1)S(1)}, bf16[64,1024]{1,0:T(8,128)(2,1)S(1)}) custom-call(bf16[128,128]{1,0:T(8,128)(2,1)S(1)} %bitcast.9, bf16[128,128]{1,0:T(8,128)(2,1)S(1)} %bitcast.12, bf16[128,128]{1,0:T(8,128)(2,1)S(1)} %collective-permute-done.kr, bf16[128,128]{1,0:T(8,128)(2,1)S(1)} %collective-permute-done.1.vr, ...), custom_call_target="tpu_custom_call" | custom-call | flops 268435456 | bytes 4194304 | tf_op jit(solution)/shard_map/pallas_call | solution.py:120
  10.3 1.9 %collective-permute-start.8 = (bf16[64,2048]{1,0:T(8,128)(2,1)S(1)}, bf16[64,2048]{1,0:T(8,128)(2,1)S(1)}, u32[]{:S(2)}, u32[]{:S(2)}) collective-permute-start(bf16[64,2048]{1,0:T(8,128)(2,1)S(1)} %get-tuple-element.20), channel_id=1, source_target_pairs={{0,1},{1,0},{2,3},{3,2},{4,5},{5,4},{6,7},{7,6},{8,9},{9,8},{10,11... | collective-permute-start | bytes 786440 | tf_op jit(solution)/shard_map/ppermute | solution.py:212
  12.1 1.5 %collective-permute-start.3 = (bf16[64,1024]{1,0:T(8,128)(2,1)S(1)}, bf16[64,1024]{1,0:T(8,128)(2,1)S(1)}, u32[]{:S(2)}, u32[]{:S(2)}) collective-permute-start(bf16[64,1024]{1,0:T(8,128)(2,1)S(1)} %get-tuple-element.21.qy_ref), channel_id=1, source_target_pairs={{0,4},{4,0},{1,5},{5,1},{2,6},{6,2},{3,7},{7,3},{8,12},{12,8},{9,1... | collective-permute-start | bytes 393224 | tf_op jit(solution)/shard_map/ppermute | solution.py:212
  13.7 0.8 %shard_map.76 = bf16[64,2048]{1,0:T(8,128)(2,1)S(1)} custom-call(bf16[64,1024]{1,0:T(8,128)(2,1)S(1)} %get-tuple-element.23.att_ref, bf16[1024,4096]{1,0:T(8,128)(2,1)S(1)} %copy-done), custom_call_target="tpu_custom_call" | custom-call | flops 268435456 | bytes 4194304 | tf_op jit(solution)/shard_map/pallas_call | solution.py:138
  14.5 0.5 %collective-permute-start.4 = (bf16[64,2048]{1,0:T(8,128)(2,1)S(1)}, bf16[64,2048]{1,0:T(8,128)(2,1)S(1)}, u32[]{:S(2)}, u32[]{:S(2)}) collective-permute-start(bf16[64,2048]{1,0:T(8,128)(2,1)S(1)} %shard_map.76), channel_id=1, source_target_pairs={{0,1},{1,0},{2,3},{3,2},{4,5},{5,4},{6,7},{7,6},{8,9},{9,8},{10,11... | collective-permute-start | bytes 786440 | tf_op jit(solution)/shard_map/ppermute | solution.py:212
  15.0 2.1 %collective-permute-done.3.ry_ref = bf16[64,1024]{1,0:T(8,128)(2,1)S(1)} collective-permute-done((bf16[64,1024]{1,0:T(8,128)(2,1)S(1)}, bf16[64,1024]{1,0:T(8,128)(2,1)S(1)}, u32[]{:S(2)}, u32[]{:S(2)}) %collective-permute-start.3) | collective-permute-done | bytes 131104 | tf_op jit(solution)/shard_map/ppermute | solution.py:212
  17.1 0.8 %shard_map.75.att_ref = bf16[192,1024]{1,0:T(8,128)(2,1)S(1)} custom-call(bf16[128,128]{1,0:T(8,128)(2,1)S(1)} %bitcast.10, bf16[128,128]{1,0:T(8,128)(2,1)S(1)} %bitcast.13, bf16[128,128]{1,0:T(8,128)(2,1)S(1)} %collective-permute-done.kr, bf16[128,128]{1,0:T(8,128)(2,1)S(1)} %collective-permute-done.1.vr, f32[256,256]{1,0:T(8,128)S(1)} %shard_map.73.bias_ref, ...), custom_call_target="tpu_custom_call" | custom-call | bytes 262144 | tf_op jit(solution)/shard_map/pallas_call | solution.py:98
  17.9 1.7 %collective-permute-done.8.got_ref = bf16[64,2048]{1,0:T(8,128)(2,1)S(1)} collective-permute-done((bf16[64,2048]{1,0:T(8,128)(2,1)S(1)}, bf16[64,2048]{1,0:T(8,128)(2,1)S(1)}, u32[]{:S(2)}, u32[]{:S(2)}) %collective-permute-start.8) | collective-permute-done | bytes 262176 | tf_op jit(solution)/shard_map/ppermute | solution.py:212
  19.6 1.0 %shard_map.78 = (bf16[64,2048]{1,0:T(8,128)(2,1)S(1)}, bf16[64,2048]{1,0:T(8,128)(2,1)S(1)}, f32[64,2048]{1,0:T(8,128)S(1)}) custom-call(bf16[192,1024]{1,0:T(8,128)(2,1)S(1)} %shard_map.75.att_ref, bf16[1024,4096]{1,0:T(8,128)(2,1)S(1)} %copy-done, bf16[64,2048]{1,0:T(8,128)(2,1)S(1)} %collective-permute-done.8.got_ref), custom_call_target="tpu_custom_call" | custom-call | flops 5000000000 | bytes 4194304 | tf_op jit(solution)/shard_map/pallas_call | solution.py:160
  20.6 0.0 copy-start.5
  20.6 0.0 copy-start.1
  20.6 2.9 %collective-permute-start.9 = (bf16[64,2048]{1,0:T(8,128)(2,1)S(1)}, bf16[64,2048]{1,0:T(8,128)(2,1)S(1)}, u32[]{:S(2)}, u32[]{:S(2)}) collective-permute-start(bf16[64,2048]{1,0:T(8,128)(2,1)S(1)} %get-tuple-element.29), channel_id=1, source_target_pairs={{0,2},{1,3},{2,0},{3,1},{4,6},{5,7},{6,4},{7,5},{8,10},{9,11},{10,... | collective-permute-start | bytes 786440 | tf_op jit(solution)/shard_map/ppermute | solution.py:212
  23.5 1.6 %collective-permute-start.10 = (bf16[64,2048]{1,0:T(8,128)(2,1)S(1)}, bf16[64,2048]{1,0:T(8,128)(2,1)S(1)}, u32[]{:S(2)}, u32[]{:S(2)}) collective-permute-start(bf16[64,2048]{1,0:T(8,128)(2,1)S(1)} %get-tuple-element.30), channel_id=1, source_target_pairs={{0,1},{1,0},{2,3},{3,2},{4,5},{5,4},{6,7},{7,6},{8,9},{9,8},{10,11... | collective-permute-start | bytes 786440 | tf_op jit(solution)/shard_map/ppermute | solution.py:212
  25.1 4.4 %collective-permute-done.4.got_ref = bf16[64,2048]{1,0:T(8,128)(2,1)S(1)} collective-permute-done((bf16[64,2048]{1,0:T(8,128)(2,1)S(1)}, bf16[64,2048]{1,0:T(8,128)(2,1)S(1)}, u32[]{:S(2)}, u32[]{:S(2)}) %collective-permute-start.4) | collective-permute-done | bytes 262176 | tf_op jit(solution)/shard_map/ppermute | solution.py:212
  29.5 1.0 %shard_map.77 = (bf16[64,2048]{1,0:T(8,128)(2,1)S(1)}, bf16[64,2048]{1,0:T(8,128)(2,1)S(1)}, f32[64,2048]{1,0:T(8,128)S(1)}) custom-call(bf16[192,1024]{1,0:T(8,128)(2,1)S(1)} %shard_map.75.att_ref, bf16[1024,4096]{1,0:T(8,128)(2,1)S(1)} %copy-done, bf16[64,2048]{1,0:T(8,128)(2,1)S(1)} %collective-permute-done.4.got_ref), custom_call_target="tpu_custom_call" | custom-call | bytes 4194304 | tf_op jit(solution)/shard_map/pallas_call | solution.py:160
  30.5 1.6 %collective-permute-start.5 = (bf16[64,2048]{1,0:T(8,128)(2,1)S(1)}, bf16[64,2048]{1,0:T(8,128)(2,1)S(1)}, u32[]{:S(2)}, u32[]{:S(2)}) collective-permute-start(bf16[64,2048]{1,0:T(8,128)(2,1)S(1)} %get-tuple-element.25), channel_id=1, source_target_pairs={{0,2},{1,3},{2,0},{3,1},{4,6},{5,7},{6,4},{7,5},{8,10},{9,11},{10,... | collective-permute-start | bytes 786440 | tf_op jit(solution)/shard_map/ppermute | solution.py:212
  32.2 1.3 %collective-permute-start.11 = (bf16[64,2048]{1,0:T(8,128)(2,1)S(1)}, bf16[64,2048]{1,0:T(8,128)(2,1)S(1)}, u32[]{:S(2)}, u32[]{:S(2)}) collective-permute-start(bf16[64,2048]{1,0:T(8,128)(2,1)S(1)} %get-tuple-element.31), channel_id=1, source_target_pairs={{0,8},{8,16},{16,24},{1,9},{9,17},{17,25},{2,10},{10,18},{18,26},{... | collective-permute-start | bytes 786440 | tf_op jit(solution)/shard_map/ppermute | solution.py:222
  33.5 3.0 %collective-permute-start.6 = (bf16[64,2048]{1,0:T(8,128)(2,1)S(1)}, bf16[64,2048]{1,0:T(8,128)(2,1)S(1)}, u32[]{:S(2)}, u32[]{:S(2)}) collective-permute-start(bf16[64,2048]{1,0:T(8,128)(2,1)S(1)} %get-tuple-element.26), channel_id=1, source_target_pairs={{0,1},{1,0},{2,3},{3,2},{4,5},{5,4},{6,7},{7,6},{8,9},{9,8},{10,11... | collective-permute-start | bytes 786440 | tf_op jit(solution)/shard_map/ppermute | solution.py:212
  36.5 3.8 %collective-permute-start.7 = (bf16[64,2048]{1,0:T(8,128)(2,1)S(1)}, bf16[64,2048]{1,0:T(8,128)(2,1)S(1)}, u32[]{:S(2)}, u32[]{:S(2)}) collective-permute-start(bf16[64,2048]{1,0:T(8,128)(2,1)S(1)} %get-tuple-element.32), channel_id=1, source_target_pairs={{0,8},{8,16},{16,24},{1,9},{9,17},{17,25},{2,10},{10,18},{18,26},{... | collective-permute-start | bytes 786440 | tf_op jit(solution)/shard_map/ppermute | solution.py:222
  40.4 0.0 collective-permute-done.11.refs_3_
  40.4 0.8 %shard_map.80.refs_5_ = bf16[64,4096]{1,0:T(8,128)(2,1)} custom-call(f32[64,2048]{1,0:T(8,128)S(1)} %shard_map.79.refs_0_, bf16[64,2048]{1,0:T(8,128)(2,1)S(1)} %collective-permute-done.10.refs_1_, bf16[64,4096]{1,0:T(8,128)(2,1)S(1)} %copy-done.1, bf16[64,2048]{1,0:T(8,128)(2,1)S(1)} %collective-permute-done.11.refs_3_), custom_call_target="tpu_custom_call" | custom-call | bytes 1048576 | tf_op jit(solution)/shard_map/pallas_call | solution.py:198
  41.2 3.9 %collective-permute-done.6.refs_2_ = bf16[64,2048]{1,0:T(8,128)(2,1)S(1)} collective-permute-done((bf16[64,2048]{1,0:T(8,128)(2,1)S(1)}, bf16[64,2048]{1,0:T(8,128)(2,1)S(1)}, u32[]{:S(2)}, u32[]{:S(2)}) %collective-permute-start.6) | collective-permute-done | bytes 262176 | tf_op jit(solution)/shard_map/ppermute | solution.py:212
  45.1 0.8 %shard_map.81 = bf16[64,4096]{1,0:T(8,128)(2,1)} custom-call(f32[64,2048]{1,0:T(8,128)S(1)} %get-tuple-element.24.refs_0_, bf16[64,2048]{1,0:T(8,128)(2,1)S(1)} %collective-permute-done.5.refs_1_, bf16[64,2048]{1,0:T(8,128)(2,1)S(1)} %collective-permute-done.6.refs_2_, bf16[64,4096]{1,0:T(8,128)(2,1)S(1)} %copy-done.1, ...), custom_call_target="tpu_custom_call", output_to_operand_aliasing={{}: (5, {})} | custom-call | bytes 1048576 | tf_op jit(solution)/shard_map/pallas_call | solution.py:198
  (15 shorter events, 0.1 us)
Async XLA Ops:
  0.0 9.1 %copy-start.2 = (bf16[1,128,128]{2,1,0:T(8,128)(2,1)S(1)}, bf16[1,128,128]{2,1,0:T(8,128)(2,1)}, u32[]{:S(2)}) copy-start(bf16[1,128,128]{2,1,0:T(8,128)(2,1)} %param.8) | copy-start | bytes 98308
  0.0 9.1 %copy-start.3 = (bf16[1,128,128]{2,1,0:T(8,128)(2,1)S(1)}, bf16[1,128,128]{2,1,0:T(8,128)(2,1)}, u32[]{:S(2)}) copy-start(bf16[1,128,128]{2,1,0:T(8,128)(2,1)} %param.9) | copy-start | bytes 98308
  0.0 9.1 %copy-start = (bf16[1024,4096]{1,0:T(8,128)(2,1)S(1)}, bf16[1024,4096]{1,0:T(8,128)(2,1)}, u32[]{:S(2)}) copy-start(bf16[1024,4096]{1,0:T(8,128)(2,1)} %w_ref.7) | copy-start | bytes 25165828
  1.1 7.9 %collective-permute-start.2 = (bf16[64,1024]{1,0:T(8,128)(2,1)S(1)}, bf16[64,1024]{1,0:T(8,128)(2,1)S(1)}, u32[]{:S(2)}, u32[]{:S(2)}) collective-permute-start(bf16[64,1024]{1,0:T(8,128)(2,1)S(1)} %get-tuple-element.34.qx_ref), channel_id=1, source_target_pairs={{0,4},{4,0},{1,5},{5,1},{2,6},{6,2},{3,7},{7,3},{8,12},{12,8},{9,1... | collective-permute-start | bytes 393224 | tf_op jit(solution)/shard_map/ppermute | solution.py:212
  4.2 4.5 %collective-permute-start = (bf16[128,128]{1,0:T(8,128)(2,1)}, bf16[128,128]{1,0:T(8,128)(2,1)S(1)}, u32[]{:S(2)}, u32[]{:S(2)}) collective-permute-start(bf16[128,128]{1,0:T(8,128)(2,1)} %bitcast.8), channel_id=1, source_target_pairs={{0,4},{4,0},{1,5},{5,1},{2,6},{6,2},{3,7},{7,3},{8,12},{12,8},{9,1... | collective-permute-start | bytes 98312 | tf_op jit(solution)/shard_map/ppermute | solution.py:212
  4.3 4.8 %collective-permute-start.1 = (bf16[128,128]{1,0:T(8,128)(2,1)}, bf16[128,128]{1,0:T(8,128)(2,1)S(1)}, u32[]{:S(2)}, u32[]{:S(2)}) collective-permute-start(bf16[128,128]{1,0:T(8,128)(2,1)} %bitcast.11), channel_id=1, source_target_pairs={{0,4},{4,0},{1,5},{5,1},{2,6},{6,2},{3,7},{7,3},{8,12},{12,8},{9,1... | collective-permute-start | bytes 98312 | tf_op jit(solution)/shard_map/ppermute | solution.py:212
  6.2 0.7 %copy-start.4 = (s32[1,256]{1,0:T(1,128)S(1)}, s32[1,256]{1,0:T(1,128)}, u32[]{:S(2)}) copy-start(s32[1,256]{1,0:T(1,128)} %seg_ref.1) | copy-start | bytes 3076
  10.3 9.3 %collective-permute-start.8 = (bf16[64,2048]{1,0:T(8,128)(2,1)S(1)}, bf16[64,2048]{1,0:T(8,128)(2,1)S(1)}, u32[]{:S(2)}, u32[]{:S(2)}) collective-permute-start(bf16[64,2048]{1,0:T(8,128)(2,1)S(1)} %get-tuple-element.20), channel_id=1, source_target_pairs={{0,1},{1,0},{2,3},{3,2},{4,5},{5,4},{6,7},{7,6},{8,9},{9,8},{10,11... | collective-permute-start | bytes 786440 | tf_op jit(solution)/shard_map/ppermute | solution.py:212
  12.1 5.0 %collective-permute-start.3 = (bf16[64,1024]{1,0:T(8,128)(2,1)S(1)}, bf16[64,1024]{1,0:T(8,128)(2,1)S(1)}, u32[]{:S(2)}, u32[]{:S(2)}) collective-permute-start(bf16[64,1024]{1,0:T(8,128)(2,1)S(1)} %get-tuple-element.21.qy_ref), channel_id=1, source_target_pairs={{0,4},{4,0},{1,5},{5,1},{2,6},{6,2},{3,7},{7,3},{8,12},{12,8},{9,1... | collective-permute-start | bytes 393224 | tf_op jit(solution)/shard_map/ppermute | solution.py:212
  14.5 14.9 %collective-permute-start.4 = (bf16[64,2048]{1,0:T(8,128)(2,1)S(1)}, bf16[64,2048]{1,0:T(8,128)(2,1)S(1)}, u32[]{:S(2)}, u32[]{:S(2)}) collective-permute-start(bf16[64,2048]{1,0:T(8,128)(2,1)S(1)} %shard_map.76), channel_id=1, source_target_pairs={{0,1},{1,0},{2,3},{3,2},{4,5},{5,4},{6,7},{7,6},{8,9},{9,8},{10,11... | collective-permute-start | bytes 786440 | tf_op jit(solution)/shard_map/ppermute | solution.py:212
  20.6 11.5 %copy-start.5 = (bf16[1,64,4096]{2,1,0:T(8,128)(2,1)S(1)}, bf16[1,64,4096]{2,1,0:T(8,128)(2,1)}, u32[]{:S(2)}) copy-start(bf16[1,64,4096]{2,1,0:T(8,128)(2,1)} %param.13) | copy-start | bytes 1572868
  20.6 19.8 %copy-start.1 = (bf16[64,4096]{1,0:T(8,128)(2,1)S(1)}, bf16[64,4096]{1,0:T(8,128)(2,1)}, u32[]{:S(2)}) copy-start(bf16[64,4096]{1,0:T(8,128)(2,1)} %refs_3_.1) | copy-start | bytes 1572868
  20.6 15.9 %collective-permute-start.9 = (bf16[64,2048]{1,0:T(8,128)(2,1)S(1)}, bf16[64,2048]{1,0:T(8,128)(2,1)S(1)}, u32[]{:S(2)}, u32[]{:S(2)}) collective-permute-start(bf16[64,2048]{1,0:T(8,128)(2,1)S(1)} %get-tuple-element.29), channel_id=1, source_target_pairs={{0,2},{1,3},{2,0},{3,1},{4,6},{5,7},{6,4},{7,5},{8,10},{9,11},{10,... | collective-permute-start | bytes 786440 | tf_op jit(solution)/shard_map/ppermute | solution.py:212
  23.5 16.9 %collective-permute-start.10 = (bf16[64,2048]{1,0:T(8,128)(2,1)S(1)}, bf16[64,2048]{1,0:T(8,128)(2,1)S(1)}, u32[]{:S(2)}, u32[]{:S(2)}) collective-permute-start(bf16[64,2048]{1,0:T(8,128)(2,1)S(1)} %get-tuple-element.30), channel_id=1, source_target_pairs={{0,1},{1,0},{2,3},{3,2},{4,5},{5,4},{6,7},{7,6},{8,9},{9,8},{10,11... | collective-permute-start | bytes 786440 | tf_op jit(solution)/shard_map/ppermute | solution.py:212
  30.5 14.6 %collective-permute-start.5 = (bf16[64,2048]{1,0:T(8,128)(2,1)S(1)}, bf16[64,2048]{1,0:T(8,128)(2,1)S(1)}, u32[]{:S(2)}, u32[]{:S(2)}) collective-permute-start(bf16[64,2048]{1,0:T(8,128)(2,1)S(1)} %get-tuple-element.25), channel_id=1, source_target_pairs={{0,2},{1,3},{2,0},{3,1},{4,6},{5,7},{6,4},{7,5},{8,10},{9,11},{10,... | collective-permute-start | bytes 786440 | tf_op jit(solution)/shard_map/ppermute | solution.py:212
  32.2 8.3 %collective-permute-start.11 = (bf16[64,2048]{1,0:T(8,128)(2,1)S(1)}, bf16[64,2048]{1,0:T(8,128)(2,1)S(1)}, u32[]{:S(2)}, u32[]{:S(2)}) collective-permute-start(bf16[64,2048]{1,0:T(8,128)(2,1)S(1)} %get-tuple-element.31), channel_id=1, source_target_pairs={{0,8},{8,16},{16,24},{1,9},{9,17},{17,25},{2,10},{10,18},{18,26},{... | collective-permute-start | bytes 786440 | tf_op jit(solution)/shard_map/ppermute | solution.py:222
  33.5 11.6 %collective-permute-start.6 = (bf16[64,2048]{1,0:T(8,128)(2,1)S(1)}, bf16[64,2048]{1,0:T(8,128)(2,1)S(1)}, u32[]{:S(2)}, u32[]{:S(2)}) collective-permute-start(bf16[64,2048]{1,0:T(8,128)(2,1)S(1)} %get-tuple-element.26), channel_id=1, source_target_pairs={{0,1},{1,0},{2,3},{3,2},{4,5},{5,4},{6,7},{7,6},{8,9},{9,8},{10,11... | collective-permute-start | bytes 786440 | tf_op jit(solution)/shard_map/ppermute | solution.py:212
  36.5 8.6 %collective-permute-start.7 = (bf16[64,2048]{1,0:T(8,128)(2,1)S(1)}, bf16[64,2048]{1,0:T(8,128)(2,1)S(1)}, u32[]{:S(2)}, u32[]{:S(2)}) collective-permute-start(bf16[64,2048]{1,0:T(8,128)(2,1)S(1)} %get-tuple-element.32), channel_id=1, source_target_pairs={{0,8},{8,16},{16,24},{1,9},{9,17},{17,25},{2,10},{10,18},{18,26},{... | collective-permute-start | bytes 786440 | tf_op jit(solution)/shard_map/ppermute | solution.py:222

commit v6 on v5

--- a/solution.py
+++ b/solution.py
@@ -7,7 +7,7 @@
 
 HEAD_DIM = 128
 NEG = -1e30
-LONG = 3 * 10**9
+LONG = 6 * 10**9
 HOLD = 5 * 10**9
 VMEM = pl.BlockSpec(memory_space=pltpu.VMEM)
 HBM = pl.BlockSpec(memory_space=pltpu.HBM)

time: 46.3 us -> 46.1 us (level)
  waiting for transfers between devices: 14 us -> 13.5 us
    ppermute x10, waiting for transfers between devices: 14 us -> 13.5 us  [swap(): return lax.ppermute(x, axis, [(i, i ^ by) for i in range(peers)])]
    unnamed x12 -> x14, local copies, waits for them, and re-layouts: 0.7 us -> 1.17 us
where the time goes in v6:
time: 46.1 us; the launch traced here: 45.7 us
  starting transfers between devices  23.3 us (51%)
  waiting for transfers between devices  13.5 us (29%)
  Pallas kernels  6.59 us (14%)
  local copies, waits for them, and re-layouts  2.19 us (5%)
    ppermute x10, starting transfers between devices, swap(): return lax.ppermute(x, axis, [(i, i ^ by) for i in range(peers)])  18.1 us
    ppermute x10, waiting for transfers between devices, swap(): return lax.ppermute(x, axis, [(i, i ^ by) for i in range(peers)])  13.5 us
    ppermute x2, starting transfers between devices, passed_along(): return lax.ppermute(shard, axis, pairs)  5.17 us
    pallas_call x2, Pallas kernels, other_parts(): kernel_call(body, (part, part, jax.ShapeDtypeStruct((rows, cols), F32)),...  1.99 us
    pallas_call x2, Pallas kernels, finish(): pl.pallas_call(body, out_shape=jax.ShapeDtypeStruct(embedded.shape, BF16)...  1.57 us
    pallas_call x1, Pallas kernels, first_block(): kernel_call(body, (jax.ShapeDtypeStruct((rows, cols), BF16), jax.ShapeDty...  1.17 us
    unnamed x14, local copies, waits for them, and re-layouts  1.17 us
    dynamic_slice x1, local copies, waits for them, and re-layouts, on_pair(): qy = lax.dynamic_slice_in_dim(q, low * rows, rows)  0.98 us
  transfers between devices with their start and end apart: 12, of which 6 were waited for; matrix products, arithmetic and copies ran while one was open for 0% of the time, Pallas kernels for 10%

profile of v6, /device:TPU:0, one launch (start us, length us, event | category | flops | bytes accessed | tf_op | source)
XLA Modules:
  0.0 45.7 jit_solution(16992212123154455420)
XLA Ops:
  0.0 1.0 %dynamic-slice_bitcast_fusion = (bf16[64,1024]{1,0:T(8,128)(2,1)S(1)}, bf16[64,1024]{1,0:T(8,128)(2,1)S(1)}) fusion(bf16[1,128,1024]{2,1,0:T(8,128)(2,1)} %param.7, s32[]{:T(128)S(6)} %select_n.7, s32[]{:T(128)S(6)} %select_n.6), kind=kLoop, calls=%fused_computation | loop fusion | bytes 524296 | tf_op jit(solution)/shard_map/dynamic_slice | solution.py:237
  1.0 3.0 %collective-permute-start.2 = (bf16[64,1024]{1,0:T(8,128)(2,1)S(1)}, bf16[64,1024]{1,0:T(8,128)(2,1)S(1)}, u32[]{:S(2)}, u32[]{:S(2)}) collective-permute-start(bf16[64,1024]{1,0:T(8,128)(2,1)S(1)} %get-tuple-element.34.qx_ref), channel_id=1, source_target_pairs={{0,4},{4,0},{1,5},{5,1},{2,6},{6,2},{3,7},{7,3},{8,12},{12,8},{9,1... | collective-permute-start | bytes 393224 | tf_op jit(solution)/shard_map/ppermute | solution.py:212
  4.0 0.1 collective-permute-start
  4.1 2.0 %collective-permute-start.1 = (bf16[128,128]{1,0:T(8,128)(2,1)}, bf16[128,128]{1,0:T(8,128)(2,1)S(1)}, u32[]{:S(2)}, u32[]{:S(2)}) collective-permute-start(bf16[128,128]{1,0:T(8,128)(2,1)} %bitcast.13), channel_id=1, source_target_pairs={{0,4},{4,0},{1,5},{5,1},{2,6},{6,2},{3,7},{7,3},{8,12},{12,8},{9,1... | collective-permute-start | bytes 98312 | tf_op jit(solution)/shard_map/ppermute | solution.py:212
  6.1 1.1 %copy-done.3 = s32[1,256]{1,0:T(1,128)S(1)} copy-done((s32[1,256]{1,0:T(1,128)S(1)}, s32[1,256]{1,0:T(1,128)}, u32[]{:S(2)}) %copy-start.3) | copy-done | bytes 1048
  7.3 0.2 shard_map.73.bias_ref
  7.5 1.1 %collective-permute-done.kr = bf16[128,128]{1,0:T(8,128)(2,1)S(1)} collective-permute-done((bf16[128,128]{1,0:T(8,128)(2,1)}, bf16[128,128]{1,0:T(8,128)(2,1)S(1)}, u32[]{:S(2)}, u32[]{:S(2)}) %collective-permute-start) | collective-permute-done | bytes 32800 | tf_op jit(solution)/shard_map/ppermute | solution.py:212
  8.6 0.4 collective-permute-done.1.vr
  9.0 1.2 %shard_map.74 = (bf16[64,2048]{1,0:T(8,128)(2,1)S(1)}, bf16[64,1024]{1,0:T(8,128)(2,1)S(1)}) custom-call(bf16[128,128]{1,0:T(8,128)(2,1)S(1)} %bitcast.11, bf16[128,128]{1,0:T(8,128)(2,1)S(1)} %bitcast.14, bf16[128,128]{1,0:T(8,128)(2,1)S(1)} %collective-permute-done.kr, bf16[128,128]{1,0:T(8,128)(2,1)S(1)} %collective-permute-done.1.vr, ...), custom_call_target="tpu_custom_call" | custom-call | flops 268435456 | bytes 4194304 | tf_op jit(solution)/shard_map/pallas_call | solution.py:120
  10.1 1.9 %collective-permute-start.8 = (bf16[64,2048]{1,0:T(8,128)(2,1)S(1)}, bf16[64,2048]{1,0:T(8,128)(2,1)S(1)}, u32[]{:S(2)}, u32[]{:S(2)}) collective-permute-start(bf16[64,2048]{1,0:T(8,128)(2,1)S(1)} %get-tuple-element.20), channel_id=1, source_target_pairs={{0,1},{1,0},{2,3},{3,2},{4,5},{5,4},{6,7},{7,6},{8,9},{9,8},{10,11... | collective-permute-start | bytes 786440 | tf_op jit(solution)/shard_map/ppermute | solution.py:212
  12.0 1.5 %collective-permute-start.3 = (bf16[64,1024]{1,0:T(8,128)(2,1)S(1)}, bf16[64,1024]{1,0:T(8,128)(2,1)S(1)}, u32[]{:S(2)}, u32[]{:S(2)}) collective-permute-start(bf16[64,1024]{1,0:T(8,128)(2,1)S(1)} %get-tuple-element.21.qy_ref), channel_id=1, source_target_pairs={{0,4},{4,0},{1,5},{5,1},{2,6},{6,2},{3,7},{7,3},{8,12},{12,8},{9,1... | collective-permute-start | bytes 393224 | tf_op jit(solution)/shard_map/ppermute | solution.py:212
  13.5 0.8 %shard_map.76 = bf16[64,2048]{1,0:T(8,128)(2,1)S(1)} custom-call(bf16[64,1024]{1,0:T(8,128)(2,1)S(1)} %get-tuple-element.23.att_ref, bf16[1024,4096]{1,0:T(8,128)(2,1)S(1)} %bitcast.9), custom_call_target="tpu_custom_call" | custom-call | flops 268435456 | bytes 4194304 | tf_op jit(solution)/shard_map/pallas_call | solution.py:138
  14.4 0.5 %collective-permute-start.4 = (bf16[64,2048]{1,0:T(8,128)(2,1)S(1)}, bf16[64,2048]{1,0:T(8,128)(2,1)S(1)}, u32[]{:S(2)}, u32[]{:S(2)}) collective-permute-start(bf16[64,2048]{1,0:T(8,128)(2,1)S(1)} %shard_map.76), channel_id=1, source_target_pairs={{0,1},{1,0},{2,3},{3,2},{4,5},{5,4},{6,7},{7,6},{8,9},{9,8},{10,11... | collective-permute-start | bytes 786440 | tf_op jit(solution)/shard_map/ppermute | solution.py:212
  14.9 2.1 %collective-permute-done.3.ry_ref = bf16[64,1024]{1,0:T(8,128)(2,1)S(1)} collective-permute-done((bf16[64,1024]{1,0:T(8,128)(2,1)S(1)}, bf16[64,1024]{1,0:T(8,128)(2,1)S(1)}, u32[]{:S(2)}, u32[]{:S(2)}) %collective-permute-start.3) | collective-permute-done | bytes 131104 | tf_op jit(solution)/shard_map/ppermute | solution.py:212
  17.0 0.8 %shard_map.75.att_ref = bf16[192,1024]{1,0:T(8,128)(2,1)S(1)} custom-call(bf16[128,128]{1,0:T(8,128)(2,1)S(1)} %bitcast.12, bf16[128,128]{1,0:T(8,128)(2,1)S(1)} %bitcast.15, bf16[128,128]{1,0:T(8,128)(2,1)S(1)} %collective-permute-done.kr, bf16[128,128]{1,0:T(8,128)(2,1)S(1)} %collective-permute-done.1.vr, f32[256,256]{1,0:T(8,128)S(1)} %shard_map.73.bias_ref, ...), custom_call_target="tpu_custom_call" | custom-call | bytes 262144 | tf_op jit(solution)/shard_map/pallas_call | solution.py:98
  17.8 1.7 %collective-permute-done.8.got_ref = bf16[64,2048]{1,0:T(8,128)(2,1)S(1)} collective-permute-done((bf16[64,2048]{1,0:T(8,128)(2,1)S(1)}, bf16[64,2048]{1,0:T(8,128)(2,1)S(1)}, u32[]{:S(2)}, u32[]{:S(2)}) %collective-permute-start.8) | collective-permute-done | bytes 262176 | tf_op jit(solution)/shard_map/ppermute | solution.py:212
  19.4 1.0 %shard_map.78 = (bf16[64,2048]{1,0:T(8,128)(2,1)S(1)}, bf16[64,2048]{1,0:T(8,128)(2,1)S(1)}, f32[64,2048]{1,0:T(8,128)S(1)}) custom-call(bf16[192,1024]{1,0:T(8,128)(2,1)S(1)} %shard_map.75.att_ref, bf16[1024,4096]{1,0:T(8,128)(2,1)S(1)} %bitcast.9, bf16[64,2048]{1,0:T(8,128)(2,1)S(1)} %collective-permute-done.8.got_ref), custom_call_target="tpu_custom_call" | custom-call | flops 5000000000 | bytes 4194304 | tf_op jit(solution)/shard_map/pallas_call | solution.py:160
  20.4 0.0 copy-start.4
  20.5 0.0 copy-start
  20.5 2.9 %collective-permute-start.9 = (bf16[64,2048]{1,0:T(8,128)(2,1)S(1)}, bf16[64,2048]{1,0:T(8,128)(2,1)S(1)}, u32[]{:S(2)}, u32[]{:S(2)}) collective-permute-start(bf16[64,2048]{1,0:T(8,128)(2,1)S(1)} %get-tuple-element.29), channel_id=1, source_target_pairs={{0,2},{1,3},{2,0},{3,1},{4,6},{5,7},{6,4},{7,5},{8,10},{9,11},{10,... | collective-permute-start | bytes 786440 | tf_op jit(solution)/shard_map/ppermute | solution.py:212
  23.3 1.6 %collective-permute-start.10 = (bf16[64,2048]{1,0:T(8,128)(2,1)S(1)}, bf16[64,2048]{1,0:T(8,128)(2,1)S(1)}, u32[]{:S(2)}, u32[]{:S(2)}) collective-permute-start(bf16[64,2048]{1,0:T(8,128)(2,1)S(1)} %get-tuple-element.30), channel_id=1, source_target_pairs={{0,1},{1,0},{2,3},{3,2},{4,5},{5,4},{6,7},{7,6},{8,9},{9,8},{10,11... | collective-permute-start | bytes 786440 | tf_op jit(solution)/shard_map/ppermute | solution.py:212
  24.9 4.4 %collective-permute-done.4.got_ref = bf16[64,2048]{1,0:T(8,128)(2,1)S(1)} collective-permute-done((bf16[64,2048]{1,0:T(8,128)(2,1)S(1)}, bf16[64,2048]{1,0:T(8,128)(2,1)S(1)}, u32[]{:S(2)}, u32[]{:S(2)}) %collective-permute-start.4) | collective-permute-done | bytes 262176 | tf_op jit(solution)/shard_map/ppermute | solution.py:212
  29.3 1.0 %shard_map.77 = (bf16[64,2048]{1,0:T(8,128)(2,1)S(1)}, bf16[64,2048]{1,0:T(8,128)(2,1)S(1)}, f32[64,2048]{1,0:T(8,128)S(1)}) custom-call(bf16[192,1024]{1,0:T(8,128)(2,1)S(1)} %shard_map.75.att_ref, bf16[1024,4096]{1,0:T(8,128)(2,1)S(1)} %bitcast.9, bf16[64,2048]{1,0:T(8,128)(2,1)S(1)} %collective-permute-done.4.got_ref), custom_call_target="tpu_custom_call" | custom-call | bytes 4194304 | tf_op jit(solution)/shard_map/pallas_call | solution.py:160
  30.3 1.6 %collective-permute-start.5 = (bf16[64,2048]{1,0:T(8,128)(2,1)S(1)}, bf16[64,2048]{1,0:T(8,128)(2,1)S(1)}, u32[]{:S(2)}, u32[]{:S(2)}) collective-permute-start(bf16[64,2048]{1,0:T(8,128)(2,1)S(1)} %get-tuple-element.25), channel_id=1, source_target_pairs={{0,2},{1,3},{2,0},{3,1},{4,6},{5,7},{6,4},{7,5},{8,10},{9,11},{10,... | collective-permute-start | bytes 786440 | tf_op jit(solution)/shard_map/ppermute | solution.py:212
  32.0 1.3 %collective-permute-start.11 = (bf16[64,2048]{1,0:T(8,128)(2,1)S(1)}, bf16[64,2048]{1,0:T(8,128)(2,1)S(1)}, u32[]{:S(2)}, u32[]{:S(2)}) collective-permute-start(bf16[64,2048]{1,0:T(8,128)(2,1)S(1)} %get-tuple-element.31), channel_id=1, source_target_pairs={{0,8},{8,16},{16,24},{1,9},{9,17},{17,25},{2,10},{10,18},{18,26},{... | collective-permute-start | bytes 786440 | tf_op jit(solution)/shard_map/ppermute | solution.py:222
  33.3 3.0 %collective-permute-start.6 = (bf16[64,2048]{1,0:T(8,128)(2,1)S(1)}, bf16[64,2048]{1,0:T(8,128)(2,1)S(1)}, u32[]{:S(2)}, u32[]{:S(2)}) collective-permute-start(bf16[64,2048]{1,0:T(8,128)(2,1)S(1)} %get-tuple-element.26), channel_id=1, source_target_pairs={{0,1},{1,0},{2,3},{3,2},{4,5},{5,4},{6,7},{7,6},{8,9},{9,8},{10,11... | collective-permute-start | bytes 786440 | tf_op jit(solution)/shard_map/ppermute | solution.py:212
  36.3 0.0 collective-permute-done.9.y_ref
  36.3 3.9 %collective-permute-start.7 = (bf16[64,2048]{1,0:T(8,128)(2,1)S(1)}, bf16[64,2048]{1,0:T(8,128)(2,1)S(1)}, u32[]{:S(2)}, u32[]{:S(2)}) collective-permute-start(bf16[64,2048]{1,0:T(8,128)(2,1)S(1)} %get-tuple-element.32), channel_id=1, source_target_pairs={{0,8},{8,16},{16,24},{1,9},{9,17},{17,25},{2,10},{10,18},{18,26},{... | collective-permute-start | bytes 786440 | tf_op jit(solution)/shard_map/ppermute | solution.py:222
  40.3 0.0 collective-permute-done.10.refs_1_
  40.3 0.8 %shard_map.80.refs_5_ = bf16[64,4096]{1,0:T(8,128)(2,1)} custom-call(f32[64,2048]{1,0:T(8,128)S(1)} %shard_map.79.refs_0_, bf16[64,2048]{1,0:T(8,128)(2,1)S(1)} %collective-permute-done.10.refs_1_, bf16[64,4096]{1,0:T(8,128)(2,1)S(1)} %copy-done, bf16[64,2048]{1,0:T(8,128)(2,1)S(1)} %collective-permute-done.11.refs_3_), custom_call_target="tpu_custom_call" | custom-call | bytes 1048576 | tf_op jit(solution)/shard_map/pallas_call | solution.py:198
  41.1 3.8 %collective-permute-done.6.refs_2_ = bf16[64,2048]{1,0:T(8,128)(2,1)S(1)} collective-permute-done((bf16[64,2048]{1,0:T(8,128)(2,1)S(1)}, bf16[64,2048]{1,0:T(8,128)(2,1)S(1)}, u32[]{:S(2)}, u32[]{:S(2)}) %collective-permute-start.6) | collective-permute-done | bytes 262176 | tf_op jit(solution)/shard_map/ppermute | solution.py:212
  44.9 0.8 %shard_map.81 = bf16[64,4096]{1,0:T(8,128)(2,1)} custom-call(f32[64,2048]{1,0:T(8,128)S(1)} %get-tuple-element.24.refs_0_, bf16[64,2048]{1,0:T(8,128)(2,1)S(1)} %collective-permute-done.5.refs_1_, bf16[64,2048]{1,0:T(8,128)(2,1)S(1)} %collective-permute-done.6.refs_2_, bf16[64,4096]{1,0:T(8,128)(2,1)S(1)} %copy-done, ...), custom_call_target="tpu_custom_call", output_to_operand_aliasing={{}: (5, {})} | custom-call | bytes 1048576 | tf_op jit(solution)/shard_map/pallas_call | solution.py:198
  (18 shorter events, 0.1 us)
Async XLA Ops:
  1.0 7.9 %collective-permute-start.2 = (bf16[64,1024]{1,0:T(8,128)(2,1)S(1)}, bf16[64,1024]{1,0:T(8,128)(2,1)S(1)}, u32[]{:S(2)}, u32[]{:S(2)}) collective-permute-start(bf16[64,1024]{1,0:T(8,128)(2,1)S(1)} %get-tuple-element.34.qx_ref), channel_id=1, source_target_pairs={{0,4},{4,0},{1,5},{5,1},{2,6},{6,2},{3,7},{7,3},{8,12},{12,8},{9,1... | collective-permute-start | bytes 393224 | tf_op jit(solution)/shard_map/ppermute | solution.py:212
  4.0 4.5 %collective-permute-start = (bf16[128,128]{1,0:T(8,128)(2,1)}, bf16[128,128]{1,0:T(8,128)(2,1)S(1)}, u32[]{:S(2)}, u32[]{:S(2)}) collective-permute-start(bf16[128,128]{1,0:T(8,128)(2,1)} %bitcast.10), channel_id=1, source_target_pairs={{0,4},{4,0},{1,5},{5,1},{2,6},{6,2},{3,7},{7,3},{8,12},{12,8},{9,1... | collective-permute-start | bytes 98312 | tf_op jit(solution)/shard_map/ppermute | solution.py:212
  4.1 4.8 %slice-start = ((s8[8388608]{0:T(1024)(128)(4,1)}), s8[4194304]{0:T(1024)(128)(4,1)S(1)}, s32[]{:S(2)}) async-start(s8[8388608]{0:T(1024)(128)(4,1)} %bitcast.8), calls=%async_computation | async-start | bytes 8388608
  4.1 4.8 %slice-start.1 = ((s8[8388608]{0:T(1024)(128)(4,1)}), s8[4194304]{0:T(1024)(128)(4,1)S(1)}, s32[]{:S(2)}) async-start(s8[8388608]{0:T(1024)(128)(4,1)} %bitcast.8), calls=%async_computation.1 | async-start | bytes 8388608
  4.1 4.8 %copy-start.1 = (bf16[1,128,128]{2,1,0:T(8,128)(2,1)S(1)}, bf16[1,128,128]{2,1,0:T(8,128)(2,1)}, u32[]{:S(2)}) copy-start(bf16[1,128,128]{2,1,0:T(8,128)(2,1)} %param.8) | copy-start | bytes 98308
  4.1 4.8 %copy-start.2 = (bf16[1,128,128]{2,1,0:T(8,128)(2,1)S(1)}, bf16[1,128,128]{2,1,0:T(8,128)(2,1)}, u32[]{:S(2)}) copy-start(bf16[1,128,128]{2,1,0:T(8,128)(2,1)} %param.9) | copy-start | bytes 98308
  4.1 4.8 %collective-permute-start.1 = (bf16[128,128]{1,0:T(8,128)(2,1)}, bf16[128,128]{1,0:T(8,128)(2,1)S(1)}, u32[]{:S(2)}, u32[]{:S(2)}) collective-permute-start(bf16[128,128]{1,0:T(8,128)(2,1)} %bitcast.13), channel_id=1, source_target_pairs={{0,4},{4,0},{1,5},{5,1},{2,6},{6,2},{3,7},{7,3},{8,12},{12,8},{9,1... | collective-permute-start | bytes 98312 | tf_op jit(solution)/shard_map/ppermute | solution.py:212
  6.1 1.1 %copy-start.3 = (s32[1,256]{1,0:T(1,128)S(1)}, s32[1,256]{1,0:T(1,128)}, u32[]{:S(2)}) copy-start(s32[1,256]{1,0:T(1,128)} %seg_ref.1) | copy-start | bytes 3076
  10.1 9.3 %collective-permute-start.8 = (bf16[64,2048]{1,0:T(8,128)(2,1)S(1)}, bf16[64,2048]{1,0:T(8,128)(2,1)S(1)}, u32[]{:S(2)}, u32[]{:S(2)}) collective-permute-start(bf16[64,2048]{1,0:T(8,128)(2,1)S(1)} %get-tuple-element.20), channel_id=1, source_target_pairs={{0,1},{1,0},{2,3},{3,2},{4,5},{5,4},{6,7},{7,6},{8,9},{9,8},{10,11... | collective-permute-start | bytes 786440 | tf_op jit(solution)/shard_map/ppermute | solution.py:212
  12.0 5.0 %collective-permute-start.3 = (bf16[64,1024]{1,0:T(8,128)(2,1)S(1)}, bf16[64,1024]{1,0:T(8,128)(2,1)S(1)}, u32[]{:S(2)}, u32[]{:S(2)}) collective-permute-start(bf16[64,1024]{1,0:T(8,128)(2,1)S(1)} %get-tuple-element.21.qy_ref), channel_id=1, source_target_pairs={{0,4},{4,0},{1,5},{5,1},{2,6},{6,2},{3,7},{7,3},{8,12},{12,8},{9,1... | collective-permute-start | bytes 393224 | tf_op jit(solution)/shard_map/ppermute | solution.py:212
  14.4 14.9 %collective-permute-start.4 = (bf16[64,2048]{1,0:T(8,128)(2,1)S(1)}, bf16[64,2048]{1,0:T(8,128)(2,1)S(1)}, u32[]{:S(2)}, u32[]{:S(2)}) collective-permute-start(bf16[64,2048]{1,0:T(8,128)(2,1)S(1)} %shard_map.76), channel_id=1, source_target_pairs={{0,1},{1,0},{2,3},{3,2},{4,5},{5,4},{6,7},{7,6},{8,9},{9,8},{10,11... | collective-permute-start | bytes 786440 | tf_op jit(solution)/shard_map/ppermute | solution.py:212
  20.4 11.5 %copy-start.4 = (bf16[1,64,4096]{2,1,0:T(8,128)(2,1)S(1)}, bf16[1,64,4096]{2,1,0:T(8,128)(2,1)}, u32[]{:S(2)}) copy-start(bf16[1,64,4096]{2,1,0:T(8,128)(2,1)} %param.13) | copy-start | bytes 1572868
  20.5 19.8 %copy-start = (bf16[64,4096]{1,0:T(8,128)(2,1)S(1)}, bf16[64,4096]{1,0:T(8,128)(2,1)}, u32[]{:S(2)}) copy-start(bf16[64,4096]{1,0:T(8,128)(2,1)} %refs_3_.1) | copy-start | bytes 1572868
  20.5 15.9 %collective-permute-start.9 = (bf16[64,2048]{1,0:T(8,128)(2,1)S(1)}, bf16[64,2048]{1,0:T(8,128)(2,1)S(1)}, u32[]{:S(2)}, u32[]{:S(2)}) collective-permute-start(bf16[64,2048]{1,0:T(8,128)(2,1)S(1)} %get-tuple-element.29), channel_id=1, source_target_pairs={{0,2},{1,3},{2,0},{3,1},{4,6},{5,7},{6,4},{7,5},{8,10},{9,11},{10,... | collective-permute-start | bytes 786440 | tf_op jit(solution)/shard_map/ppermute | solution.py:212
  23.3 16.9 %collective-permute-start.10 = (bf16[64,2048]{1,0:T(8,128)(2,1)S(1)}, bf16[64,2048]{1,0:T(8,128)(2,1)S(1)}, u32[]{:S(2)}, u32[]{:S(2)}) collective-permute-start(bf16[64,2048]{1,0:T(8,128)(2,1)S(1)} %get-tuple-element.30), channel_id=1, source_target_pairs={{0,1},{1,0},{2,3},{3,2},{4,5},{5,4},{6,7},{7,6},{8,9},{9,8},{10,11... | collective-permute-start | bytes 786440 | tf_op jit(solution)/shard_map/ppermute | solution.py:212
  30.3 14.6 %collective-permute-start.5 = (bf16[64,2048]{1,0:T(8,128)(2,1)S(1)}, bf16[64,2048]{1,0:T(8,128)(2,1)S(1)}, u32[]{:S(2)}, u32[]{:S(2)}) collective-permute-start(bf16[64,2048]{1,0:T(8,128)(2,1)S(1)} %get-tuple-element.25), channel_id=1, source_target_pairs={{0,2},{1,3},{2,0},{3,1},{4,6},{5,7},{6,4},{7,5},{8,10},{9,11},{10,... | collective-permute-start | bytes 786440 | tf_op jit(solution)/shard_map/ppermute | solution.py:212
  32.0 8.3 %collective-permute-start.11 = (bf16[64,2048]{1,0:T(8,128)(2,1)S(1)}, bf16[64,2048]{1,0:T(8,128)(2,1)S(1)}, u32[]{:S(2)}, u32[]{:S(2)}) collective-permute-start(bf16[64,2048]{1,0:T(8,128)(2,1)S(1)} %get-tuple-element.31), channel_id=1, source_target_pairs={{0,8},{8,16},{16,24},{1,9},{9,17},{17,25},{2,10},{10,18},{18,26},{... | collective-permute-start | bytes 786440 | tf_op jit(solution)/shard_map/ppermute | solution.py:222
  33.3 11.6 %collective-permute-start.6 = (bf16[64,2048]{1,0:T(8,128)(2,1)S(1)}, bf16[64,2048]{1,0:T(8,128)(2,1)S(1)}, u32[]{:S(2)}, u32[]{:S(2)}) collective-permute-start(bf16[64,2048]{1,0:T(8,128)(2,1)S(1)} %get-tuple-element.26), channel_id=1, source_target_pairs={{0,1},{1,0},{2,3},{3,2},{4,5},{5,4},{6,7},{7,6},{8,9},{9,8},{10,11... | collective-permute-start | bytes 786440 | tf_op jit(solution)/shard_map/ppermute | solution.py:212
  36.3 8.6 %collective-permute-start.7 = (bf16[64,2048]{1,0:T(8,128)(2,1)S(1)}, bf16[64,2048]{1,0:T(8,128)(2,1)S(1)}, u32[]{:S(2)}, u32[]{:S(2)}) collective-permute-start(bf16[64,2048]{1,0:T(8,128)(2,1)S(1)} %get-tuple-element.32), channel_id=1, source_target_pairs={{0,8},{8,16},{16,24},{1,9},{9,17},{17,25},{2,10},{10,18},{18,26},{... | collective-permute-start | bytes 786440 | tf_op jit(solution)/shard_map/ppermute | solution.py:222
